TPU v7x, 256 devices: a whole 4x4x8 slice. The times are simulated.
256 devices in a mesh: dom: 64 (over x, z, core), sub: 4 (over y).
Axes of the slice: x: 4, y: 4, z: 8, core: 2. Of those that a mesh axis runs over, the one named last changes fastest.
Arguments:
- node_features: bfloat16 [524288, 256], P(('dom', 'sub')), may hold values from -40 to 40
- cotangent: bfloat16 [524288, 256], P(('dom', 'sub')), may hold values from -23 to 23
- tile_vals: bfloat16 [16384, 128, 128], P(('dom', 'sub')), may hold values from -0.25 to 0.25
- tile_src: int32 [16384], P(('dom', 'sub')), may hold values from 0 to 21
- tile_dst: int32 [16384], P(('dom', 'sub')), may hold values from 0 to 15
- halo_rows: int32 [256, 6, 128], P(('dom', 'sub')), may hold values from 0 to 2047
- halo_count: int32 [256, 6], P(('dom', 'sub')), may hold values from 32 to 128, as said below
- w_in: bfloat16 [512, 256], replicated, may hold values from -0.25 to 0.25
- b_in: float32 [256], replicated, may hold values from -4 to 4
- w_out: bfloat16 [256, 256], replicated, may hold values from -0.375 to 0.375
Outputs:
- new_features: bfloat16 [524288, 256], P(('dom', 'sub'))
- grad_features: float32 [524288, 256], P(('dom', 'sub'))
- grad_w_in: float32 [512, 256], replicated
- grad_b_in: float32 [256], replicated
- grad_w_out: float32 [256, 256], replicated
Inputs may be any that keep to these rules, and one draw needn't show every extreme that they name: `halo_count`: one device, drawn from the seed, has 128 live rows in every slot.
All inputs are finite; a program needn't handle non-finite values.
Results may differ from a plain program's by a relative error of at most 0.0075.
Values may be sent and summed in bfloat16 or wider, within the bound.
No kernel may reach another device: no remote copies, remote signals or barrier semaphores. Data moves between devices by JAX's collectives and lax.ppermute only.
A program may use at most 128 MiB of HBM per device.

v0:
```python
import jax
import jax.numpy as jnp
from jax import lax
from jax.sharding import PartitionSpec as P

clip_norm = 256.0
ln_eps = 1e-05


def with_halo(value, sides, width):
    for axis, dim in sides:
        peers, length = (lax.axis_size(axis), value.shape[dim])
        up = [(i, (i + 1) % peers) for i in range(peers)]
        down = [(j, i) for i, j in up]
        last = lax.slice_in_dim(value, length - width, length, axis=dim)
        first = lax.slice_in_dim(value, 0, width, axis=dim)
        before = lax.ppermute(last, axis, up)
        after = lax.ppermute(first, axis, down)
        value = jnp.concatenate([before, value, after], axis=dim)
    return value


def silu_slope(preact):
    sigmoid_v = jax.nn.sigmoid(preact)
    return sigmoid_v * (1.0 + preact * (1.0 - sigmoid_v))


def node_update(feature_rows, aggregate, w_in, b_in, w_out, cotangent):
    joined = jnp.concatenate([feature_rows, aggregate], axis=1)
    preact = jnp.dot(joined, w_in, preferred_element_type=jnp.float32) + b_in
    activated = jax.nn.silu(preact).astype(jnp.bfloat16)
    lifted = jnp.dot(activated, w_out, preferred_element_type=jnp.float32)
    centred = lifted - jnp.mean(lifted, axis=1, keepdims=True)
    inv_std = lax.rsqrt(jnp.mean(centred * centred, axis=1, keepdims=True) + ln_eps)
    normed = centred * inv_std
    new_rows = (feature_rows.astype(jnp.float32) + normed).astype(jnp.bfloat16)
    upstream = cotangent.astype(jnp.float32)
    grad_lifted = inv_std * (
        upstream
        - jnp.mean(upstream, axis=1, keepdims=True)
        - normed * jnp.mean(upstream * normed, axis=1, keepdims=True)
    )
    grad_lifted = grad_lifted.astype(jnp.bfloat16)
    grad_out = jnp.dot(activated.T, grad_lifted, preferred_element_type=jnp.float32)
    grad_act = jnp.dot(grad_lifted, w_out.T, preferred_element_type=jnp.float32)
    grad_pre = (grad_act * silu_slope(preact)).astype(jnp.bfloat16)
    grad_in = jnp.dot(joined.T, grad_pre, preferred_element_type=jnp.float32)
    grad_bias = jnp.sum(grad_pre.astype(jnp.float32), axis=0)
    grad_joined = jnp.dot(grad_pre, w_in.T, preferred_element_type=jnp.float32)
    latent = feature_rows.shape[1]
    direct = upstream + grad_joined[:, :latent]
    grad_agg = grad_joined[:, latent:].astype(jnp.bfloat16)
    return (new_rows, direct, grad_agg, grad_in, grad_bias, grad_out)


def block_sum(products, segment_ids, segments):
    totals = jnp.zeros((segments,) + products.shape[1:], jnp.float32)
    return totals.at[segment_ids].add(products)


def local(
    node_features,
    cotangent,
    tile_vals,
    tile_src,
    tile_dst,
    halo_rows,
    halo_count,
    w_in,
    b_in,
    w_out,
):
    node_count, latent = node_features.shape
    block = tile_vals.shape[1]
    node_blocks = node_count // block
    sub_count = lax.axis_size("sub")
    send_rows = halo_rows[0]
    live_count = halo_count[0]
    peer_count, halo_len = send_rows.shape
    live_mask = lax.broadcasted_iota(jnp.int32, (peer_count, halo_len), 1) < live_count[:, None]
    picked = node_features[send_rows]
    outgoing = jnp.where(live_mask[:, :, None], picked, jnp.zeros_like(picked))
    from_sub = lax.all_to_all(outgoing[:sub_count], "sub", split_axis=0, concat_axis=0, tiled=True)
    from_dom = with_halo(
        jnp.stack([outgoing[sub_count + 1], outgoing[sub_count]]), (("dom", 0),), 1
    )
    buffer = jnp.concatenate(
        [node_features, from_sub.reshape(-1, latent), from_dom[0], from_dom[3]], axis=0
    )
    buffer_blocks = buffer.shape[0] // block
    gathered = buffer.reshape(buffer_blocks, block, latent)[tile_src]
    products = jnp.einsum("tij,tjh->tih", tile_vals, gathered, preferred_element_type=jnp.float32)
    aggregate = (
        block_sum(products, tile_dst, node_blocks).reshape(node_count, latent).astype(jnp.bfloat16)
    )
    new_rows, direct, grad_agg, grad_in, grad_bias, grad_out = node_update(
        node_features, aggregate, w_in, b_in, w_out, cotangent
    )
    down_blocks = grad_agg.reshape(node_blocks, block, latent)[tile_dst]
    backward = jnp.einsum(
        "tji,tjh->tih", tile_vals, down_blocks, preferred_element_type=jnp.float32
    )
    grad_buffer = block_sum(backward, tile_src, buffer_blocks).reshape(-1, latent)
    halo_grad = grad_buffer[node_count:].reshape(peer_count, halo_len, latent)
    back_sub = lax.all_to_all(
        halo_grad[:sub_count].astype(jnp.bfloat16), "sub", split_axis=0, concat_axis=0, tiled=True
    ).astype(jnp.float32)
    back_dom = with_halo(
        jnp.stack([halo_grad[sub_count], halo_grad[sub_count + 1]]).astype(jnp.bfloat16),
        (("dom", 0),),
        1,
    ).astype(jnp.float32)
    returned = jnp.concatenate([back_sub, back_dom[3:4], back_dom[0:1]], axis=0)
    returned = jnp.where(live_mask[:, :, None], returned, jnp.zeros_like(returned))
    landed = (
        jnp.zeros((node_count, latent), jnp.float32)
        .at[send_rows.reshape(-1)]
        .add(returned.reshape(-1, latent))
    )
    grad_features = direct + grad_buffer[:node_count] + landed
    sum_in, sum_bias, sum_out = lax.psum((grad_in, grad_bias, grad_out), ("dom", "sub"))
    squares = jnp.sum(sum_in * sum_in) + jnp.sum(sum_bias * sum_bias) + jnp.sum(sum_out * sum_out)
    factor = jnp.minimum(1.0, clip_norm / jnp.sqrt(squares + 1e-06))
    clip_in, clip_bias, clip_out = (sum_in * factor, sum_bias * factor, sum_out * factor)
    return (new_rows, grad_features, clip_in, clip_bias, clip_out)


def solution(mesh):
    return jax.shard_map(
        local,
        mesh=mesh,
        in_specs=(
            P(("dom", "sub"), None),
            P(("dom", "sub"), None),
            P(("dom", "sub"), None, None),
            P(("dom", "sub")),
            P(("dom", "sub")),
            P(("dom", "sub"), None, None),
            P(("dom", "sub"), None),
            P(),
            P(),
            P(),
        ),
        out_specs=(P(("dom", "sub"), None), P(("dom", "sub"), None), P(), P(), P()),
        check_vma=False,
    )
```

profile of v0, /device:TPU:1, one launch (start us, length us, event | category | flops | bytes accessed | tf_op | source)
XLA Modules:
  0.0 481.7 jit_solution(11260602041390074216)
XLA Ops:
  8.8 3.5 gather_fusion
  13.2 3.0 collective-permute-start
  17.2 4.0 all-to-all-start
  23.8 2.3 copy.27
  27.9 4.1 gather_fusion.1
  32.1 6.7 %convolution_bitcast_fusion.1 = f32[64,128,256]{1,2,0:T(8,128)} fusion(bf16[64,128,256]{2,1,0:T(8,128)(2,1)} %gather_fusion.1, bf16[64,128,128]{2,1,0:T(8,128)(2,1)S(1)} %copy-done), kind=kOutput, calls=%fused_computation.11 | convolution fusion | flops 536870912 | bytes 14680064 | tf_op jit(solution)/shard_map/tij,tjh->tih/dot_general | solution.py:92
  38.8 9.0 %copy.26 = f32[64,128,256]{2,1,0:T(8,128)} copy(f32[64,128,256]{1,2,0:T(8,128)} %convolution_bitcast_fusion.1) | data formatting | bytes 16777216 | tf_op jit(solution)/shard_map/tij,tjh->tih/dot_general | solution.py:92
  47.8 1.5 broadcast_in_dim.25
  49.3 18.8 %scatter_fusion = f32[16,128,256]{2,1,0:T(8,128)} fusion(f32[16,128,256]{2,1,0:T(8,128)} %broadcast_in_dim.25, s32[64]{0:T(128)S(1)} %copy-done.15, f32[64,128,256]{2,1,0:T(8,128)} %copy.26), kind=kCustom, calls=%fused_computation.3 | custom fusion | flops 2097152 | bytes 25166080 | tf_op jit(solution)/shard_map/scatter-add | solution.py:58
  68.2 1.8 convert_element_type.37
  72.9 1.7 fusion.3
  77.8 1.5 fusion.6
  79.4 2.0 fusion.16
  81.3 1.9 copy-done.2
  83.4 2.8 gather_fusion.2
  86.2 6.7 %convolution_bitcast_fusion = f32[64,128,256]{1,2,0:T(8,128)} fusion(bf16[64,128,256]{2,1,0:T(8,128)(2,1)} %gather_fusion.2, bf16[64,128,128]{2,1,0:T(8,128)(2,1)S(1)} %copy-done), kind=kOutput, calls=%fused_computation.10 | convolution fusion | flops 536870912 | bytes 14680064 | tf_op jit(solution)/shard_map/tji,tjh->tih/dot_general | solution.py:100
  92.9 9.0 %copy.30 = f32[64,128,256]{2,1,0:T(8,128)} copy(f32[64,128,256]{1,2,0:T(8,128)} %convolution_bitcast_fusion) | data formatting | bytes 16777216 | tf_op jit(solution)/shard_map/tji,tjh->tih/dot_general | solution.py:100
  102.5 12.4 %scatter_fusion.1 = f32[22,128,256]{2,1,0:T(8,128)S(1)} fusion(f32[22,128,256]{2,1,0:T(8,128)S(1)} %broadcast_in_dim.51, s32[64]{0:T(128)S(1)} %copy-done.14, f32[64,128,256]{2,1,0:T(8,128)} %copy.30), kind=kCustom, calls=%fused_computation.4 | custom fusion | flops 2097152 | bytes 25166080 | tf_op jit(solution)/shard_map/scatter-add | solution.py:58
  115.9 1.5 slice.73
  117.5 79.8 %psum.22 = f32[256]{0:T(256)S(1)} all-reduce(f32[256]{0:T(256)S(1)} %get-tuple-element.33), channel_id=1, replica_groups=mesh['dom'=64,'sub'=4] {'dom','sub'}, use_global_device_ids=true, to_apply=%region_10.11 | all-reduce | flops 256 | bytes 2048 | tf_op jit(solution)/shard_map/psum | solution.py:121
  197.2 2.8 collective-permute-start.2
  200.1 3.4 all-to-all-start.1
  203.6 3.1 copy.36
  206.7 1.8 copy.37
  208.5 2.7 fusion.5
  211.2 1.8 copy.32
  216.1 9.0 %scatter_fusion.2 = f32[2048,256]{1,0:T(8,128)} fusion(f32[2048,256]{1,0:T(8,128)} %copy.32, s32[768]{0:T(1024)S(1)} %fusion.9, f32[768,256]{1,0:T(8,128)S(1)} %bitcast_select_fusion), kind=kCustom, calls=%fused_computation.5 | custom fusion | flops 196608 | bytes 2362368 | tf_op jit(solution)/shard_map/scatter-add | solution.py:118
  225.1 240.3 %all-reduce.3.cloned.1.call-done = (f32[512,256]{1,0:T(8,128)}, f32[256,256]{1,0:T(8,128)}) async-done(((f32[512,256]{1,0:T(8,128)}, f32[256,256]{1,0:T(8,128)}), (f32[512,256]{1,0:T(8,128)}, f32[256,256]{1,0:T(8,128)})) %all-reduce.3.cloned.1.call-update) | async-done | bytes 786448 | tf_op jit(solution)/shard_map/psum | solution.py:121
  465.4 1.8 multiply_reduce_fusion.1
  467.2 1.6 multiply_reduce_fusion.2
  470.7 1.7 broadcast_multiply_fusion.1
  473.0 1.9 broadcast_multiply_fusion
  (83 shorter events, 19.3 us)
Async XLA Ops:
  7.2 24.9 %copy-start = (bf16[64,128,128]{2,1,0:T(8,128)(2,1)S(1)}, bf16[64,128,128]{2,1,0:T(8,128)(2,1)}, u32[]{:S(2)}) copy-start(bf16[64,128,128]{2,1,0:T(8,128)(2,1)} %param.12) | copy-start | bytes 6291460
  8.8 12.4 %copy-start.3 = (bf16[2048,256]{1,0:T(8,128)(2,1)S(1)}, bf16[2048,256]{1,0:T(8,128)(2,1)}, u32[]{:S(2)}) copy-start(bf16[2048,256]{1,0:T(8,128)(2,1)} %param.10) | copy-start | bytes 3145732
  12.3 10.2 %copy-start.12 = (s32[1,6,128]{2,0,1:T(1,128)S(1)}, s32[1,6,128]{2,0,1:T(1,128)}, u32[]{:S(2)}) copy-start(s32[1,6,128]{2,0,1:T(1,128)} %param.15) | copy-start | bytes 9220
  12.5 10.1 %copy-start.17 = (s32[64]{0:T(128)S(1)}, s32[64]{0:T(128)}, u32[]{:S(2)}) copy-start(s32[64]{0:T(128)} %param.13) | copy-start | bytes 772
  13.2 13.5 %collective-permute-start = (bf16[1,128,256]{2,1,0:T(8,128)(2,1)}, bf16[1,128,256]{2,1,0:T(8,128)(2,1)S(1)}, u32[]{:S(2)}, u32[]{:S(2)}) collective-permute-start(bf16[1,128,256]{2,1,0:T(8,128)(2,1)} %get-tuple-element.23), channel_id=1, source_target_pairs={{0,4},{4,8},{8,12},{12,16},{16,20},{20,24},{24,28},{28,32},{32,36}... | collective-permute-start | bytes 196616 | tf_op jit(solution)/shard_map/ppermute | solution.py:17
  16.2 10.5 %collective-permute-start.1 = (bf16[1,128,256]{2,1,0:T(8,128)(2,1)}, bf16[1,128,256]{2,1,0:T(8,128)(2,1)S(1)}, u32[]{:S(2)}, u32[]{:S(2)}) collective-permute-start(bf16[1,128,256]{2,1,0:T(8,128)(2,1)} %get-tuple-element.24), channel_id=1, source_target_pairs={{4,0},{8,4},{12,8},{16,12},{20,16},{24,20},{28,24},{32,28},{36,32}... | collective-permute-start | bytes 196616 | tf_op jit(solution)/shard_map/ppermute | solution.py:18
  17.2 9.6 %all-to-all-start = ((bf16[4,128,256]{2,1,0:T(8,128)(2,1)}), bf16[4,128,256]{2,1,0:T(8,128)(2,1)S(1)}, u32[]{:S(2)}, u32[]{:S(2)}) async-start(bf16[4,128,256]{2,1,0:T(8,128)(2,1)} %slice.68), calls=%async_computation | async-start | bytes 524288 | tf_op jit(solution)/shard_map/all_to_all | solution.py:83
  22.6 3.4 copy-start.13
  47.8 1.5 copy-start.15
  68.2 1.8 copy-start.10
  68.2 1.8 copy-start.16
  69.9 0.9 copy-start.11
  70.9 1.2 copy-start.4
  71.6 1.3 copy-start.7
  76.8 1.0 copy-start.8
  81.3 1.9 copy-start.2
  101.9 0.6 copy-start.14
  115.1 2.3 copy-start.9
  197.2 17.6 %collective-permute-start.2 = (bf16[1,128,256]{2,1,0:T(8,128)(2,1)S(1)}, bf16[1,128,256]{2,1,0:T(8,128)(2,1)}, u32[]{:S(2)}, u32[]{:S(2)}) collective-permute-start(bf16[1,128,256]{2,1,0:T(8,128)(2,1)S(1)} %get-tuple-element.21), channel_id=1, source_target_pairs={{0,4},{4,8},{8,12},{12,16},{16,20},{20,24},{24,28},{28,32},{32,36}... | collective-permute-start | bytes 196616 | tf_op jit(solution)/shard_map/ppermute | solution.py:17
  200.1 14.8 %collective-permute-start.3 = (bf16[1,128,256]{2,1,0:T(8,128)(2,1)S(1)}, bf16[1,128,256]{2,1,0:T(8,128)(2,1)}, u32[]{:S(2)}, u32[]{:S(2)}) collective-permute-start(bf16[1,128,256]{2,1,0:T(8,128)(2,1)S(1)} %get-tuple-element.22), channel_id=1, source_target_pairs={{4,0},{8,4},{12,8},{16,12},{20,16},{24,20},{28,24},{32,28},{36,32}... | collective-permute-start | bytes 196616 | tf_op jit(solution)/shard_map/ppermute | solution.py:18
  200.1 15.7 %all-to-all-start.1 = ((bf16[4,128,256]{2,1,0:T(8,128)(2,1)}), bf16[4,128,256]{2,1,0:T(8,128)(2,1)S(1)}, u32[]{:S(2)}, u32[]{:S(2)}) async-start(bf16[4,128,256]{2,1,0:T(8,128)(2,1)} %slice.74), calls=%async_computation.1 | async-start | bytes 524288 | tf_op jit(solution)/shard_map/all_to_all | solution.py:105
  203.5 261.9 %all-reduce.3.cloned.1.call-start = ((), (), s32[]{:S(2)}) async-start(), calls=%async_computation.2 | async-start | bytes 1572864 | tf_op jit(solution)/shard_map/psum | solution.py:121
  203.5 3.1 slice-start
  206.7 1.8 copy-start.5
  211.1 1.8 copy-start.6
  213.0 1.9 slice-start.1
  216.1 258.8 %copy-start.1 = (bf16[64,128,128]{2,1,0:T(8,128)(2,1)S(1)}, bf16[64,128,128]{2,1,0:T(8,128)(2,1)}, u32[]{:S(2)}) copy-start(bf16[64,128,128]{2,1,0:T(8,128)(2,1)} %param.12) | copy-start | bytes 6291460
Sparse Core Ops, SparseCore 0:
  214.4 250.9 all-reduce.2
where the time goes:
time: 484 us; the launch traced here: 482 us
  waiting for transfers between devices  240 us (50%)
  blocking collectives  79.8 us (16%)
  other arithmetic  61.4 us (13%)
  local copies, waits for them, and re-layouts  50.1 us (10%)
  matrix products  20.3 us (4%)
  between operations  16.3 us (3%)
  starting transfers between devices  13.5 us (3%)
    psum x1, waiting for transfers between devices, local(): lax.psum((grad_in, grad_bias, grad_out), ('dom', 'sub'))  240 us
    psum x1, blocking collectives, local(): lax.psum((grad_in, grad_bias, grad_out), ('dom', 'sub'))  79.8 us
    scatter-add x2, other arithmetic, block_sum(): return totals.at[segment_ids].add(products)  31.3 us
    unnamed x40, local copies, waits for them, and re-layouts  11 us
  transfers between devices with their start and end apart: 7, of which 1 were waited for; matrix products, arithmetic and copies ran while one was open for 6% of the time, Pallas kernels for 0%

commit v1 on v0

v1 whole, which is shorter than its diff:
```python
import jax
import jax.numpy as jnp
from jax import lax
from jax.experimental import pallas as pl
from jax.experimental.pallas import tpu as pltpu
from jax.sharding import Mesh, PartitionSpec as P

H = 256
BLK = 128
NB = 16
N = NB * BLK
T = 64
PEERS = 6
SUB = 4
BUF = NB + PEERS
CHUNKS = 16
CROWS = 56
CH = 256
UNROLL = 4
clip_norm = 256.0
ln_eps = 1e-05
F32 = jnp.float32
BF16 = jnp.bfloat16
ALL = ("x", "z", "core", "sub")
DOM = ("x", "z", "core")
PLANE = ("x", "sub")
MIB = 1024 * 1024
VM = pl.BlockSpec(memory_space=pltpu.VMEM)
SM = pl.BlockSpec(memory_space=pltpu.SMEM)


def params(mib):
    return pltpu.CompilerParams(vmem_limit_bytes=mib * MIB)


def sds(shape, dtype):
    return jax.ShapeDtypeStruct(shape, dtype)


def dot(a, b):
    return jnp.dot(a, b, preferred_element_type=F32)


def dot_t0(a, b):
    return lax.dot_general(a, b, (((0,), (0,)), ((), ())), preferred_element_type=F32)


def dot_t1(a, b):
    return lax.dot_general(a, b, (((1,), (1,)), ((), ())), preferred_element_type=F32)


def pick_kernel(rows_ref, count_ref, feat_ref, *outs):
    me = lax.axis_index("sub")
    for d in range(PEERS):
        q = lax.rem(me + d, SUB) if d < SUB else d
        ids = rows_ref[0, pl.ds(q, 1), :]
        lane = lax.broadcasted_iota(jnp.int32, (1, BLK), 1)
        ids = jnp.where(lane < count_ref[0, q], ids, -1)
        column = jnp.transpose(jnp.broadcast_to(ids, (8, BLK)))[:, :1]
        hot = lax.broadcasted_iota(jnp.int32, (BLK, N), 1) == column
        hot = jnp.where(hot, 1.0, 0.0).astype(BF16)
        outs[d][...] = dot(hot, feat_ref[...]).astype(BF16)


def list_tiles(src_ref, dst_ref, listed, least, most):
    def step(t, n):
        s = src_ref[t]
        listed[n] = (dst_ref[t] * 32 + s) * 64 + t
        return n + jnp.where((s >= least) & (s < most), 1, 0)

    n = lax.fori_loop(0, T, step, jnp.int32(0))
    for p in range(UNROLL):
        listed[n + p] = (NB * 32 + least) * 64
    return n


def near_kernel(src_ref, dst_ref, feat_ref, vals_ref, total, listed):
    n = list_tiles(src_ref, dst_ref, listed, 0, NB)
    total[...] = jnp.zeros_like(total)

    def step(i, _):
        for u in range(UNROLL):
            packed = listed[i * UNROLL + u]
            t, s, d = packed % 64, (packed // 64) % 32, packed // 2048
            rows = feat_ref[pl.ds(pl.multiple_of(s * BLK, BLK), BLK), :]
            total[d] += dot(vals_ref[t], rows)
        return 0

    lax.fori_loop(0, pl.cdiv(n, UNROLL), step, 0)


def node_kernel(
    src_ref, dst_ref, h0, h1, h2, h3, h4, h5, feat_ref, cot_ref, vals_ref, near_ref,
    win_ref, bin_ref, wout_ref, new_ref, gpre_ref, pay_ref, listed, halo, total, sum_in, sum_out, sem,
):
    copy = pltpu.make_async_copy(near_ref, total, sem)
    copy.start()
    n = list_tiles(src_ref, dst_ref, listed, NB, BUF)
    me = lax.axis_index("sub")
    for d, h in enumerate((h0, h1, h2, h3, h4, h5)):
        q = lax.rem(me + SUB - d, SUB) if d < SUB else d
        halo[q] = h[...]
    copy.wait()

    def step(i, _):
        for u in range(UNROLL):
            packed = listed[i * UNROLL + u]
            t, s, d = packed % 64, (packed // 64) % 32, packed // 2048
            total[d] += dot(vals_ref[t], halo[s - NB])
        return 0

    lax.fori_loop(0, pl.cdiv(n, UNROLL), step, 0)
    w_in, b_in, w_out = win_ref[...], bin_ref[...], wout_ref[...]
    sum_bias = jnp.zeros((1, H), F32)
    for c in range(N // CH):
        rows = pl.ds(c * CH, CH)
        per = CH // BLK
        agg = total[pl.ds(c * per, per)].reshape(CH, H).astype(BF16)
        feat = feat_ref[rows, :]
        joined = jnp.concatenate([feat, agg], axis=1)
        pre = dot(joined, w_in) + b_in
        sig = 1.0 / (1.0 + jnp.exp(-pre))
        act = (pre * sig).astype(BF16)
        slope = sig * (1.0 + pre * (1.0 - sig))
        lifted = dot(act, w_out)
        centred = lifted - jnp.mean(lifted, axis=1, keepdims=True)
        inv_std = lax.rsqrt(jnp.mean(centred * centred, axis=1, keepdims=True) + ln_eps)
        normed = centred * inv_std
        new_ref[rows, :] = (feat.astype(F32) + normed).astype(BF16)
        up = cot_ref[rows, :].astype(F32)
        grad_lifted = inv_std * (
            up
            - jnp.mean(up, axis=1, keepdims=True)
            - normed * jnp.mean(up * normed, axis=1, keepdims=True)
        )
        grad_lifted = grad_lifted.astype(BF16)
        gpre = (dot_t1(grad_lifted, w_out) * slope).astype(BF16)
        gpre_ref[rows, :] = gpre
        g_out = dot_t0(act, grad_lifted)
        g_in = dot_t0(joined, gpre)
        sum_bias = sum_bias + jnp.sum(gpre.astype(F32), axis=0, keepdims=True)
        if c == 0:
            sum_in[...] = g_in
            sum_out[...] = g_out
        else:
            sum_in[...] += g_in
            sum_out[...] += g_out
    for k in range(CHUNKS):
        last = jnp.broadcast_to(sum_bias, (8, H)) if k == 0 else jnp.zeros((8, H), F32)
        piece = jnp.concatenate(
            [sum_in[pl.ds(32 * k, 32), :], sum_out[pl.ds(16 * k, 16), :], last], axis=0
        )
        pay_ref[k] = piece.astype(BF16)


def back_kernel(
    src_ref, dst_ref, gpre_ref, cot_ref, vals_ref, win_ref, own_ref, o0, o1, o2, o3, o4, o5, grad_agg, total
):
    w_in = win_ref[...]
    for c in range(N // CH):
        rows = pl.ds(c * CH, CH)
        per = CH // BLK
        joined = dot_t1(gpre_ref[rows, :], w_in)
        grad_agg[rows, :] = joined[:, H:].astype(BF16)
        direct = cot_ref[rows, :].astype(F32) + joined[:, :H]
        total[pl.ds(c * per, per)] = direct.reshape(per, BLK, H)
    total[pl.ds(NB, PEERS)] = jnp.zeros((PEERS, BLK, H), F32)

    def step(i, _):
        for u in range(UNROLL):
            t = i * UNROLL + u
            s, d = src_ref[t], dst_ref[t]
            down = grad_agg[pl.ds(pl.multiple_of(d * BLK, BLK), BLK), :]
            total[s] += dot_t0(vals_ref[t], down)
        return 0

    lax.fori_loop(0, T // UNROLL, step, 0)
    own_ref[...] = total[pl.ds(0, NB)].reshape(N, H)
    me = lax.axis_index("sub")
    for d, o in enumerate((o0, o1, o2, o3, o4, o5)):
        q = lax.rem(me + d, SUB) if d < SUB else d
        o[...] = total[NB + q].astype(BF16)


def land_kernel(rows_ref, count_ref, r0, r1, r2, r3, r4, r5, own_ref, out_ref):
    me = lax.axis_index("sub")
    lane = lax.broadcasted_iota(jnp.int32, (1, BLK), 1)
    ids = []
    for d in range(PEERS):
        q = lax.rem(me + SUB - d, SUB) if d < SUB else d
        ids.append(jnp.where(lane < count_ref[0, q], rows_ref[0, pl.ds(q, 1), :], -1))
    ids = jnp.concatenate(ids, axis=1)
    back = jnp.concatenate([r[...] for r in (r0, r1, r2, r3, r4, r5)], axis=0)
    for c in range(N // CH):
        rows = pl.ds(c * CH, CH)
        hot = lax.broadcasted_iota(jnp.int32, (CH, PEERS * BLK), 0) + c * CH == ids
        hot = jnp.where(hot, 1.0, 0.0).astype(BF16)
        out_ref[rows, :] = own_ref[rows, :] + dot(hot, back)


def fold_kernel(parts, out_ref):
    out_ref[...] = jnp.sum(parts[...].astype(F32), axis=0).astype(BF16)


def pair_kernel(mine, other, out_ref):
    both = (mine[...].astype(F32) + other[...].astype(F32)).astype(BF16)
    for i in range(out_ref.shape[0]):
        out_ref[i] = both


def spread_kernel(parts, out_ref):
    whole = jnp.sum(parts[...].astype(F32), axis=0).astype(BF16)
    for i in range(out_ref.shape[0]):
        out_ref[i] = whole


def clip_kernel(parts, in_ref, bias_ref, out_ref):
    squares = jnp.zeros((8, H), F32)
    for k in range(CHUNKS):
        piece = parts[k].astype(F32)
        squares = squares + jnp.sum(jnp.square(piece[:48]).reshape(6, 8, H), axis=0)
    bias = parts[0].astype(F32)[48:49]
    norm = jnp.sum(squares, keepdims=True) + jnp.sum(jnp.square(bias), keepdims=True)
    factor = jnp.minimum(1.0, clip_norm * lax.rsqrt(norm + 1e-06))
    for k in range(CHUNKS):
        piece = parts[k].astype(F32) * factor
        in_ref[pl.ds(32 * k, 32), :] = piece[:32]
        out_ref[pl.ds(16 * k, 16), :] = piece[32:48]
    bias_ref[...] = bias * factor


def shift(value, axis, by, size):
    return lax.ppermute(value, axis, [(i, (i + by) % size) for i in range(size)])


def exchange(slots):
    got = [slots[0]]
    got += [shift(slots[d], "sub", d, SUB) for d in range(1, SUB)]
    dom = 1
    for axis in DOM:
        dom *= lax.axis_size(axis)
    return got, dom


def local(feat, cot, vals, src, dst, halo_rows, halo_count, w_in, b_in, w_out):
    block = sds((BLK, H), BF16)
    slots = pl.pallas_call(
        pick_kernel,
        out_shape=[block] * PEERS,
        in_specs=[VM, SM, VM],
        out_specs=[VM] * PEERS,
        compiler_params=params(24),
        name="pick",
    )(halo_rows, halo_count, feat)
    got, dom = exchange(slots)
    got += [shift(slots[4], DOM, 1, dom), shift(slots[5], DOM, -1, dom)]
    near = pl.pallas_call(
        near_kernel,
        out_shape=sds((NB + 1, BLK, H), F32),
        in_specs=[SM, SM, VM, VM],
        out_specs=VM,
        scratch_shapes=[pltpu.SMEM((T + UNROLL,), jnp.int32)],
        compiler_params=params(24),
        cost_estimate=pl.CostEstimate(flops=800_000_000, bytes_accessed=6_000_000, transcendentals=0),
        name="near",
    )(src, dst, feat, vals)
    new_rows, gpre, pay = pl.pallas_call(
        node_kernel,
        out_shape=[sds((N, H), BF16), sds((N, H), BF16), sds((CHUNKS, CROWS, H), BF16)],
        in_specs=[SM, SM] + [VM] * 9 + [pl.BlockSpec(memory_space=pl.ANY)] + [VM] * 3,
        out_specs=[VM] * 3,
        scratch_shapes=[
            pltpu.SMEM((T + UNROLL,), jnp.int32),
            pltpu.VMEM((PEERS, BLK, H), BF16),
            pltpu.VMEM((NB + 1, BLK, H), F32),
            pltpu.VMEM((2 * H, H), F32),
            pltpu.VMEM((H, H), F32),
            pltpu.SemaphoreType.DMA,
        ],
        compiler_params=params(32),
        name="node",
    )(src, dst, *got, feat, cot, vals, near, w_in, b_in.reshape(1, H), w_out)
    parts = lax.all_to_all(pay, PLANE, split_axis=0, concat_axis=0, tiled=True)
    back = pl.pallas_call(
        back_kernel,
        out_shape=[sds((N, H), F32)] + [block] * PEERS,
        in_specs=[SM, SM] + [VM] * 4,
        out_specs=[VM] * 7,
        scratch_shapes=[pltpu.VMEM((N, H), BF16), pltpu.VMEM((BUF, BLK, H), F32)],
        compiler_params=params(32),
        cost_estimate=pl.CostEstimate(flops=4_000_000_000, bytes_accessed=9_000_000, transcendentals=0),
        name="back",
    )(src, dst, gpre, cot, vals, w_in)
    own, slots = back[0], back[1:]
    got, dom = exchange(slots)
    got += [shift(slots[4], DOM, -1, dom), shift(slots[5], DOM, 1, dom)]
    grad_features = pl.pallas_call(
        land_kernel,
        out_shape=sds((N, H), F32),
        in_specs=[VM, SM] + [VM] * 7,
        out_specs=VM,
        compiler_params=params(24),
        cost_estimate=pl.CostEstimate(flops=3_000_000_000, bytes_accessed=5_000_000, transcendentals=0),
        name="land",
    )(halo_rows, halo_count, *got, own)
    piece = sds((CROWS, H), BF16)
    folded = pl.pallas_call(
        fold_kernel, out_shape=piece, in_specs=[VM], out_specs=VM, compiler_params=params(4), name="fold"
    )(parts)
    other = shift(folded, "core", 1, 2)
    depth = lax.axis_size("z")
    paired = pl.pallas_call(
        pair_kernel,
        out_shape=sds((depth, CROWS, H), BF16),
        in_specs=[VM] * 2,
        out_specs=VM,
        compiler_params=params(4),
        name="pair",
    )(folded, other)
    column = lax.all_to_all(paired, "z", split_axis=0, concat_axis=0, tiled=True)
    spread = pl.pallas_call(
        spread_kernel,
        out_shape=sds((CHUNKS, CROWS, H), BF16),
        in_specs=[VM],
        out_specs=VM,
        compiler_params=params(4),
        name="spread",
    )(column)
    whole = lax.all_to_all(spread, PLANE, split_axis=0, concat_axis=0, tiled=True)
    g_in, g_bias, g_out = pl.pallas_call(
        clip_kernel,
        out_shape=[sds((2 * H, H), F32), sds((1, H), F32), sds((H, H), F32)],
        in_specs=[VM],
        out_specs=[VM] * 3,
        compiler_params=params(8),
        name="clip",
    )(whole)
    return new_rows, grad_features, g_in, g_bias.reshape(H), g_out


def solution(mesh):
    grid = Mesh(mesh.devices.reshape(4, 8, 2, 4), ALL)
    split2, split1 = P(ALL, None), P(ALL)
    split3 = P(ALL, None, None)
    return jax.shard_map(
        local,
        mesh=grid,
        in_specs=(split2, split2, split3, split1, split1, split3, split2, P(), P(), P()),
        out_specs=(split2, split2, P(), P(), P()),
        check_vma=False,
    )
```

time: 484 us -> 96.1 us (0.20)
  the two profiles are of different devices: /device:TPU:1 before, /device:TPU:8 now
where the time goes in v1:
time: 96.1 us; the launch traced here: 95.6 us
  blocking collectives  30.1 us (31%)
  Pallas kernels  25.9 us (27%)
  starting transfers between devices  21.9 us (23%)
  local copies, waits for them, and re-layouts  9.18 us (10%)
  waiting for transfers between devices  7.7 us (8%)
    all_to_all x1, blocking collectives, local(): lax.all_to_all(paired, 'z', split_axis=0, concat_axis=0, tiled=True)  17.8 us
    ppermute x11, starting transfers between devices, shift(): lax.ppermute(value, axis, [(i, (i + by) % size) for i in range(size)])  17 us
    all_to_all x1, blocking collectives, local(): parts = lax.all_to_all(pay, PLANE, split_axis=0, concat_axis=0, tiled=True)  12.4 us
    pallas_call x1, Pallas kernels, local(): pl.pallas_call(node_kernel, out_shape=[sds((N, H), BF16), sds((N, H), BF1...  9.67 us
    unnamed x37, local copies, waits for them, and re-layouts  9.18 us
    ppermute x11, waiting for transfers between devices, shift(): lax.ppermute(value, axis, [(i, (i + by) % size) for i in range(size)])  7.7 us
    pallas_call x1, Pallas kernels, local(): pl.pallas_call(back_kernel, out_shape=[sds((N, H), F32)] + [block] * PEER...  5.71 us
    all_to_all x1, starting transfers between devices, local(): lax.all_to_all(spread, PLANE, split_axis=0, concat_axis=0, tiled=True)  4.82 us
  transfers between devices with their start and end apart: 12, of which 4 were waited for; matrix products, arithmetic and copies ran while one was open for 0% of the time, Pallas kernels for 13%

profile of v1, /device:TPU:8, one launch (start us, length us, event | category | flops | bytes accessed | tf_op | source)
XLA Modules:
  0.0 95.6 jit_solution(3515950499283737225)
XLA Ops:
  0.6 0.7 copy.15.rows_ref
  1.3 1.2 %copy-done = bf16[2048,256]{1,0:T(8,128)(2,1)S(1)} copy-done((bf16[2048,256]{1,0:T(8,128)(2,1)S(1)}, bf16[2048,256]{1,0:T(8,128)(2,1)}, u32[]{:S(2)}) %copy-start) | copy-done | bytes 1048600
  2.5 0.7 copy-done.14
  3.2 1.7 %pick.1 = (bf16[128,256]{1,0:T(8,128)(2,1)S(1)}, bf16[128,256]{1,0:T(8,128)(2,1)S(1)}, bf16[128,256]{1,0:T(8,128)(2,1)S(1)}, bf16[128,256]{1,0:T(8,128)(2,1)S(1)...) custom-call(s32[1,6,128]{2,1,0:T(8,128)S(1)} %copy.15.rows_ref, s32[1,6]{1,0:T(1,128)S(1)} %copy-done.14, ...), custom_call_target="tpu_custom_call" | custom-call | tf_op jit(solution)/shard_map/pick/pallas_call | solution.py:247
  4.9 1.7 %collective-permute-start = (bf16[128,256]{1,0:T(8,128)(2,1)S(1)}, bf16[128,256]{1,0:T(8,128)(2,1)S(1)}, u32[]{:S(2)}, u32[]{:S(2)}) collective-permute-start(bf16[128,256]{1,0:T(8,128)(2,1)S(1)} %get-tuple-element.25), channel_id=1, source_target_pairs={{0,1},{1,2},{2,3},{3,0},{4,5},{5,6},{6,7},{7,4},{8,9},{9,10},{10,1... | collective-permute-start | bytes 196616 | tf_op jit(solution)/shard_map/ppermute | solution.py:233
  6.6 2.7 %collective-permute-start.1 = (bf16[128,256]{1,0:T(8,128)(2,1)S(1)}, bf16[128,256]{1,0:T(8,128)(2,1)S(1)}, u32[]{:S(2)}, u32[]{:S(2)}) collective-permute-start(bf16[128,256]{1,0:T(8,128)(2,1)S(1)} %get-tuple-element.26), channel_id=1, source_target_pairs={{0,2},{1,3},{2,0},{3,1},{4,6},{5,7},{6,4},{7,5},{8,10},{9,11},{10,... | collective-permute-start | bytes 196616 | tf_op jit(solution)/shard_map/ppermute | solution.py:233
  9.2 0.7 collective-permute-start.2
  9.9 6.6 %collective-permute-start.4 = (bf16[128,256]{1,0:T(8,128)(2,1)S(1)}, bf16[128,256]{1,0:T(8,128)(2,1)S(1)}, u32[]{:S(2)}, u32[]{:S(2)}) collective-permute-start(bf16[128,256]{1,0:T(8,128)(2,1)S(1)} %get-tuple-element.29), channel_id=1, source_target_pairs={{0,252},{4,0},{8,4},{12,8},{16,12},{20,16},{24,20},{28,24},{32,28}... | collective-permute-start | bytes 196616 | tf_op jit(solution)/shard_map/ppermute | solution.py:233
  16.6 1.2 %copy-done.1 = bf16[2048,256]{1,0:T(8,128)(2,1)S(1)} copy-done((bf16[2048,256]{1,0:T(8,128)(2,1)S(1)}, bf16[2048,256]{1,0:T(8,128)(2,1)}, u32[]{:S(2)}) %copy-start.1) | copy-done | bytes 1048600
  17.8 1.6 %copy-done.3 = bf16[64,128,128]{2,1,0:T(8,128)(2,1)S(1)} copy-done((bf16[64,128,128]{2,1,0:T(8,128)(2,1)S(1)}, bf16[64,128,128]{2,1,0:T(8,128)(2,1)}, u32[]{:S(2)}) %copy-start.3) | copy-done | bytes 2097176
  19.4 0.7 copy-done.9
  20.1 0.7 copy-done.11
  20.7 4.0 %near.1.near_ref = f32[17,128,256]{2,1,0:T(8,128)S(1)} custom-call(s32[64]{0:T(128)S(1)} %copy-done.9, s32[64]{0:T(128)S(1)} %copy-done.11, bf16[2048,256]{1,0:T(8,128)(2,1)S(1)} %copy-done.1, bf16[64,128,128]{2,1,0:T(8,128)(2,1)S(1)} %copy-done.3), custom_call_target="tpu_custom_call" | custom-call | flops 800000000 | bytes 6000000 | tf_op jit(solution)/shard_map/near/pallas_call | solution.py:257
  24.9 9.7 %node.1 = (bf16[2048,256]{1,0:T(8,128)(2,1)}, bf16[2048,256]{1,0:T(8,128)(2,1)S(1)}, bf16[16,56,256]{2,1,0:T(8,128)(2,1)S(1)}) custom-call(s32[64]{0:T(128)S(1)} %copy-done.10, s32[64]{0:T(128)S(1)} %copy-done.11, bf16[128,256]{1,0:T(8,128)(2,1)S(1)} %get-tuple-element.24.h0, bf16[128,256]{1,0:T(8,128)(2,1)S(1)} %collective-permute-done.h1, ...), custom_call_target="tpu_custom_call" | custom-call | tf_op jit(solution)/shard_map/node/pallas_call | solution.py:267
  34.6 12.4 %all_to_all.15.parts = bf16[16,56,256]{2,1,0:T(8,128)(2,1)S(1)} all-to-all(bf16[16,56,256]{2,1,0:T(8,128)(2,1)S(1)} %get-tuple-element.39), channel_id=1, replica_groups=mesh['x'=4,'z'=8,'core'=2,'sub'=4] {'x','sub'}, dimensions={0} | all-to-all | bytes 917504 | tf_op jit(solution)/shard_map/all_to_all | solution.py:283
  47.0 0.1 collective-permute-start.10
  47.1 1.2 %collective-permute-done.10.other = bf16[56,256]{1,0:T(8,128)(2,1)S(1)} collective-permute-done((bf16[56,256]{1,0:T(8,128)(2,1)S(1)}, bf16[56,256]{1,0:T(8,128)(2,1)S(1)}, u32[]{:S(2)}, u32[]{:S(2)}) %collective-permute-start.10) | collective-permute-done | bytes 28704 | tf_op jit(solution)/shard_map/ppermute | solution.py:233
  48.3 17.8 %all_to_all.16.parts = bf16[8,56,256]{2,1,0:T(8,128)(2,1)S(1)} all-to-all(bf16[8,56,256]{2,1,0:T(8,128)(2,1)S(1)} %pair.1), channel_id=1, replica_groups=mesh['x'=4,'z'=8,'core'=2,'sub'=4] {'z'}, dimensions={0} | all-to-all | bytes 458752 | tf_op jit(solution)/shard_map/all_to_all | solution.py:320
  66.1 0.8 spread.1
  66.9 4.8 %all-to-all-start.2 = ((bf16[16,56,256]{2,1,0:T(8,128)(2,1)}), bf16[16,56,256]{2,1,0:T(8,128)(2,1)S(1)}, u32[]{:S(2)}, u32[]{:S(2)}) async-start(bf16[16,56,256]{2,1,0:T(8,128)(2,1)} %spread.1), calls=%async_computation.2 | async-start | bytes 917504 | tf_op jit(solution)/shard_map/all_to_all | solution.py:329
  71.7 1.2 %copy-done.6 = bf16[2048,256]{1,0:T(8,128)(2,1)S(1)} copy-done((bf16[2048,256]{1,0:T(8,128)(2,1)S(1)}, bf16[2048,256]{1,0:T(8,128)(2,1)}, u32[]{:S(2)}) %copy-start.6) | copy-done | bytes 1048600
  73.0 1.2 %copy-done.17 = bf16[2048,256]{1,0:T(8,128)(2,1)S(1)} copy-done((bf16[2048,256]{1,0:T(8,128)(2,1)S(1)}, bf16[2048,256]{1,0:T(8,128)(2,1)}, u32[]{:S(2)}) %copy-start.17) | copy-done | bytes 1048600
  74.2 5.7 %back.1 = (f32[2048,256]{1,0:T(8,128)S(1)}, bf16[128,256]{1,0:T(8,128)(2,1)S(1)}, bf16[128,256]{1,0:T(8,128)(2,1)S(1)}, bf16[128,256]{1,0:T(8,128)(2,1)S(1)}, bf...) custom-call(s32[64]{0:T(128)S(1)} %copy-done.10, s32[64]{0:T(128)S(1)} %copy-done.12, ...), custom_call_target="tpu_custom_call" | custom-call | flops 4000000000 | bytes 9000000 | tf_op jit(solution)/shard_map/back/pallas_call | solution.py:284
  79.9 1.5 %collective-permute-start.5 = (bf16[128,256]{1,0:T(8,128)(2,1)S(1)}, bf16[128,256]{1,0:T(8,128)(2,1)S(1)}, u32[]{:S(2)}, u32[]{:S(2)}) collective-permute-start(bf16[128,256]{1,0:T(8,128)(2,1)S(1)} %get-tuple-element.33), channel_id=1, source_target_pairs={{0,1},{1,2},{2,3},{3,0},{4,5},{5,6},{6,7},{7,4},{8,9},{9,10},{10,1... | collective-permute-start | bytes 196616 | tf_op jit(solution)/shard_map/ppermute | solution.py:233
  81.4 1.0 %collective-permute-start.6 = (bf16[128,256]{1,0:T(8,128)(2,1)S(1)}, bf16[128,256]{1,0:T(8,128)(2,1)S(1)}, u32[]{:S(2)}, u32[]{:S(2)}) collective-permute-start(bf16[128,256]{1,0:T(8,128)(2,1)S(1)} %get-tuple-element.34), channel_id=1, source_target_pairs={{0,2},{1,3},{2,0},{3,1},{4,6},{5,7},{6,4},{7,5},{8,10},{9,11},{10,... | collective-permute-start | bytes 196616 | tf_op jit(solution)/shard_map/ppermute | solution.py:233
  82.4 2.2 %collective-permute-start.7 = (bf16[128,256]{1,0:T(8,128)(2,1)S(1)}, bf16[128,256]{1,0:T(8,128)(2,1)S(1)}, u32[]{:S(2)}, u32[]{:S(2)}) collective-permute-start(bf16[128,256]{1,0:T(8,128)(2,1)S(1)} %get-tuple-element.35), channel_id=1, source_target_pairs={{0,3},{1,0},{2,1},{3,2},{4,7},{5,4},{6,5},{7,6},{8,11},{9,8},{10,9... | collective-permute-start | bytes 196616 | tf_op jit(solution)/shard_map/ppermute | solution.py:233
  84.7 0.5 collective-permute-start.9
  85.2 2.1 %collective-permute-done.6.r2 = bf16[128,256]{1,0:T(8,128)(2,1)S(1)} collective-permute-done((bf16[128,256]{1,0:T(8,128)(2,1)S(1)}, bf16[128,256]{1,0:T(8,128)(2,1)S(1)}, u32[]{:S(2)}, u32[]{:S(2)}) %collective-permute-start.6) | collective-permute-done | bytes 65568 | tf_op jit(solution)/shard_map/ppermute | solution.py:233
  87.3 0.1 collective-permute-done.7.r3
  87.4 4.3 %collective-permute-done.9.r5 = bf16[128,256]{1,0:T(8,128)(2,1)S(1)} collective-permute-done((bf16[128,256]{1,0:T(8,128)(2,1)S(1)}, bf16[128,256]{1,0:T(8,128)(2,1)S(1)}, u32[]{:S(2)}, u32[]{:S(2)}) %collective-permute-start.9) | collective-permute-done | bytes 65568 | tf_op jit(solution)/shard_map/ppermute | solution.py:233
  91.7 2.8 %land.1 = f32[2048,256]{1,0:T(8,128)} custom-call(s32[1,6,128]{2,1,0:T(8,128)S(1)} %copy.15.rows_ref, s32[1,6]{1,0:T(1,128)S(1)} %copy-done.15, bf16[128,256]{1,0:T(8,128)(2,1)S(1)} %get-tuple-element.32.r0, bf16[128,256]{1,0:T(8,128)(2,1)S(1)} %collective-permute-done.5.r1, bf16[128,256]{1,0:T(8,128)(2,1)S(1)} %collective-permute-done.6.r2, ...), custom_call_target="tpu_custom_call" | custom-call | flops 3000000000 | bytes 5000000 | tf_op jit(solution)/shard_map/land/pallas_call | solution.py:297
  94.5 1.1 %clip.1 = (f32[512,256]{1,0:T(8,128)}, f32[1,256]{1,0:T(1,128)}, f32[256,256]{1,0:T(8,128)}) custom-call(bf16[16,56,256]{2,1,0:T(8,128)(2,1)S(1)} %all-to-all-done.2.parts), custom_call_target="tpu_custom_call" | custom-call | tf_op jit(solution)/shard_map/clip/pallas_call | solution.py:330
  (40 shorter events, 0.2 us)
Async XLA Ops:
  1.3 1.2 %copy-start = (bf16[2048,256]{1,0:T(8,128)(2,1)S(1)}, bf16[2048,256]{1,0:T(8,128)(2,1)}, u32[]{:S(2)}) copy-start(bf16[2048,256]{1,0:T(8,128)(2,1)} %feat_ref.5) | copy-start | bytes 3145732
  2.5 0.7 copy-start.14
  4.9 19.8 %collective-permute-start = (bf16[128,256]{1,0:T(8,128)(2,1)S(1)}, bf16[128,256]{1,0:T(8,128)(2,1)S(1)}, u32[]{:S(2)}, u32[]{:S(2)}) collective-permute-start(bf16[128,256]{1,0:T(8,128)(2,1)S(1)} %get-tuple-element.25), channel_id=1, source_target_pairs={{0,1},{1,2},{2,3},{3,0},{4,5},{5,6},{6,7},{7,4},{8,9},{9,10},{10,1... | collective-permute-start | bytes 196616 | tf_op jit(solution)/shard_map/ppermute | solution.py:233
  6.6 18.2 %collective-permute-start.1 = (bf16[128,256]{1,0:T(8,128)(2,1)S(1)}, bf16[128,256]{1,0:T(8,128)(2,1)S(1)}, u32[]{:S(2)}, u32[]{:S(2)}) collective-permute-start(bf16[128,256]{1,0:T(8,128)(2,1)S(1)} %get-tuple-element.26), channel_id=1, source_target_pairs={{0,2},{1,3},{2,0},{3,1},{4,6},{5,7},{6,4},{7,5},{8,10},{9,11},{10,... | collective-permute-start | bytes 196616 | tf_op jit(solution)/shard_map/ppermute | solution.py:233
  9.2 15.5 %collective-permute-start.2 = (bf16[128,256]{1,0:T(8,128)(2,1)S(1)}, bf16[128,256]{1,0:T(8,128)(2,1)S(1)}, u32[]{:S(2)}, u32[]{:S(2)}) collective-permute-start(bf16[128,256]{1,0:T(8,128)(2,1)S(1)} %get-tuple-element.27), channel_id=1, source_target_pairs={{0,3},{1,0},{2,1},{3,2},{4,7},{5,4},{6,5},{7,6},{8,11},{9,8},{10,9... | collective-permute-start | bytes 196616 | tf_op jit(solution)/shard_map/ppermute | solution.py:233
  9.9 14.8 %collective-permute-start.3 = (bf16[128,256]{1,0:T(8,128)(2,1)S(1)}, bf16[128,256]{1,0:T(8,128)(2,1)S(1)}, u32[]{:S(2)}, u32[]{:S(2)}) collective-permute-start(bf16[128,256]{1,0:T(8,128)(2,1)S(1)} %get-tuple-element.28), channel_id=1, source_target_pairs={{0,4},{4,8},{8,12},{12,16},{16,20},{20,24},{24,28},{28,32},{32,36}... | collective-permute-start | bytes 196616 | tf_op jit(solution)/shard_map/ppermute | solution.py:233
  9.9 14.9 %collective-permute-start.4 = (bf16[128,256]{1,0:T(8,128)(2,1)S(1)}, bf16[128,256]{1,0:T(8,128)(2,1)S(1)}, u32[]{:S(2)}, u32[]{:S(2)}) collective-permute-start(bf16[128,256]{1,0:T(8,128)(2,1)S(1)} %get-tuple-element.29), channel_id=1, source_target_pairs={{0,252},{4,0},{8,4},{12,8},{16,12},{20,16},{24,20},{28,24},{32,28}... | collective-permute-start | bytes 196616 | tf_op jit(solution)/shard_map/ppermute | solution.py:233
  16.6 1.2 %copy-start.1 = (bf16[2048,256]{1,0:T(8,128)(2,1)S(1)}, bf16[2048,256]{1,0:T(8,128)(2,1)}, u32[]{:S(2)}) copy-start(bf16[2048,256]{1,0:T(8,128)(2,1)} %feat_ref.5) | copy-start | bytes 3145732
  17.8 1.6 %copy-start.3 = (bf16[64,128,128]{2,1,0:T(8,128)(2,1)S(1)}, bf16[64,128,128]{2,1,0:T(8,128)(2,1)}, u32[]{:S(2)}) copy-start(bf16[64,128,128]{2,1,0:T(8,128)(2,1)} %vals_ref.5) | copy-start | bytes 6291460
  19.4 0.7 copy-start.9
  20.0 0.7 copy-start.11
  20.7 4.1 %copy-start.2 = (bf16[2048,256]{1,0:T(8,128)(2,1)S(1)}, bf16[2048,256]{1,0:T(8,128)(2,1)}, u32[]{:S(2)}) copy-start(bf16[2048,256]{1,0:T(8,128)(2,1)} %feat_ref.5) | copy-start | bytes 3145732
  20.7 4.1 %copy-start.4 = (bf16[64,128,128]{2,1,0:T(8,128)(2,1)S(1)}, bf16[64,128,128]{2,1,0:T(8,128)(2,1)}, u32[]{:S(2)}) copy-start(bf16[64,128,128]{2,1,0:T(8,128)(2,1)} %vals_ref.5) | copy-start | bytes 6291460
  20.7 4.1 %copy-start.5 = (bf16[2048,256]{1,0:T(8,128)(2,1)S(1)}, bf16[2048,256]{1,0:T(8,128)(2,1)}, u32[]{:S(2)}) copy-start(bf16[2048,256]{1,0:T(8,128)(2,1)} %cot_ref.3) | copy-start | bytes 3145732
  20.7 4.1 %copy-start.7 = (bf16[512,256]{1,0:T(8,128)(2,1)S(1)}, bf16[512,256]{1,0:T(8,128)(2,1)}, u32[]{:S(2)}) copy-start(bf16[512,256]{1,0:T(8,128)(2,1)} %win_ref.3) | copy-start | bytes 786436
  20.7 4.1 %copy-start.8 = (bf16[256,256]{1,0:T(8,128)(2,1)S(1)}, bf16[256,256]{1,0:T(8,128)(2,1)}, u32[]{:S(2)}) copy-start(bf16[256,256]{1,0:T(8,128)(2,1)} %wout_ref.1) | copy-start | bytes 393220
  20.7 4.1 %copy-start.10 = (s32[64]{0:T(128)S(1)}, s32[64]{0:T(128)}, u32[]{:S(2)}) copy-start(s32[64]{0:T(128)} %src_ref.5) | copy-start | bytes 772
  20.7 4.1 %copy-start.13 = (f32[256]{0:T(256)S(1)}, f32[256]{0:T(256)}, u32[]{:S(2)}) copy-start(f32[256]{0:T(256)} %param.18) | copy-start | bytes 3076
  34.5 31.6 %copy-start.16 = (bf16[2048,256]{1,0:T(8,128)(2,1)}, bf16[2048,256]{1,0:T(8,128)(2,1)S(1)}, u32[]{:S(2)}) copy-start(bf16[2048,256]{1,0:T(8,128)(2,1)S(1)} %get-tuple-element.31.gpre_ref) | copy-start | bytes 3145732
  34.5 37.2 %copy-start.12 = (s32[64]{0:T(128)S(1)}, s32[64]{0:T(128)}, u32[]{:S(2)}) copy-start(s32[64]{0:T(128)} %dst_ref.5) | copy-start | bytes 772
  47.0 1.3 %collective-permute-start.10 = (bf16[56,256]{1,0:T(8,128)(2,1)S(1)}, bf16[56,256]{1,0:T(8,128)(2,1)S(1)}, u32[]{:S(2)}, u32[]{:S(2)}) collective-permute-start(bf16[56,256]{1,0:T(8,128)(2,1)S(1)} %fold.1.mine), channel_id=1, source_target_pairs={{0,4},{4,0},{1,5},{5,1},{2,6},{6,2},{3,7},{7,3},{8,12},{12,8},{9,1... | collective-permute-start | bytes 86024 | tf_op jit(solution)/shard_map/ppermute | solution.py:233
  66.9 27.6 %all-to-all-start.2 = ((bf16[16,56,256]{2,1,0:T(8,128)(2,1)}), bf16[16,56,256]{2,1,0:T(8,128)(2,1)S(1)}, u32[]{:S(2)}, u32[]{:S(2)}) async-start(bf16[16,56,256]{2,1,0:T(8,128)(2,1)} %spread.1), calls=%async_computation.2 | async-start | bytes 917504 | tf_op jit(solution)/shard_map/all_to_all | solution.py:329
  71.7 1.2 %copy-start.6 = (bf16[2048,256]{1,0:T(8,128)(2,1)S(1)}, bf16[2048,256]{1,0:T(8,128)(2,1)}, u32[]{:S(2)}) copy-start(bf16[2048,256]{1,0:T(8,128)(2,1)} %cot_ref.3) | copy-start | bytes 3145732
  73.0 1.2 %copy-start.17 = (bf16[2048,256]{1,0:T(8,128)(2,1)S(1)}, bf16[2048,256]{1,0:T(8,128)(2,1)}, u32[]{:S(2)}) copy-start(bf16[2048,256]{1,0:T(8,128)(2,1)} %copy-done.16) | copy-start | bytes 3145732
  74.2 17.5 %copy-start.15 = (s32[1,6]{1,0:T(1,128)S(1)}, s32[1,6]{1,0:T(1,128)}, u32[]{:S(2)}) copy-start(s32[1,6]{1,0:T(1,128)} %count_ref.3) | copy-start | bytes 76
  79.9 5.3 %collective-permute-start.5 = (bf16[128,256]{1,0:T(8,128)(2,1)S(1)}, bf16[128,256]{1,0:T(8,128)(2,1)S(1)}, u32[]{:S(2)}, u32[]{:S(2)}) collective-permute-start(bf16[128,256]{1,0:T(8,128)(2,1)S(1)} %get-tuple-element.33), channel_id=1, source_target_pairs={{0,1},{1,2},{2,3},{3,0},{4,5},{5,6},{6,7},{7,4},{8,9},{9,10},{10,1... | collective-permute-start | bytes 196616 | tf_op jit(solution)/shard_map/ppermute | solution.py:233
  81.4 5.9 %collective-permute-start.6 = (bf16[128,256]{1,0:T(8,128)(2,1)S(1)}, bf16[128,256]{1,0:T(8,128)(2,1)S(1)}, u32[]{:S(2)}, u32[]{:S(2)}) collective-permute-start(bf16[128,256]{1,0:T(8,128)(2,1)S(1)} %get-tuple-element.34), channel_id=1, source_target_pairs={{0,2},{1,3},{2,0},{3,1},{4,6},{5,7},{6,4},{7,5},{8,10},{9,11},{10,... | collective-permute-start | bytes 196616 | tf_op jit(solution)/shard_map/ppermute | solution.py:233
  82.4 5.0 %collective-permute-start.7 = (bf16[128,256]{1,0:T(8,128)(2,1)S(1)}, bf16[128,256]{1,0:T(8,128)(2,1)S(1)}, u32[]{:S(2)}, u32[]{:S(2)}) collective-permute-start(bf16[128,256]{1,0:T(8,128)(2,1)S(1)} %get-tuple-element.35), channel_id=1, source_target_pairs={{0,3},{1,0},{2,1},{3,2},{4,7},{5,4},{6,5},{7,6},{8,11},{9,8},{10,9... | collective-permute-start | bytes 196616 | tf_op jit(solution)/shard_map/ppermute | solution.py:233
  84.7 2.7 %collective-permute-start.8 = (bf16[128,256]{1,0:T(8,128)(2,1)S(1)}, bf16[128,256]{1,0:T(8,128)(2,1)S(1)}, u32[]{:S(2)}, u32[]{:S(2)}) collective-permute-start(bf16[128,256]{1,0:T(8,128)(2,1)S(1)} %get-tuple-element.36), channel_id=1, source_target_pairs={{0,252},{4,0},{8,4},{12,8},{16,12},{20,16},{24,20},{28,24},{32,28}... | collective-permute-start | bytes 196616 | tf_op jit(solution)/shard_map/ppermute | solution.py:233
  84.7 7.0 %collective-permute-start.9 = (bf16[128,256]{1,0:T(8,128)(2,1)S(1)}, bf16[128,256]{1,0:T(8,128)(2,1)S(1)}, u32[]{:S(2)}, u32[]{:S(2)}) collective-permute-start(bf16[128,256]{1,0:T(8,128)(2,1)S(1)} %get-tuple-element.37), channel_id=1, source_target_pairs={{0,4},{4,8},{8,12},{12,16},{16,20},{20,24},{24,28},{28,32},{32,36}... | collective-permute-start | bytes 196616 | tf_op jit(solution)/shard_map/ppermute | solution.py:233

commit v2 on v1

--- a/solution.py
+++ b/solution.py
@@ -15,8 +15,10 @@
 BUF = NB + PEERS
 CHUNKS = 16
 CROWS = 56
-CH = 256
-UNROLL = 4
+CH = 1024
+NEAR_STEP = 16
+FAR_STEP = 8
+BACK_STEP = 64
 clip_norm = 256.0
 ln_eps = 1e-05
 F32 = jnp.float32
@@ -26,6 +28,7 @@
 PLANE = ("x", "sub")
 MIB = 1024 * 1024
 VM = pl.BlockSpec(memory_space=pltpu.VMEM)
+HB = pl.BlockSpec(memory_space=pltpu.HBM)
 SM = pl.BlockSpec(memory_space=pltpu.SMEM)
 
 
@@ -49,67 +52,87 @@
     return lax.dot_general(a, b, (((1,), (1,)), ((), ())), preferred_element_type=F32)
 
 
-def pick_kernel(rows_ref, count_ref, feat_ref, *outs):
+def pick_kernel(rows_hbm, count_hbm, feat_hbm, o0, o1, o2, o3, o4, o5, rows, count, feat, hot, sems):
+    load_rows = pltpu.make_async_copy(rows_hbm, rows, sems.at[0])
+    load_count = pltpu.make_async_copy(count_hbm, count, sems.at[1])
+    load_feat = pltpu.make_async_copy(feat_hbm, feat, sems.at[2])
+    load_rows.start()
+    load_count.start()
+    load_feat.start()
     me = lax.axis_index("sub")
+    load_rows.wait()
+    load_count.wait()
+    lane = lax.broadcasted_iota(jnp.int32, (1, BLK), 1)
+    node = lax.broadcasted_iota(jnp.int32, (BLK, N), 1)
     for d in range(PEERS):
         q = lax.rem(me + d, SUB) if d < SUB else d
-        ids = rows_ref[0, pl.ds(q, 1), :]
-        lane = lax.broadcasted_iota(jnp.int32, (1, BLK), 1)
-        ids = jnp.where(lane < count_ref[0, q], ids, -1)
+        ids = jnp.where(lane < count[0, q], rows[q], -1)
         column = jnp.transpose(jnp.broadcast_to(ids, (8, BLK)))[:, :1]
-        hot = lax.broadcasted_iota(jnp.int32, (BLK, N), 1) == column
-        hot = jnp.where(hot, 1.0, 0.0).astype(BF16)
-        outs[d][...] = dot(hot, feat_ref[...]).astype(BF16)
-
-
-def list_tiles(src_ref, dst_ref, listed, least, most):
+        hot[pl.ds(d * BLK, BLK), :] = jnp.where(node == column, 1.0, 0.0).astype(BF16)
+    load_feat.wait()
+    picked = dot(hot[...], feat[...]).astype(BF16)
+    for d, o in enumerate((o0, o1, o2, o3, o4, o5)):
+        o[...] = picked[d * BLK : (d + 1) * BLK]
+
+
+def list_tiles(src_ref, dst_ref, listed, least, most, spare):
     def step(t, n):
         s = src_ref[t]
         listed[n] = (dst_ref[t] * 32 + s) * 64 + t
         return n + jnp.where((s >= least) & (s < most), 1, 0)
 
-    n = lax.fori_loop(0, T, step, jnp.int32(0))
-    for p in range(UNROLL):
+    n = lax.fori_loop(0, T, step, jnp.int32(0), unroll=True)
+    for p in range(spare):
         listed[n + p] = (NB * 32 + least) * 64
     return n
 
 
-def near_kernel(src_ref, dst_ref, feat_ref, vals_ref, total, listed):
-    n = list_tiles(src_ref, dst_ref, listed, 0, NB)
+def near_kernel(src_hbm, dst_hbm, feat_hbm, vals_hbm, total, src, dst, listed, feat, vals, sems):
+    load_src = pltpu.make_async_copy(src_hbm, src, sems.at[0])
+    load_dst = pltpu.make_async_copy(dst_hbm, dst, sems.at[1])
+    load_feat = pltpu.make_async_copy(feat_hbm, feat, sems.at[2])
+    load_vals = pltpu.make_async_copy(vals_hbm, vals, sems.at[3])
+    load_src.start()
+    load_dst.start()
+    load_feat.start()
+    load_vals.start()
     total[...] = jnp.zeros_like(total)
+    load_src.wait()
+    load_dst.wait()
+    n = list_tiles(src, dst, listed, 0, NB, NEAR_STEP)
+    load_feat.wait()
+    load_vals.wait()
 
     def step(i, _):
-        for u in range(UNROLL):
-            packed = listed[i * UNROLL + u]
+        for u in range(NEAR_STEP):
+            packed = listed[i * NEAR_STEP + u]
             t, s, d = packed % 64, (packed // 64) % 32, packed // 2048
-            rows = feat_ref[pl.ds(pl.multiple_of(s * BLK, BLK), BLK), :]
-            total[d] += dot(vals_ref[t], rows)
+            rows = feat[pl.ds(pl.multiple_of(s * BLK, BLK), BLK), :]
+            total[d] += dot(vals[t], rows)
         return 0
 
-    lax.fori_loop(0, pl.cdiv(n, UNROLL), step, 0)
+    lax.fori_loop(0, pl.cdiv(n, NEAR_STEP), step, 0)
 
 
 def node_kernel(
     src_ref, dst_ref, h0, h1, h2, h3, h4, h5, feat_ref, cot_ref, vals_ref, near_ref,
-    win_ref, bin_ref, wout_ref, new_ref, gpre_ref, pay_ref, listed, halo, total, sum_in, sum_out, sem,
+    win_ref, bin_ref, wout_ref, new_ref, gpre_ref, pay_ref, listed, halo, total, sum_in, sum_out,
 ):
-    copy = pltpu.make_async_copy(near_ref, total, sem)
-    copy.start()
-    n = list_tiles(src_ref, dst_ref, listed, NB, BUF)
+    n = list_tiles(src_ref, dst_ref, listed, NB, BUF, FAR_STEP)
     me = lax.axis_index("sub")
     for d, h in enumerate((h0, h1, h2, h3, h4, h5)):
         q = lax.rem(me + SUB - d, SUB) if d < SUB else d
         halo[q] = h[...]
-    copy.wait()
+    total[...] = near_ref[...]
 
     def step(i, _):
-        for u in range(UNROLL):
-            packed = listed[i * UNROLL + u]
+        for u in range(FAR_STEP):
+            packed = listed[i * FAR_STEP + u]
             t, s, d = packed % 64, (packed // 64) % 32, packed // 2048
             total[d] += dot(vals_ref[t], halo[s - NB])
         return 0
 
-    lax.fori_loop(0, pl.cdiv(n, UNROLL), step, 0)
+    lax.fori_loop(0, pl.cdiv(n, FAR_STEP), step, 0)
     w_in, b_in, w_out = win_ref[...], bin_ref[...], wout_ref[...]
     sum_bias = jnp.zeros((1, H), F32)
     for c in range(N // CH):
@@ -167,14 +190,14 @@
     total[pl.ds(NB, PEERS)] = jnp.zeros((PEERS, BLK, H), F32)
 
     def step(i, _):
-        for u in range(UNROLL):
-            t = i * UNROLL + u
+        for u in range(BACK_STEP):
+            t = i * BACK_STEP + u
             s, d = src_ref[t], dst_ref[t]
             down = grad_agg[pl.ds(pl.multiple_of(d * BLK, BLK), BLK), :]
             total[s] += dot_t0(vals_ref[t], down)
         return 0
 
-    lax.fori_loop(0, T // UNROLL, step, 0)
+    lax.fori_loop(0, T // BACK_STEP, step, 0)
     own_ref[...] = total[pl.ds(0, NB)].reshape(N, H)
     me = lax.axis_index("sub")
     for d, o in enumerate((o0, o1, o2, o3, o4, o5)):
@@ -188,7 +211,7 @@
     ids = []
     for d in range(PEERS):
         q = lax.rem(me + SUB - d, SUB) if d < SUB else d
-        ids.append(jnp.where(lane < count_ref[0, q], rows_ref[0, pl.ds(q, 1), :], -1))
+        ids.append(jnp.where(lane < count_ref[0, q], rows_ref[q], -1))
     ids = jnp.concatenate(ids, axis=1)
     back = jnp.concatenate([r[...] for r in (r0, r1, r2, r3, r4, r5)], axis=0)
     for c in range(N // CH):
@@ -244,38 +267,52 @@
 
 def local(feat, cot, vals, src, dst, halo_rows, halo_count, w_in, b_in, w_out):
     block = sds((BLK, H), BF16)
+    by_slot = jnp.transpose(halo_rows, (1, 0, 2))
     slots = pl.pallas_call(
         pick_kernel,
         out_shape=[block] * PEERS,
-        in_specs=[VM, SM, VM],
+        in_specs=[HB] * 3,
         out_specs=[VM] * PEERS,
+        scratch_shapes=[
+            pltpu.VMEM((PEERS, 1, BLK), jnp.int32),
+            pltpu.SMEM((1, PEERS), jnp.int32),
+            pltpu.VMEM((N, H), BF16),
+            pltpu.VMEM((PEERS * BLK, N), BF16),
+            pltpu.SemaphoreType.DMA((3,)),
+        ],
         compiler_params=params(24),
         name="pick",
-    )(halo_rows, halo_count, feat)
+    )(*[pltpu.with_memory_space_constraint(v, pltpu.HBM) for v in (by_slot, halo_count, feat)])
     got, dom = exchange(slots)
     got += [shift(slots[4], DOM, 1, dom), shift(slots[5], DOM, -1, dom)]
     near = pl.pallas_call(
         near_kernel,
         out_shape=sds((NB + 1, BLK, H), F32),
-        in_specs=[SM, SM, VM, VM],
+        in_specs=[HB] * 4,
         out_specs=VM,
-        scratch_shapes=[pltpu.SMEM((T + UNROLL,), jnp.int32)],
+        scratch_shapes=[
+            pltpu.SMEM((T,), jnp.int32),
+            pltpu.SMEM((T,), jnp.int32),
+            pltpu.SMEM((T + NEAR_STEP,), jnp.int32),
+            pltpu.VMEM((N, H), BF16),
+            pltpu.VMEM((T, BLK, BLK), BF16),
+            pltpu.SemaphoreType.DMA((4,)),
+        ],
         compiler_params=params(24),
         cost_estimate=pl.CostEstimate(flops=800_000_000, bytes_accessed=6_000_000, transcendentals=0),
         name="near",
-    )(src, dst, feat, vals)
+    )(*[pltpu.with_memory_space_constraint(v, pltpu.HBM) for v in (src, dst, feat, vals)])
     new_rows, gpre, pay = pl.pallas_call(
         node_kernel,
         out_shape=[sds((N, H), BF16), sds((N, H), BF16), sds((CHUNKS, CROWS, H), BF16)],
-        in_specs=[SM, SM] + [VM] * 9 + [pl.BlockSpec(memory_space=pl.ANY)] + [VM] * 3,
+        in_specs=[SM, SM] + [VM] * 13,
         out_specs=[VM] * 3,
         scratch_shapes=[
-            pltpu.SMEM((T + UNROLL,), jnp.int32),
+            pltpu.SMEM((T + NEAR_STEP,), jnp.int32),
             pltpu.VMEM((PEERS, BLK, H), BF16),
             pltpu.VMEM((NB + 1, BLK, H), F32),
             pltpu.VMEM((2 * H, H), F32),
             pltpu.VMEM((H, H), F32),
-            pltpu.SemaphoreType.DMA,
         ],
         compiler_params=params(32),
         name="node",
@@ -292,17 +329,7 @@
         name="back",
     )(src, dst, gpre, cot, vals, w_in)
     own, slots = back[0], back[1:]
-    got, dom = exchange(slots)
-    got += [shift(slots[4], DOM, -1, dom), shift(slots[5], DOM, 1, dom)]
-    grad_features = pl.pallas_call(
-        land_kernel,
-        out_shape=sds((N, H), F32),
-        in_specs=[VM, SM] + [VM] * 7,
-        out_specs=VM,
-        compiler_params=params(24),
-        cost_estimate=pl.CostEstimate(flops=3_000_000_000, bytes_accessed=5_000_000, transcendentals=0),
-        name="land",
-    )(halo_rows, halo_count, *got, own)
+    parts, own = lax.optimization_barrier((parts, own))
     piece = sds((CROWS, H), BF16)
     folded = pl.pallas_call(
         fold_kernel, out_shape=piece, in_specs=[VM], out_specs=VM, compiler_params=params(4), name="fold"
@@ -317,7 +344,11 @@
         compiler_params=params(4),
         name="pair",
     )(folded, other)
+    paired, *slots = lax.optimization_barrier((paired, *slots))
     column = lax.all_to_all(paired, "z", split_axis=0, concat_axis=0, tiled=True)
+    got, dom = exchange(slots)
+    got += [shift(slots[4], DOM, -1, dom), shift(slots[5], DOM, 1, dom)]
+    column, *got = lax.optimization_barrier((column, *got))
     spread = pl.pallas_call(
         spread_kernel,
         out_shape=sds((CHUNKS, CROWS, H), BF16),
@@ -327,6 +358,16 @@
         name="spread",
     )(column)
     whole = lax.all_to_all(spread, PLANE, split_axis=0, concat_axis=0, tiled=True)
+    grad_features = pl.pallas_call(
+        land_kernel,
+        out_shape=sds((N, H), F32),
+        in_specs=[VM, SM] + [VM] * 7,
+        out_specs=VM,
+        compiler_params=params(24),
+        cost_estimate=pl.CostEstimate(flops=3_000_000_000, bytes_accessed=5_000_000, transcendentals=0),
+        name="land",
+    )(by_slot, halo_count, *got, own)
+    whole, grad_features = lax.optimization_barrier((whole, grad_features))
     g_in, g_bias, g_out = pl.pallas_call(
         clip_kernel,
         out_shape=[sds((2 * H, H), F32), sds((1, H), F32), sds((H, H), F32)],

time: 96.1 us -> 76.3 us (0.79)
  blocking collectives: 30.1 us -> 0 us
  starting transfers between devices: 21.9 us -> 33.6 us
  waiting for transfers between devices: 7.7 us -> 14.2 us
  Pallas kernels: 25.9 us -> 20.7 us
  local copies, waits for them, and re-layouts: 9.18 us -> 6.36 us
    all_to_all x2 -> x0, blocking collectives: 30.1 us -> none  [the longest x1 17.8 us: local(): lax.all_to_all(paired, 'z', split_axis=0, concat_axis=0, tiled=True)]
    all_to_all x0 -> x2, starting transfers between devices: none -> 10.4 us  [the longest x1 5.74 us: local(): lax.all_to_all(paired, 'z', split_axis=0, concat_axis=0, tiled=True)]
    all_to_all x1, waiting for transfers between devices: 0.01 us -> 4.02 us  [local(): lax.all_to_all(spread, PLANE, split_axis=0, concat_axis=0, tiled=True)]
    pallas_call x1, Pallas kernels: 9.67 us -> 6.33 us  [local(): pl.pallas_call(node_kernel, out_shape=[sds((N, H), BF16), sds((N, H), BF1...]
    pallas_call x1, Pallas kernels: 5.71 us -> 2.72 us  [local(): pl.pallas_call(back_kernel, out_shape=[sds((N, H), F32)] + [block] * PEER...]
    unnamed x37 -> x30, local copies, waits for them, and re-layouts: 9.18 us -> 6.36 us
    all_to_all x0 -> x2, waiting for transfers between devices: none -> 1.97 us  [the longest x1 1.96 us: local(): parts = lax.all_to_all(pay, PLANE, split_axis=0, concat_axis=0, tiled=True)]
    ppermute x11, starting transfers between devices: 17 us -> 18.4 us  [shift(): lax.ppermute(value, axis, [(i, (i + by) % size) for i in range(size)])]
  transfers between devices with their start and end apart: 12 -> 14, of which waited for: 4 -> 6; matrix products, arithmetic and copies ran while one was open for 0% -> 0% of each run, Pallas kernels for 13% -> 12%
where the time goes in v2:
time: 76.3 us; the launch traced here: 75.7 us
  starting transfers between devices  33.6 us (44%)
  Pallas kernels  20.7 us (27%)
  waiting for transfers between devices  14.2 us (19%)
  local copies, waits for them, and re-layouts  6.36 us (8%)
  between operations  0.87 us (1%)
    ppermute x11, starting transfers between devices, shift(): lax.ppermute(value, axis, [(i, (i + by) % size) for i in range(size)])  18.4 us
    ppermute x11, waiting for transfers between devices, shift(): lax.ppermute(value, axis, [(i, (i + by) % size) for i in range(size)])  8.2 us
    unnamed x30, local copies, waits for them, and re-layouts  6.36 us
    pallas_call x1, Pallas kernels, local(): pl.pallas_call(node_kernel, out_shape=[sds((N, H), BF16), sds((N, H), BF1...  6.33 us
    all_to_all x1, starting transfers between devices, local(): lax.all_to_all(paired, 'z', split_axis=0, concat_axis=0, tiled=True)  5.74 us
    all_to_all x1, starting transfers between devices, local(): lax.all_to_all(spread, PLANE, split_axis=0, concat_axis=0, tiled=True)  4.82 us
    all_to_all x1, starting transfers between devices, local(): parts = lax.all_to_all(pay, PLANE, split_axis=0, concat_axis=0, tiled=True)  4.7 us
    all_to_all x1, waiting for transfers between devices, local(): lax.all_to_all(spread, PLANE, split_axis=0, concat_axis=0, tiled=True)  4.02 us
  transfers between devices with their start and end apart: 14, of which 6 were waited for; matrix products, arithmetic and copies ran while one was open for 0% of the time, Pallas kernels for 12%

profile of v2, /device:TPU:8, one launch (start us, length us, event | category | flops | bytes accessed | tf_op | source)
XLA Modules:
  0.0 75.7 jit_solution(14646665548207968505)
XLA Ops:
  0.6 2.8 %pick.1 = (bf16[128,256]{1,0:T(8,128)(2,1)S(1)}, bf16[128,256]{1,0:T(8,128)(2,1)S(1)}, bf16[128,256]{1,0:T(8,128)(2,1)S(1)}, bf16[128,256]{1,0:T(8,128)(2,1)S(1)...) custom-call(s32[6,1,128]{2,1,0:T(1,128)} %bitcast.3, s32[1,6]{1,0:T(1,128)} %count_ref.1, ...), custom_call_target="tpu_custom_call" | custom-call | tf_op jit(solution)/shard_map/pick/pallas_call | solution.py:271
  3.4 1.7 %collective-permute-start = (bf16[128,256]{1,0:T(8,128)(2,1)S(1)}, bf16[128,256]{1,0:T(8,128)(2,1)S(1)}, u32[]{:S(2)}, u32[]{:S(2)}) collective-permute-start(bf16[128,256]{1,0:T(8,128)(2,1)S(1)} %get-tuple-element.43), channel_id=1, source_target_pairs={{0,1},{1,2},{2,3},{3,0},{4,5},{5,6},{6,7},{7,4},{8,9},{9,10},{10,1... | collective-permute-start | bytes 196616 | tf_op jit(solution)/shard_map/ppermute | solution.py:256
  5.1 2.7 %collective-permute-start.1 = (bf16[128,256]{1,0:T(8,128)(2,1)S(1)}, bf16[128,256]{1,0:T(8,128)(2,1)S(1)}, u32[]{:S(2)}, u32[]{:S(2)}) collective-permute-start(bf16[128,256]{1,0:T(8,128)(2,1)S(1)} %get-tuple-element.44), channel_id=1, source_target_pairs={{0,2},{1,3},{2,0},{3,1},{4,6},{5,7},{6,4},{7,5},{8,10},{9,11},{10,... | collective-permute-start | bytes 196616 | tf_op jit(solution)/shard_map/ppermute | solution.py:256
  7.8 0.7 collective-permute-start.2
  8.4 0.0 copy-start.4
  8.5 6.7 %collective-permute-start.4 = (bf16[128,256]{1,0:T(8,128)(2,1)S(1)}, bf16[128,256]{1,0:T(8,128)(2,1)S(1)}, u32[]{:S(2)}, u32[]{:S(2)}) collective-permute-start(bf16[128,256]{1,0:T(8,128)(2,1)S(1)} %get-tuple-element.47), channel_id=1, source_target_pairs={{0,252},{4,0},{8,4},{12,8},{16,12},{20,16},{24,20},{28,24},{32,28}... | collective-permute-start | bytes 196616 | tf_op jit(solution)/shard_map/ppermute | solution.py:256
  15.2 3.3 %near.1.near_ref = f32[17,128,256]{2,1,0:T(8,128)S(1)} custom-call(s32[64]{0:T(128)} %src_ref.3, s32[64]{0:T(128)} %dst_ref.3, bf16[2048,256]{1,0:T(8,128)(2,1)} %feat_ref.1, bf16[64,128,128]{2,1,0:T(8,128)(2,1)} %vals_ref.3), custom_call_target="tpu_custom_call" | custom-call | flops 800000000 | bytes 6000000 | tf_op jit(solution)/shard_map/near/pallas_call | solution.py:288
  18.7 6.3 %node.1 = (bf16[2048,256]{1,0:T(8,128)(2,1)}, bf16[2048,256]{1,0:T(8,128)(2,1)S(1)}, bf16[16,56,256]{2,1,0:T(8,128)(2,1)}) custom-call(s32[64]{0:T(128)S(1)} %copy-done.7, s32[64]{0:T(128)S(1)} %copy-done.8, bf16[128,256]{1,0:T(8,128)(2,1)S(1)} %get-tuple-element.42.h0, bf16[128,256]{1,0:T(8,128)(2,1)S(1)} %collective-permute-done.h1, ...), custom_call_target="tpu_custom_call" | custom-call | tf_op jit(solution)/shard_map/node/pallas_call | solution.py:305
  25.0 1.0 %copy-done.11 = bf16[2048,256]{1,0:T(8,128)(2,1)} copy-done((bf16[2048,256]{1,0:T(8,128)(2,1)}, bf16[2048,256]{1,0:T(8,128)(2,1)S(1)}, u32[]{:S(2)}) %copy-start.11) | copy-done | bytes 1048600
  26.0 4.7 %all-to-all-start = ((bf16[16,56,256]{2,1,0:T(8,128)(2,1)}), bf16[16,56,256]{2,1,0:T(8,128)(2,1)S(1)}, u32[]{:S(2)}, u32[]{:S(2)}) async-start(bf16[16,56,256]{2,1,0:T(8,128)(2,1)} %get-tuple-element.49), calls=%async_computation | async-start | bytes 917504 | tf_op jit(solution)/shard_map/all_to_all | solution.py:320
  30.7 1.2 %copy-done.3 = bf16[2048,256]{1,0:T(8,128)(2,1)S(1)} copy-done((bf16[2048,256]{1,0:T(8,128)(2,1)S(1)}, bf16[2048,256]{1,0:T(8,128)(2,1)}, u32[]{:S(2)}) %copy-start.3) | copy-done | bytes 1048600
  31.9 1.2 %copy-done.12 = bf16[2048,256]{1,0:T(8,128)(2,1)S(1)} copy-done((bf16[2048,256]{1,0:T(8,128)(2,1)S(1)}, bf16[2048,256]{1,0:T(8,128)(2,1)}, u32[]{:S(2)}) %copy-start.12) | copy-done | bytes 1048600
  33.2 2.7 %back.1 = (f32[2048,256]{1,0:T(8,128)S(1)}, bf16[128,256]{1,0:T(8,128)(2,1)S(1)}, bf16[128,256]{1,0:T(8,128)(2,1)S(1)}, bf16[128,256]{1,0:T(8,128)(2,1)S(1)}, bf...) custom-call(s32[64]{0:T(128)S(1)} %copy-done.7, s32[64]{0:T(128)S(1)} %copy-done.8, ...), custom_call_target="tpu_custom_call" | custom-call | flops 4000000000 | bytes 9000000 | tf_op jit(solution)/shard_map/back/pallas_call | solution.py:321
  35.9 1.3 %copy-done.13 = f32[2048,256]{1,0:T(8,128)} copy-done((f32[2048,256]{1,0:T(8,128)}, f32[2048,256]{1,0:T(8,128)S(1)}, u32[]{:S(2)}) %copy-start.13) | copy-done | bytes 2097176
  37.2 2.0 %all-to-all-done.parts = bf16[16,56,256]{2,1,0:T(8,128)(2,1)S(1)} async-done(((bf16[16,56,256]{2,1,0:T(8,128)(2,1)}), bf16[16,56,256]{2,1,0:T(8,128)(2,1)S(1)}, u32[]{:S(2)}, u32[]{:S(2)}) %all-to-all-start) | async-done | bytes 458784 | tf_op jit(solution)/shard_map/all_to_all | solution.py:320
  39.2 0.1 fold.1.mine
  39.2 0.1 collective-permute-start.5
  39.3 1.2 %collective-permute-done.5.other = bf16[56,256]{1,0:T(8,128)(2,1)S(1)} collective-permute-done((bf16[56,256]{1,0:T(8,128)(2,1)S(1)}, bf16[56,256]{1,0:T(8,128)(2,1)S(1)}, u32[]{:S(2)}, u32[]{:S(2)}) %collective-permute-start.5) | collective-permute-done | bytes 28704 | tf_op jit(solution)/shard_map/ppermute | solution.py:256
  40.5 0.7 pair.1
  41.2 5.7 %all-to-all-start.1 = ((bf16[8,56,256]{2,1,0:T(8,128)(2,1)}), bf16[8,56,256]{2,1,0:T(8,128)(2,1)S(1)}, u32[]{:S(2)}, u32[]{:S(2)}) async-start(bf16[8,56,256]{2,1,0:T(8,128)(2,1)} %pair.1), calls=%async_computation.1 | async-start | bytes 458752 | tf_op jit(solution)/shard_map/all_to_all | solution.py:348
  47.0 0.6 collective-permute-start.6
  47.5 3.0 %collective-permute-start.7 = (bf16[128,256]{1,0:T(8,128)(2,1)S(1)}, bf16[128,256]{1,0:T(8,128)(2,1)S(1)}, u32[]{:S(2)}, u32[]{:S(2)}) collective-permute-start(bf16[128,256]{1,0:T(8,128)(2,1)S(1)} %get-tuple-element.62), channel_id=1, source_target_pairs={{0,2},{1,3},{2,0},{3,1},{4,6},{5,7},{6,4},{7,5},{8,10},{9,11},{10,... | collective-permute-start | bytes 196616 | tf_op jit(solution)/shard_map/ppermute | solution.py:256
  50.5 3.0 %collective-permute-start.9 = (bf16[128,256]{1,0:T(8,128)(2,1)S(1)}, bf16[128,256]{1,0:T(8,128)(2,1)S(1)}, u32[]{:S(2)}, u32[]{:S(2)}) collective-permute-start(bf16[128,256]{1,0:T(8,128)(2,1)S(1)} %get-tuple-element.64), channel_id=1, source_target_pairs={{0,252},{4,0},{8,4},{12,8},{16,12},{20,16},{24,20},{28,24},{32,28}... | collective-permute-start | bytes 196616 | tf_op jit(solution)/shard_map/ppermute | solution.py:256
  53.5 1.2 %collective-permute-done.8.r3 = bf16[128,256]{1,0:T(8,128)(2,1)S(1)} collective-permute-done((bf16[128,256]{1,0:T(8,128)(2,1)S(1)}, bf16[128,256]{1,0:T(8,128)(2,1)S(1)}, u32[]{:S(2)}, u32[]{:S(2)}) %collective-permute-start.8) | collective-permute-done | bytes 65568 | tf_op jit(solution)/shard_map/ppermute | solution.py:256
  54.8 0.7 collective-permute-done.9.r4
  55.4 5.1 %collective-permute-done.10.r5 = bf16[128,256]{1,0:T(8,128)(2,1)S(1)} collective-permute-done((bf16[128,256]{1,0:T(8,128)(2,1)S(1)}, bf16[128,256]{1,0:T(8,128)(2,1)S(1)}, u32[]{:S(2)}, u32[]{:S(2)}) %collective-permute-start.10) | collective-permute-done | bytes 65568 | tf_op jit(solution)/shard_map/ppermute | solution.py:256
  60.5 0.8 %spread.1 = bf16[16,56,256]{2,1,0:T(8,128)(2,1)} custom-call(bf16[8,56,256]{2,1,0:T(8,128)(2,1)S(1)} %all-to-all-done.1.parts), custom_call_target="tpu_custom_call" | custom-call | tf_op jit(solution)/shard_map/spread/pallas_call | solution.py:352
  61.4 4.8 %all-to-all-start.2 = ((bf16[16,56,256]{2,1,0:T(8,128)(2,1)}), bf16[16,56,256]{2,1,0:T(8,128)(2,1)S(1)}, u32[]{:S(2)}, u32[]{:S(2)}) async-start(bf16[16,56,256]{2,1,0:T(8,128)(2,1)} %spread.1), calls=%async_computation.2 | async-start | bytes 917504 | tf_op jit(solution)/shard_map/all_to_all | solution.py:360
  66.2 1.6 %copy-done.14 = f32[2048,256]{1,0:T(8,128)S(1)} copy-done((f32[2048,256]{1,0:T(8,128)S(1)}, f32[2048,256]{1,0:T(8,128)}, u32[]{:S(2)}) %copy-start.14) | copy-done | bytes 2097176
  67.8 2.8 %land.1 = f32[2048,256]{1,0:T(8,128)} custom-call(s32[6,1,128]{2,1,0:T(1,128)S(1)} %bitcast.4, s32[1,6]{1,0:T(1,128)S(1)} %copy-done.10, bf16[128,256]{1,0:T(8,128)(2,1)S(1)} %get-tuple-element.67.r0, bf16[128,256]{1,0:T(8,128)(2,1)S(1)} %collective-permute-done.6.r1, bf16[128,256]{1,0:T(8,128)(2,1)S(1)} %collective-permute-done.7.r2, ...), custom_call_target="tpu_custom_call" | custom-call | flops 3000000000 | bytes 5000000 | tf_op jit(solution)/shard_map/land/pallas_call | solution.py:361
  70.6 4.0 %all-to-all-done.2.parts = bf16[16,56,256]{2,1,0:T(8,128)(2,1)S(1)} async-done(((bf16[16,56,256]{2,1,0:T(8,128)(2,1)}), bf16[16,56,256]{2,1,0:T(8,128)(2,1)S(1)}, u32[]{:S(2)}, u32[]{:S(2)}) %all-to-all-start.2) | async-done | bytes 458784 | tf_op jit(solution)/shard_map/all_to_all | solution.py:360
  74.6 1.1 %clip.1 = (f32[512,256]{1,0:T(8,128)}, f32[1,256]{1,0:T(1,128)}, f32[256,256]{1,0:T(8,128)}) custom-call(bf16[16,56,256]{2,1,0:T(8,128)(2,1)S(1)} %all-to-all-done.2.parts), custom_call_target="tpu_custom_call" | custom-call | tf_op jit(solution)/shard_map/clip/pallas_call | solution.py:371
  (35 shorter events, 0.1 us)
Async XLA Ops:
  3.4 15.1 %collective-permute-start = (bf16[128,256]{1,0:T(8,128)(2,1)S(1)}, bf16[128,256]{1,0:T(8,128)(2,1)S(1)}, u32[]{:S(2)}, u32[]{:S(2)}) collective-permute-start(bf16[128,256]{1,0:T(8,128)(2,1)S(1)} %get-tuple-element.43), channel_id=1, source_target_pairs={{0,1},{1,2},{2,3},{3,0},{4,5},{5,6},{6,7},{7,4},{8,9},{9,10},{10,1... | collective-permute-start | bytes 196616 | tf_op jit(solution)/shard_map/ppermute | solution.py:256
  5.1 13.5 %collective-permute-start.1 = (bf16[128,256]{1,0:T(8,128)(2,1)S(1)}, bf16[128,256]{1,0:T(8,128)(2,1)S(1)}, u32[]{:S(2)}, u32[]{:S(2)}) collective-permute-start(bf16[128,256]{1,0:T(8,128)(2,1)S(1)} %get-tuple-element.44), channel_id=1, source_target_pairs={{0,2},{1,3},{2,0},{3,1},{4,6},{5,7},{6,4},{7,5},{8,10},{9,11},{10,... | collective-permute-start | bytes 196616 | tf_op jit(solution)/shard_map/ppermute | solution.py:256
  7.8 10.8 %collective-permute-start.2 = (bf16[128,256]{1,0:T(8,128)(2,1)S(1)}, bf16[128,256]{1,0:T(8,128)(2,1)S(1)}, u32[]{:S(2)}, u32[]{:S(2)}) collective-permute-start(bf16[128,256]{1,0:T(8,128)(2,1)S(1)} %get-tuple-element.45), channel_id=1, source_target_pairs={{0,3},{1,0},{2,1},{3,2},{4,7},{5,4},{6,5},{7,6},{8,11},{9,8},{10,9... | collective-permute-start | bytes 196616 | tf_op jit(solution)/shard_map/ppermute | solution.py:256
  8.4 10.2 %collective-permute-start.3 = (bf16[128,256]{1,0:T(8,128)(2,1)S(1)}, bf16[128,256]{1,0:T(8,128)(2,1)S(1)}, u32[]{:S(2)}, u32[]{:S(2)}) collective-permute-start(bf16[128,256]{1,0:T(8,128)(2,1)S(1)} %get-tuple-element.46), channel_id=1, source_target_pairs={{0,4},{4,8},{8,12},{12,16},{16,20},{20,24},{24,28},{28,32},{32,36}... | collective-permute-start | bytes 196616 | tf_op jit(solution)/shard_map/ppermute | solution.py:256
  8.4 10.2 %copy-start = (bf16[2048,256]{1,0:T(8,128)(2,1)S(1)}, bf16[2048,256]{1,0:T(8,128)(2,1)}, u32[]{:S(2)}) copy-start(bf16[2048,256]{1,0:T(8,128)(2,1)} %feat_ref.1) | copy-start | bytes 3145732
  8.4 10.2 %copy-start.1 = (bf16[64,128,128]{2,1,0:T(8,128)(2,1)S(1)}, bf16[64,128,128]{2,1,0:T(8,128)(2,1)}, u32[]{:S(2)}) copy-start(bf16[64,128,128]{2,1,0:T(8,128)(2,1)} %vals_ref.3) | copy-start | bytes 6291460
  8.4 10.2 %copy-start.2 = (bf16[2048,256]{1,0:T(8,128)(2,1)S(1)}, bf16[2048,256]{1,0:T(8,128)(2,1)}, u32[]{:S(2)}) copy-start(bf16[2048,256]{1,0:T(8,128)(2,1)} %cot_ref.3) | copy-start | bytes 3145732
  8.4 10.2 %copy-start.4 = (bf16[512,256]{1,0:T(8,128)(2,1)S(1)}, bf16[512,256]{1,0:T(8,128)(2,1)}, u32[]{:S(2)}) copy-start(bf16[512,256]{1,0:T(8,128)(2,1)} %win_ref.3) | copy-start | bytes 786436
  8.5 10.2 %copy-start.5 = (bf16[256,256]{1,0:T(8,128)(2,1)S(1)}, bf16[256,256]{1,0:T(8,128)(2,1)}, u32[]{:S(2)}) copy-start(bf16[256,256]{1,0:T(8,128)(2,1)} %wout_ref.1) | copy-start | bytes 393220
  8.5 10.2 %copy-start.7 = (s32[64]{0:T(128)S(1)}, s32[64]{0:T(128)}, u32[]{:S(2)}) copy-start(s32[64]{0:T(128)} %src_ref.3) | copy-start | bytes 772
  8.5 10.2 %copy-start.8 = (s32[64]{0:T(128)S(1)}, s32[64]{0:T(128)}, u32[]{:S(2)}) copy-start(s32[64]{0:T(128)} %dst_ref.3) | copy-start | bytes 772
  8.5 10.2 %copy-start.9 = (f32[256]{0:T(256)S(1)}, f32[256]{0:T(256)}, u32[]{:S(2)}) copy-start(f32[256]{0:T(256)} %param.18) | copy-start | bytes 3076
  8.5 10.1 %collective-permute-start.4 = (bf16[128,256]{1,0:T(8,128)(2,1)S(1)}, bf16[128,256]{1,0:T(8,128)(2,1)S(1)}, u32[]{:S(2)}, u32[]{:S(2)}) collective-permute-start(bf16[128,256]{1,0:T(8,128)(2,1)S(1)} %get-tuple-element.47), channel_id=1, source_target_pairs={{0,252},{4,0},{8,4},{12,8},{16,12},{20,16},{24,20},{28,24},{32,28}... | collective-permute-start | bytes 196616 | tf_op jit(solution)/shard_map/ppermute | solution.py:256
  25.0 1.0 %copy-start.11 = (bf16[2048,256]{1,0:T(8,128)(2,1)}, bf16[2048,256]{1,0:T(8,128)(2,1)S(1)}, u32[]{:S(2)}) copy-start(bf16[2048,256]{1,0:T(8,128)(2,1)S(1)} %get-tuple-element.50.gpre_ref) | copy-start | bytes 3145732
  26.0 13.2 %all-to-all-start = ((bf16[16,56,256]{2,1,0:T(8,128)(2,1)}), bf16[16,56,256]{2,1,0:T(8,128)(2,1)S(1)}, u32[]{:S(2)}, u32[]{:S(2)}) async-start(bf16[16,56,256]{2,1,0:T(8,128)(2,1)} %get-tuple-element.49), calls=%async_computation | async-start | bytes 917504 | tf_op jit(solution)/shard_map/all_to_all | solution.py:320
  30.7 1.2 %copy-start.3 = (bf16[2048,256]{1,0:T(8,128)(2,1)S(1)}, bf16[2048,256]{1,0:T(8,128)(2,1)}, u32[]{:S(2)}) copy-start(bf16[2048,256]{1,0:T(8,128)(2,1)} %cot_ref.3) | copy-start | bytes 3145732
  31.9 1.2 %copy-start.12 = (bf16[2048,256]{1,0:T(8,128)(2,1)S(1)}, bf16[2048,256]{1,0:T(8,128)(2,1)}, u32[]{:S(2)}) copy-start(bf16[2048,256]{1,0:T(8,128)(2,1)} %copy-done.11) | copy-start | bytes 3145732
  35.9 1.3 %copy-start.13 = (f32[2048,256]{1,0:T(8,128)}, f32[2048,256]{1,0:T(8,128)S(1)}, u32[]{:S(2)}) copy-start(f32[2048,256]{1,0:T(8,128)S(1)} %get-tuple-element.73.own_ref) | copy-start | bytes 6291460
  37.2 29.0 %copy-start.6 = (s32[1,6,128]{2,0,1:T(1,128)S(1)}, s32[1,6,128]{2,0,1:T(1,128)}, u32[]{:S(2)}) copy-start(s32[1,6,128]{2,0,1:T(1,128)} %param.15) | copy-start | bytes 9220
  37.2 29.0 %copy-start.10 = (s32[1,6]{1,0:T(1,128)S(1)}, s32[1,6]{1,0:T(1,128)}, u32[]{:S(2)}) copy-start(s32[1,6]{1,0:T(1,128)} %count_ref.1) | copy-start | bytes 76
  39.2 1.3 %collective-permute-start.5 = (bf16[56,256]{1,0:T(8,128)(2,1)S(1)}, bf16[56,256]{1,0:T(8,128)(2,1)S(1)}, u32[]{:S(2)}, u32[]{:S(2)}) collective-permute-start(bf16[56,256]{1,0:T(8,128)(2,1)S(1)} %fold.1.mine), channel_id=1, source_target_pairs={{0,4},{4,0},{1,5},{5,1},{2,6},{6,2},{3,7},{7,3},{8,12},{12,8},{9,1... | collective-permute-start | bytes 86024 | tf_op jit(solution)/shard_map/ppermute | solution.py:256
  41.2 19.3 %all-to-all-start.1 = ((bf16[8,56,256]{2,1,0:T(8,128)(2,1)}), bf16[8,56,256]{2,1,0:T(8,128)(2,1)S(1)}, u32[]{:S(2)}, u32[]{:S(2)}) async-start(bf16[8,56,256]{2,1,0:T(8,128)(2,1)} %pair.1), calls=%async_computation.1 | async-start | bytes 458752 | tf_op jit(solution)/shard_map/all_to_all | solution.py:348
  47.0 6.6 %collective-permute-start.6 = (bf16[128,256]{1,0:T(8,128)(2,1)S(1)}, bf16[128,256]{1,0:T(8,128)(2,1)S(1)}, u32[]{:S(2)}, u32[]{:S(2)}) collective-permute-start(bf16[128,256]{1,0:T(8,128)(2,1)S(1)} %get-tuple-element.61), channel_id=1, source_target_pairs={{0,1},{1,2},{2,3},{3,0},{4,5},{5,6},{6,7},{7,4},{8,9},{9,10},{10,1... | collective-permute-start | bytes 196616 | tf_op jit(solution)/shard_map/ppermute | solution.py:256
  47.5 6.0 %collective-permute-start.7 = (bf16[128,256]{1,0:T(8,128)(2,1)S(1)}, bf16[128,256]{1,0:T(8,128)(2,1)S(1)}, u32[]{:S(2)}, u32[]{:S(2)}) collective-permute-start(bf16[128,256]{1,0:T(8,128)(2,1)S(1)} %get-tuple-element.62), channel_id=1, source_target_pairs={{0,2},{1,3},{2,0},{3,1},{4,6},{5,7},{6,4},{7,5},{8,10},{9,11},{10,... | collective-permute-start | bytes 196616 | tf_op jit(solution)/shard_map/ppermute | solution.py:256
  50.5 4.3 %collective-permute-start.8 = (bf16[128,256]{1,0:T(8,128)(2,1)S(1)}, bf16[128,256]{1,0:T(8,128)(2,1)S(1)}, u32[]{:S(2)}, u32[]{:S(2)}) collective-permute-start(bf16[128,256]{1,0:T(8,128)(2,1)S(1)} %get-tuple-element.63), channel_id=1, source_target_pairs={{0,3},{1,0},{2,1},{3,2},{4,7},{5,4},{6,5},{7,6},{8,11},{9,8},{10,9... | collective-permute-start | bytes 196616 | tf_op jit(solution)/shard_map/ppermute | solution.py:256
  50.5 4.9 %collective-permute-start.9 = (bf16[128,256]{1,0:T(8,128)(2,1)S(1)}, bf16[128,256]{1,0:T(8,128)(2,1)S(1)}, u32[]{:S(2)}, u32[]{:S(2)}) collective-permute-start(bf16[128,256]{1,0:T(8,128)(2,1)S(1)} %get-tuple-element.64), channel_id=1, source_target_pairs={{0,252},{4,0},{8,4},{12,8},{16,12},{20,16},{24,20},{28,24},{32,28}... | collective-permute-start | bytes 196616 | tf_op jit(solution)/shard_map/ppermute | solution.py:256
  53.5 7.0 %collective-permute-start.10 = (bf16[128,256]{1,0:T(8,128)(2,1)S(1)}, bf16[128,256]{1,0:T(8,128)(2,1)S(1)}, u32[]{:S(2)}, u32[]{:S(2)}) collective-permute-start(bf16[128,256]{1,0:T(8,128)(2,1)S(1)} %get-tuple-element.65), channel_id=1, source_target_pairs={{0,4},{4,8},{8,12},{12,16},{16,20},{20,24},{24,28},{28,32},{32,36}... | collective-permute-start | bytes 196616 | tf_op jit(solution)/shard_map/ppermute | solution.py:256
  61.4 13.3 %all-to-all-start.2 = ((bf16[16,56,256]{2,1,0:T(8,128)(2,1)}), bf16[16,56,256]{2,1,0:T(8,128)(2,1)S(1)}, u32[]{:S(2)}, u32[]{:S(2)}) async-start(bf16[16,56,256]{2,1,0:T(8,128)(2,1)} %spread.1), calls=%async_computation.2 | async-start | bytes 917504 | tf_op jit(solution)/shard_map/all_to_all | solution.py:360
  66.2 1.6 %copy-start.14 = (f32[2048,256]{1,0:T(8,128)S(1)}, f32[2048,256]{1,0:T(8,128)}, u32[]{:S(2)}) copy-start(f32[2048,256]{1,0:T(8,128)} %copy-done.13) | copy-start | bytes 6291460

commit v3 on v2

--- a/solution.py
+++ b/solution.py
@@ -14,11 +14,12 @@
 SUB = 4
 BUF = NB + PEERS
 CHUNKS = 16
-CROWS = 56
+PROWS = 56
+HALF = H // 2
 CH = 1024
 NEAR_STEP = 16
 FAR_STEP = 8
-BACK_STEP = 64
+BACK_STEP = 32
 clip_norm = 256.0
 ln_eps = 1e-05
 F32 = jnp.float32
@@ -116,7 +117,7 @@
 
 def node_kernel(
     src_ref, dst_ref, h0, h1, h2, h3, h4, h5, feat_ref, cot_ref, vals_ref, near_ref,
-    win_ref, bin_ref, wout_ref, new_ref, gpre_ref, pay_ref, listed, halo, total, sum_in, sum_out,
+    win_ref, bin_ref, wout_ref, new_ref, gpre_ref, keep_ref, give_ref, listed, halo, total, sum_in, sum_out,
 ):
     n = list_tiles(src_ref, dst_ref, listed, NB, BUF, FAR_STEP)
     me = lax.axis_index("sub")
@@ -168,12 +169,17 @@
         else:
             sum_in[...] += g_in
             sum_out[...] += g_out
-    for k in range(CHUNKS):
-        last = jnp.broadcast_to(sum_bias, (8, H)) if k == 0 else jnp.zeros((8, H), F32)
-        piece = jnp.concatenate(
-            [sum_in[pl.ds(32 * k, 32), :], sum_out[pl.ds(16 * k, 16), :], last], axis=0
-        )
-        pay_ref[k] = piece.astype(BF16)
+    bias = jnp.concatenate([sum_bias[:, :HALF], sum_bias[:, HALF:], jnp.zeros((6, HALF), F32)], axis=0)
+    mine = lax.axis_index("core")
+    for half, out in ((mine, keep_ref), (1 - mine, give_ref)):
+        for k in range(CHUNKS):
+            top = sum_in[pl.ds(pl.multiple_of(32 * k + 16 * half, 8), 16), :]
+            low = sum_out[pl.ds(pl.multiple_of(16 * k + 8 * half, 8), 8), :]
+            last = bias if k == 0 else jnp.zeros((8, HALF), F32)
+            piece = jnp.concatenate(
+                [top[:, :HALF], low[:, :HALF], top[:, HALF:], low[:, HALF:], last], axis=0
+            )
+            out[k] = piece.astype(out.dtype)
 
 
 def back_kernel(
@@ -221,14 +227,8 @@
         out_ref[rows, :] = own_ref[rows, :] + dot(hot, back)
 
 
-def fold_kernel(parts, out_ref):
-    out_ref[...] = jnp.sum(parts[...].astype(F32), axis=0).astype(BF16)
-
-
-def pair_kernel(mine, other, out_ref):
-    both = (mine[...].astype(F32) + other[...].astype(F32)).astype(BF16)
-    for i in range(out_ref.shape[0]):
-        out_ref[i] = both
+def join_kernel(keep, other, out_ref):
+    out_ref[...] = (keep[...] + other[...].astype(F32)).astype(BF16)
 
 
 def spread_kernel(parts, out_ref):
@@ -237,19 +237,27 @@
         out_ref[i] = whole
 
 
-def clip_kernel(parts, in_ref, bias_ref, out_ref):
-    squares = jnp.zeros((8, H), F32)
-    for k in range(CHUNKS):
-        piece = parts[k].astype(F32)
-        squares = squares + jnp.sum(jnp.square(piece[:48]).reshape(6, 8, H), axis=0)
-    bias = parts[0].astype(F32)[48:49]
-    norm = jnp.sum(squares, keepdims=True) + jnp.sum(jnp.square(bias), keepdims=True)
+def clip_kernel(keep, other, in_ref, bias_ref, out_ref):
+    norms = []
+    for part in (keep, other):
+        squares = jnp.zeros((8, HALF), F32)
+        for k in range(CHUNKS):
+            piece = part[k].astype(F32)[:48]
+            squares = squares + jnp.sum(jnp.square(piece).reshape(6, 8, HALF), axis=0)
+        norms.append(jnp.sum(squares, keepdims=True))
+    last = keep[0].astype(F32)[48:56]
+    mine = lax.axis_index("core")
+    last = jnp.where(mine == 0, last, other[0].astype(F32)[48:56])
+    norm = norms[0] + norms[1] + jnp.sum(jnp.square(last), keepdims=True)
     factor = jnp.minimum(1.0, clip_norm * lax.rsqrt(norm + 1e-06))
-    for k in range(CHUNKS):
-        piece = parts[k].astype(F32) * factor
-        in_ref[pl.ds(32 * k, 32), :] = piece[:32]
-        out_ref[pl.ds(16 * k, 16), :] = piece[32:48]
-    bias_ref[...] = bias * factor
+    for half, part in ((mine, keep), (1 - mine, other)):
+        for k in range(CHUNKS):
+            piece = part[k].astype(F32) * factor
+            top = jnp.concatenate([piece[0:16], piece[24:40]], axis=1)
+            low = jnp.concatenate([piece[16:24], piece[40:48]], axis=1)
+            in_ref[pl.ds(pl.multiple_of(32 * k + 16 * half, 8), 16), :] = top
+            out_ref[pl.ds(pl.multiple_of(16 * k + 8 * half, 8), 8), :] = low
+    bias_ref[...] = jnp.concatenate([last[0:1], last[1:2]], axis=1) * factor
 
 
 def shift(value, axis, by, size):
@@ -267,6 +275,7 @@
 
 def local(feat, cot, vals, src, dst, halo_rows, halo_count, w_in, b_in, w_out):
     block = sds((BLK, H), BF16)
+    halves = (CHUNKS, PROWS, HALF)
     by_slot = jnp.transpose(halo_rows, (1, 0, 2))
     slots = pl.pallas_call(
         pick_kernel,
@@ -302,11 +311,11 @@
         cost_estimate=pl.CostEstimate(flops=800_000_000, bytes_accessed=6_000_000, transcendentals=0),
         name="near",
     )(*[pltpu.with_memory_space_constraint(v, pltpu.HBM) for v in (src, dst, feat, vals)])
-    new_rows, gpre, pay = pl.pallas_call(
+    new_rows, gpre, keep, give = pl.pallas_call(
         node_kernel,
-        out_shape=[sds((N, H), BF16), sds((N, H), BF16), sds((CHUNKS, CROWS, H), BF16)],
+        out_shape=[sds((N, H), BF16), sds((N, H), BF16), sds(halves, F32), sds(halves, BF16)],
         in_specs=[SM, SM] + [VM] * 13,
-        out_specs=[VM] * 3,
+        out_specs=[VM] * 4,
         scratch_shapes=[
             pltpu.SMEM((T + NEAR_STEP,), jnp.int32),
             pltpu.VMEM((PEERS, BLK, H), BF16),
@@ -317,7 +326,11 @@
         compiler_params=params(32),
         name="node",
     )(src, dst, *got, feat, cot, vals, near, w_in, b_in.reshape(1, H), w_out)
-    parts = lax.all_to_all(pay, PLANE, split_axis=0, concat_axis=0, tiled=True)
+    given = shift(give, "core", 1, 2)
+    joined = pl.pallas_call(
+        join_kernel, out_shape=sds(halves, BF16), in_specs=[VM] * 2, out_specs=VM, compiler_params=params(4), name="join"
+    )(keep, given)
+    parts = lax.all_to_all(joined, PLANE, split_axis=0, concat_axis=0, tiled=True)
     back = pl.pallas_call(
         back_kernel,
         out_shape=[sds((N, H), F32)] + [block] * PEERS,
@@ -330,20 +343,15 @@
     )(src, dst, gpre, cot, vals, w_in)
     own, slots = back[0], back[1:]
     parts, own = lax.optimization_barrier((parts, own))
-    piece = sds((CROWS, H), BF16)
-    folded = pl.pallas_call(
-        fold_kernel, out_shape=piece, in_specs=[VM], out_specs=VM, compiler_params=params(4), name="fold"
-    )(parts)
-    other = shift(folded, "core", 1, 2)
     depth = lax.axis_size("z")
     paired = pl.pallas_call(
-        pair_kernel,
-        out_shape=sds((depth, CROWS, H), BF16),
-        in_specs=[VM] * 2,
+        spread_kernel,
+        out_shape=sds((depth, PROWS, HALF), BF16),
+        in_specs=[VM],
         out_specs=VM,
         compiler_params=params(4),
-        name="pair",
-    )(folded, other)
+        name="fold",
+    )(parts)
     paired, *slots = lax.optimization_barrier((paired, *slots))
     column = lax.all_to_all(paired, "z", split_axis=0, concat_axis=0, tiled=True)
     got, dom = exchange(slots)
@@ -351,7 +359,7 @@
     column, *got = lax.optimization_barrier((column, *got))
     spread = pl.pallas_call(
         spread_kernel,
-        out_shape=sds((CHUNKS, CROWS, H), BF16),
+        out_shape=sds(halves, BF16),
         in_specs=[VM],
         out_specs=VM,
         compiler_params=params(4),
@@ -368,14 +376,15 @@
         name="land",
     )(by_slot, halo_count, *got, own)
     whole, grad_features = lax.optimization_barrier((whole, grad_features))
+    other = shift(whole, "core", 1, 2)
     g_in, g_bias, g_out = pl.pallas_call(
         clip_kernel,
         out_shape=[sds((2 * H, H), F32), sds((1, H), F32), sds((H, H), F32)],
-        in_specs=[VM],
+        in_specs=[VM] * 2,
         out_specs=[VM] * 3,
         compiler_params=params(8),
         name="clip",
-    )(whole)
+    )(whole, other)
     return new_rows, grad_features, g_in, g_bias.reshape(H), g_out
 
 

time: 76.3 us -> 81.1 us (1.063)
  the two profiles are of different devices: /device:TPU:8 before, /device:TPU:1 now
where the time goes in v3:
time: 81.1 us; the launch traced here: 80.7 us
  starting transfers between devices  42.1 us (52%)
  Pallas kernels  21.8 us (27%)
  local copies, waits for them, and re-layouts  9.4 us (12%)
  waiting for transfers between devices  6.49 us (8%)
  between operations  0.86 us (1%)
    ppermute x12, starting transfers between devices, shift(): lax.ppermute(value, axis, [(i, (i + by) % size) for i in range(size)])  29.5 us
    unnamed x40, local copies, waits for them, and re-layouts  9.4 us
    pallas_call x1, Pallas kernels, local(): pl.pallas_call(node_kernel, out_shape=[sds((N, H), BF16), sds((N, H), BF1...  6.45 us
    all_to_all x1, starting transfers between devices, local(): lax.all_to_all(paired, 'z', split_axis=0, concat_axis=0, tiled=True)  4.9 us
    ppermute x12, waiting for transfers between devices, shift(): lax.ppermute(value, axis, [(i, (i + by) % size) for i in range(size)])  4.65 us
    all_to_all x1, starting transfers between devices, local(): lax.all_to_all(spread, PLANE, split_axis=0, concat_axis=0, tiled=True)  4.06 us
    all_to_all x1, starting transfers between devices, local(): lax.all_to_all(joined, PLANE, split_axis=0, concat_axis=0, tiled=True)  3.71 us
    pallas_call x1, Pallas kernels, local(): pl.pallas_call(near_kernel, out_shape=sds((NB + 1, BLK, H), F32), in_spec...  3.47 us
  transfers between devices with their start and end apart: 15, of which 6 were waited for; matrix products, arithmetic and copies ran while one was open for 0% of the time, Pallas kernels for 11%

profile of v3, /device:TPU:1, one launch (start us, length us, event | category | flops | bytes accessed | tf_op | source)
XLA Modules:
  0.0 80.7 jit_solution(2209801655446002316)
XLA Ops:
  0.6 2.8 %pick.1 = (bf16[128,256]{1,0:T(8,128)(2,1)S(1)}, bf16[128,256]{1,0:T(8,128)(2,1)S(1)}, bf16[128,256]{1,0:T(8,128)(2,1)S(1)}, bf16[128,256]{1,0:T(8,128)(2,1)S(1)...) custom-call(s32[6,1,128]{2,1,0:T(1,128)} %bitcast.3, s32[1,6]{1,0:T(1,128)} %count_ref.1, ...), custom_call_target="tpu_custom_call" | custom-call | tf_op jit(solution)/shard_map/pick/pallas_call | solution.py:280
  3.4 2.2 %collective-permute-start = (bf16[128,256]{1,0:T(8,128)(2,1)S(1)}, bf16[128,256]{1,0:T(8,128)(2,1)S(1)}, u32[]{:S(2)}, u32[]{:S(2)}) collective-permute-start(bf16[128,256]{1,0:T(8,128)(2,1)S(1)} %get-tuple-element.44), channel_id=1, source_target_pairs={{0,1},{1,2},{2,3},{3,0},{4,5},{5,6},{6,7},{7,4},{8,9},{9,10},{10,1... | collective-permute-start | bytes 196616 | tf_op jit(solution)/shard_map/ppermute | solution.py:264
  5.6 2.6 %collective-permute-start.1 = (bf16[128,256]{1,0:T(8,128)(2,1)S(1)}, bf16[128,256]{1,0:T(8,128)(2,1)S(1)}, u32[]{:S(2)}, u32[]{:S(2)}) collective-permute-start(bf16[128,256]{1,0:T(8,128)(2,1)S(1)} %get-tuple-element.45), channel_id=1, source_target_pairs={{0,2},{1,3},{2,0},{3,1},{4,6},{5,7},{6,4},{7,5},{8,10},{9,11},{10,... | collective-permute-start | bytes 196616 | tf_op jit(solution)/shard_map/ppermute | solution.py:264
  8.2 1.1 %collective-permute-start.2 = (bf16[128,256]{1,0:T(8,128)(2,1)S(1)}, bf16[128,256]{1,0:T(8,128)(2,1)S(1)}, u32[]{:S(2)}, u32[]{:S(2)}) collective-permute-start(bf16[128,256]{1,0:T(8,128)(2,1)S(1)} %get-tuple-element.46), channel_id=1, source_target_pairs={{0,3},{1,0},{2,1},{3,2},{4,7},{5,4},{6,5},{7,6},{8,11},{9,8},{10,9... | collective-permute-start | bytes 196616 | tf_op jit(solution)/shard_map/ppermute | solution.py:264
  9.3 3.0 %collective-permute-start.3 = (bf16[128,256]{1,0:T(8,128)(2,1)S(1)}, bf16[128,256]{1,0:T(8,128)(2,1)S(1)}, u32[]{:S(2)}, u32[]{:S(2)}) collective-permute-start(bf16[128,256]{1,0:T(8,128)(2,1)S(1)} %get-tuple-element.47), channel_id=1, source_target_pairs={{0,4},{4,8},{8,12},{12,16},{16,20},{20,24},{24,28},{28,32},{32,36}... | collective-permute-start | bytes 196616 | tf_op jit(solution)/shard_map/ppermute | solution.py:264
  12.5 3.5 %near.1.near_ref = f32[17,128,256]{2,1,0:T(8,128)S(1)} custom-call(s32[64]{0:T(128)} %src_ref.3, s32[64]{0:T(128)} %dst_ref.3, bf16[2048,256]{1,0:T(8,128)(2,1)} %feat_ref.1, bf16[64,128,128]{2,1,0:T(8,128)(2,1)} %vals_ref.3), custom_call_target="tpu_custom_call" | custom-call | flops 800000000 | bytes 6000000 | tf_op jit(solution)/shard_map/near/pallas_call | solution.py:297
  16.2 6.4 %node.1 = (bf16[2048,256]{1,0:T(8,128)(2,1)}, bf16[2048,256]{1,0:T(8,128)(2,1)S(1)}, f32[16,56,128]{2,1,0:T(8,128)S(1)}, bf16[16,56,128]{2,1,0:T(8,128)(2,1)S(1)}) custom-call(s32[64]{0:T(128)S(1)} %copy-done.7, s32[64]{0:T(128)S(1)} %copy-done.8, bf16[128,256]{1,0:T(8,128)(2,1)S(1)} %get-tuple-element.43.h0, bf16[128,256]{1,0:T(8,128)(2,1)S(1)} %collective-permute-done.h1, ...), custom_call_target="tpu_custom_call" | custom-call | tf_op jit(solution)/shard_map/node/pallas_call | solution.py:314
  22.7 1.0 %copy-done.11 = bf16[2048,256]{1,0:T(8,128)(2,1)} copy-done((bf16[2048,256]{1,0:T(8,128)(2,1)}, bf16[2048,256]{1,0:T(8,128)(2,1)S(1)}, u32[]{:S(2)}) %copy-start.11) | copy-done | bytes 1048600
  23.7 5.0 %collective-permute-start.5 = (bf16[16,56,128]{2,1,0:T(8,128)(2,1)S(1)}, bf16[16,56,128]{2,1,0:T(8,128)(2,1)S(1)}, u32[]{:S(2)}, u32[]{:S(2)}) collective-permute-start(bf16[16,56,128]{2,1,0:T(8,128)(2,1)S(1)} %get-tuple-element.51), channel_id=1, source_target_pairs={{0,4},{4,0},{1,5},{5,1},{2,6},{6,2},{3,7},{7,3},{8,12},{12,8},{9,1... | collective-permute-start | bytes 688136 | tf_op jit(solution)/shard_map/ppermute | solution.py:264
  28.7 1.1 %collective-permute-done.5.other = bf16[16,56,128]{2,1,0:T(8,128)(2,1)S(1)} collective-permute-done((bf16[16,56,128]{2,1,0:T(8,128)(2,1)S(1)}, bf16[16,56,128]{2,1,0:T(8,128)(2,1)S(1)}, u32[]{:S(2)}, u32[]{:S(2)}) %collective-permute-start.5) | collective-permute-done | bytes 229408 | tf_op jit(solution)/shard_map/ppermute | solution.py:264
  29.8 0.7 join.1
  30.5 3.7 %all-to-all-start = ((bf16[16,56,128]{2,1,0:T(8,128)(2,1)}), bf16[16,56,128]{2,1,0:T(8,128)(2,1)S(1)}, u32[]{:S(2)}, u32[]{:S(2)}) async-start(bf16[16,56,128]{2,1,0:T(8,128)(2,1)} %join.1), calls=%async_computation | async-start | bytes 458752 | tf_op jit(solution)/shard_map/all_to_all | solution.py:333
  34.2 0.9 %copy-done.4 = bf16[512,256]{1,0:T(8,128)(2,1)S(1)} copy-done((bf16[512,256]{1,0:T(8,128)(2,1)S(1)}, bf16[512,256]{1,0:T(8,128)(2,1)}, u32[]{:S(2)}) %copy-start.4) | copy-done | bytes 262168
  35.2 1.2 %copy-done.12 = bf16[2048,256]{1,0:T(8,128)(2,1)S(1)} copy-done((bf16[2048,256]{1,0:T(8,128)(2,1)S(1)}, bf16[2048,256]{1,0:T(8,128)(2,1)}, u32[]{:S(2)}) %copy-start.12) | copy-done | bytes 1048600
  36.4 3.0 %back.1 = (f32[2048,256]{1,0:T(8,128)S(1)}, bf16[128,256]{1,0:T(8,128)(2,1)S(1)}, bf16[128,256]{1,0:T(8,128)(2,1)S(1)}, bf16[128,256]{1,0:T(8,128)(2,1)S(1)}, bf...) custom-call(s32[64]{0:T(128)S(1)} %copy-done.7, s32[64]{0:T(128)S(1)} %copy-done.8, ...), custom_call_target="tpu_custom_call" | custom-call | flops 4000000000 | bytes 9000000 | tf_op jit(solution)/shard_map/back/pallas_call | solution.py:334
  41.2 1.3 %copy-done.16 = f32[2048,256]{1,0:T(8,128)} copy-done((f32[2048,256]{1,0:T(8,128)}, f32[2048,256]{1,0:T(8,128)S(1)}, u32[]{:S(2)}) %copy-start.16) | copy-done | bytes 2097176
  43.9 4.9 %all-to-all-start.1 = ((bf16[8,56,128]{2,1,0:T(8,128)(2,1)}), bf16[8,56,128]{2,1,0:T(8,128)(2,1)S(1)}, u32[]{:S(2)}, u32[]{:S(2)}) async-start(bf16[8,56,128]{2,1,0:T(8,128)(2,1)} %fold.1), calls=%async_computation.1 | async-start | bytes 229376 | tf_op jit(solution)/shard_map/all_to_all | solution.py:356
  48.8 1.4 %collective-permute-start.6 = (bf16[128,256]{1,0:T(8,128)(2,1)}, bf16[128,256]{1,0:T(8,128)(2,1)S(1)}, u32[]{:S(2)}, u32[]{:S(2)}) collective-permute-start(bf16[128,256]{1,0:T(8,128)(2,1)} %copy-done.15), channel_id=1, source_target_pairs={{0,1},{1,2},{2,3},{3,0},{4,5},{5,6},{6,7},{7,4},{8,9},{9,10},{10,1... | collective-permute-start | bytes 196616 | tf_op jit(solution)/shard_map/ppermute | solution.py:264
  50.1 2.4 %collective-permute-start.7 = (bf16[128,256]{1,0:T(8,128)(2,1)}, bf16[128,256]{1,0:T(8,128)(2,1)S(1)}, u32[]{:S(2)}, u32[]{:S(2)}) collective-permute-start(bf16[128,256]{1,0:T(8,128)(2,1)} %copy-done.14), channel_id=1, source_target_pairs={{0,2},{1,3},{2,0},{3,1},{4,6},{5,7},{6,4},{7,5},{8,10},{9,11},{10,... | collective-permute-start | bytes 196616 | tf_op jit(solution)/shard_map/ppermute | solution.py:264
  52.5 1.2 %collective-permute-start.8 = (bf16[128,256]{1,0:T(8,128)(2,1)}, bf16[128,256]{1,0:T(8,128)(2,1)S(1)}, u32[]{:S(2)}, u32[]{:S(2)}) collective-permute-start(bf16[128,256]{1,0:T(8,128)(2,1)} %copy-done.13), channel_id=1, source_target_pairs={{0,3},{1,0},{2,1},{3,2},{4,7},{5,4},{6,5},{7,6},{8,11},{9,8},{10,9... | collective-permute-start | bytes 196616 | tf_op jit(solution)/shard_map/ppermute | solution.py:264
  53.7 2.0 %collective-permute-start.9 = (bf16[128,256]{1,0:T(8,128)(2,1)S(1)}, bf16[128,256]{1,0:T(8,128)(2,1)S(1)}, u32[]{:S(2)}, u32[]{:S(2)}) collective-permute-start(bf16[128,256]{1,0:T(8,128)(2,1)S(1)} %get-tuple-element.66), channel_id=1, source_target_pairs={{0,252},{4,0},{8,4},{12,8},{16,12},{20,16},{24,20},{28,24},{32,28}... | collective-permute-start | bytes 196616 | tf_op jit(solution)/shard_map/ppermute | solution.py:264
  55.8 1.6 %collective-permute-start.10 = (bf16[128,256]{1,0:T(8,128)(2,1)S(1)}, bf16[128,256]{1,0:T(8,128)(2,1)S(1)}, u32[]{:S(2)}, u32[]{:S(2)}) collective-permute-start(bf16[128,256]{1,0:T(8,128)(2,1)S(1)} %get-tuple-element.67), channel_id=1, source_target_pairs={{0,4},{4,8},{8,12},{12,16},{16,20},{20,24},{24,28},{28,32},{32,36}... | collective-permute-start | bytes 196616 | tf_op jit(solution)/shard_map/ppermute | solution.py:264
  57.4 1.9 %collective-permute-done.9.r4 = bf16[128,256]{1,0:T(8,128)(2,1)S(1)} collective-permute-done((bf16[128,256]{1,0:T(8,128)(2,1)S(1)}, bf16[128,256]{1,0:T(8,128)(2,1)S(1)}, u32[]{:S(2)}, u32[]{:S(2)}) %collective-permute-start.9) | collective-permute-done | bytes 65568 | tf_op jit(solution)/shard_map/ppermute | solution.py:264
  59.6 0.7 spread.1
  60.4 4.1 %all-to-all-start.2 = ((bf16[16,56,128]{2,1,0:T(8,128)(2,1)}), bf16[16,56,128]{2,1,0:T(8,128)(2,1)S(1)}, u32[]{:S(2)}, u32[]{:S(2)}) async-start(bf16[16,56,128]{2,1,0:T(8,128)(2,1)} %spread.1), calls=%async_computation.2 | async-start | bytes 458752 | tf_op jit(solution)/shard_map/all_to_all | solution.py:368
  64.5 1.6 %copy-done.17 = f32[2048,256]{1,0:T(8,128)S(1)} copy-done((f32[2048,256]{1,0:T(8,128)S(1)}, f32[2048,256]{1,0:T(8,128)}, u32[]{:S(2)}) %copy-start.17) | copy-done | bytes 2097176
  66.0 0.8 %copy-done.19 = bf16[128,256]{1,0:T(8,128)(2,1)S(1)} copy-done((bf16[128,256]{1,0:T(8,128)(2,1)S(1)}, bf16[128,256]{1,0:T(8,128)(2,1)}, u32[]{:S(2)}) %copy-start.19) | copy-done | bytes 65560
  66.9 2.8 %land.1 = f32[2048,256]{1,0:T(8,128)} custom-call(s32[6,1,128]{2,1,0:T(1,128)S(1)} %bitcast.4, s32[1,6]{1,0:T(1,128)S(1)} %copy-done.10, bf16[128,256]{1,0:T(8,128)(2,1)S(1)} %copy-done.19, bf16[128,256]{1,0:T(8,128)(2,1)S(1)} %collective-permute-done.6.r1, bf16[128,256]{1,0:T(8,128)(2,1)S(1)} %collective-permute-done.7.r2, ...), custom_call_target="tpu_custom_call" | custom-call | flops 3000000000 | bytes 5000000 | tf_op jit(solution)/shard_map/land/pallas_call | solution.py:369
  69.7 1.8 %all-to-all-done.2.keep = bf16[16,56,128]{2,1,0:T(8,128)(2,1)S(1)} async-done(((bf16[16,56,128]{2,1,0:T(8,128)(2,1)}), bf16[16,56,128]{2,1,0:T(8,128)(2,1)S(1)}, u32[]{:S(2)}, u32[]{:S(2)}) %all-to-all-start.2) | async-done | bytes 229408 | tf_op jit(solution)/shard_map/all_to_all | solution.py:368
  71.5 6.8 %collective-permute-start.11 = (bf16[16,56,128]{2,1,0:T(8,128)(2,1)S(1)}, bf16[16,56,128]{2,1,0:T(8,128)(2,1)S(1)}, u32[]{:S(2)}, u32[]{:S(2)}) collective-permute-start(bf16[16,56,128]{2,1,0:T(8,128)(2,1)S(1)} %all-to-all-done.2.keep), channel_id=1, source_target_pairs={{0,4},{4,0},{1,5},{5,1},{2,6},{6,2},{3,7},{7,3},{8,12},{12,8},{9,1... | collective-permute-start | bytes 688136 | tf_op jit(solution)/shard_map/ppermute | solution.py:264
  78.4 1.1 %collective-permute-done.11.other = bf16[16,56,128]{2,1,0:T(8,128)(2,1)S(1)} collective-permute-done((bf16[16,56,128]{2,1,0:T(8,128)(2,1)S(1)}, bf16[16,56,128]{2,1,0:T(8,128)(2,1)S(1)}, u32[]{:S(2)}, u32[]{:S(2)}) %collective-permute-start.11) | collective-permute-done | bytes 229408 | tf_op jit(solution)/shard_map/ppermute | solution.py:264
  79.5 1.1 %clip.1 = (f32[512,256]{1,0:T(8,128)}, f32[1,256]{1,0:T(1,128)}, f32[256,256]{1,0:T(8,128)}) custom-call(bf16[16,56,128]{2,1,0:T(8,128)(2,1)S(1)} %all-to-all-done.2.keep, bf16[16,56,128]{2,1,0:T(8,128)(2,1)S(1)} %collective-permute-done.11.other), custom_call_target="tpu_custom_call" | custom-call | tf_op jit(solution)/shard_map/clip/pallas_call | solution.py:380
  (47 shorter events, 3.8 us)
Async XLA Ops:
  3.4 12.6 %collective-permute-start = (bf16[128,256]{1,0:T(8,128)(2,1)S(1)}, bf16[128,256]{1,0:T(8,128)(2,1)S(1)}, u32[]{:S(2)}, u32[]{:S(2)}) collective-permute-start(bf16[128,256]{1,0:T(8,128)(2,1)S(1)} %get-tuple-element.44), channel_id=1, source_target_pairs={{0,1},{1,2},{2,3},{3,0},{4,5},{5,6},{6,7},{7,4},{8,9},{9,10},{10,1... | collective-permute-start | bytes 196616 | tf_op jit(solution)/shard_map/ppermute | solution.py:264
  5.6 10.4 %collective-permute-start.1 = (bf16[128,256]{1,0:T(8,128)(2,1)S(1)}, bf16[128,256]{1,0:T(8,128)(2,1)S(1)}, u32[]{:S(2)}, u32[]{:S(2)}) collective-permute-start(bf16[128,256]{1,0:T(8,128)(2,1)S(1)} %get-tuple-element.45), channel_id=1, source_target_pairs={{0,2},{1,3},{2,0},{3,1},{4,6},{5,7},{6,4},{7,5},{8,10},{9,11},{10,... | collective-permute-start | bytes 196616 | tf_op jit(solution)/shard_map/ppermute | solution.py:264
  8.2 7.8 %collective-permute-start.2 = (bf16[128,256]{1,0:T(8,128)(2,1)S(1)}, bf16[128,256]{1,0:T(8,128)(2,1)S(1)}, u32[]{:S(2)}, u32[]{:S(2)}) collective-permute-start(bf16[128,256]{1,0:T(8,128)(2,1)S(1)} %get-tuple-element.46), channel_id=1, source_target_pairs={{0,3},{1,0},{2,1},{3,2},{4,7},{5,4},{6,5},{7,6},{8,11},{9,8},{10,9... | collective-permute-start | bytes 196616 | tf_op jit(solution)/shard_map/ppermute | solution.py:264
  9.3 6.7 %collective-permute-start.3 = (bf16[128,256]{1,0:T(8,128)(2,1)S(1)}, bf16[128,256]{1,0:T(8,128)(2,1)S(1)}, u32[]{:S(2)}, u32[]{:S(2)}) collective-permute-start(bf16[128,256]{1,0:T(8,128)(2,1)S(1)} %get-tuple-element.47), channel_id=1, source_target_pairs={{0,4},{4,8},{8,12},{12,16},{16,20},{20,24},{24,28},{28,32},{32,36}... | collective-permute-start | bytes 196616 | tf_op jit(solution)/shard_map/ppermute | solution.py:264
  12.4 3.8 %copy-start = (bf16[2048,256]{1,0:T(8,128)(2,1)S(1)}, bf16[2048,256]{1,0:T(8,128)(2,1)}, u32[]{:S(2)}) copy-start(bf16[2048,256]{1,0:T(8,128)(2,1)} %feat_ref.1) | copy-start | bytes 3145732
  12.4 3.8 %copy-start.1 = (bf16[64,128,128]{2,1,0:T(8,128)(2,1)S(1)}, bf16[64,128,128]{2,1,0:T(8,128)(2,1)}, u32[]{:S(2)}) copy-start(bf16[64,128,128]{2,1,0:T(8,128)(2,1)} %vals_ref.3) | copy-start | bytes 6291460
  12.4 3.8 %copy-start.2 = (bf16[2048,256]{1,0:T(8,128)(2,1)S(1)}, bf16[2048,256]{1,0:T(8,128)(2,1)}, u32[]{:S(2)}) copy-start(bf16[2048,256]{1,0:T(8,128)(2,1)} %cot_ref.3) | copy-start | bytes 3145732
  12.4 3.8 %copy-start.3 = (bf16[512,256]{1,0:T(8,128)(2,1)S(1)}, bf16[512,256]{1,0:T(8,128)(2,1)}, u32[]{:S(2)}) copy-start(bf16[512,256]{1,0:T(8,128)(2,1)} %win_ref.3) | copy-start | bytes 786436
  12.4 3.8 %copy-start.5 = (bf16[256,256]{1,0:T(8,128)(2,1)S(1)}, bf16[256,256]{1,0:T(8,128)(2,1)}, u32[]{:S(2)}) copy-start(bf16[256,256]{1,0:T(8,128)(2,1)} %wout_ref.1) | copy-start | bytes 393220
  12.4 3.8 %copy-start.7 = (s32[64]{0:T(128)S(1)}, s32[64]{0:T(128)}, u32[]{:S(2)}) copy-start(s32[64]{0:T(128)} %src_ref.3) | copy-start | bytes 772
  12.4 3.8 %copy-start.8 = (s32[64]{0:T(128)S(1)}, s32[64]{0:T(128)}, u32[]{:S(2)}) copy-start(s32[64]{0:T(128)} %dst_ref.3) | copy-start | bytes 772
  12.4 3.8 %copy-start.9 = (f32[256]{0:T(256)S(1)}, f32[256]{0:T(256)}, u32[]{:S(2)}) copy-start(f32[256]{0:T(256)} %param.18) | copy-start | bytes 3076
  12.4 3.8 %collective-permute-start.4 = (bf16[128,256]{1,0:T(8,128)(2,1)S(1)}, bf16[128,256]{1,0:T(8,128)(2,1)S(1)}, u32[]{:S(2)}, u32[]{:S(2)}) collective-permute-start(bf16[128,256]{1,0:T(8,128)(2,1)S(1)} %get-tuple-element.48), channel_id=1, source_target_pairs={{0,252},{4,0},{8,4},{12,8},{16,12},{20,16},{24,20},{28,24},{32,28}... | collective-permute-start | bytes 196616 | tf_op jit(solution)/shard_map/ppermute | solution.py:264
  22.7 1.0 %copy-start.11 = (bf16[2048,256]{1,0:T(8,128)(2,1)}, bf16[2048,256]{1,0:T(8,128)(2,1)S(1)}, u32[]{:S(2)}) copy-start(bf16[2048,256]{1,0:T(8,128)(2,1)S(1)} %get-tuple-element.52.gpre_ref) | copy-start | bytes 3145732
  23.7 6.1 %collective-permute-start.5 = (bf16[16,56,128]{2,1,0:T(8,128)(2,1)S(1)}, bf16[16,56,128]{2,1,0:T(8,128)(2,1)S(1)}, u32[]{:S(2)}, u32[]{:S(2)}) collective-permute-start(bf16[16,56,128]{2,1,0:T(8,128)(2,1)S(1)} %get-tuple-element.51), channel_id=1, source_target_pairs={{0,4},{4,0},{1,5},{5,1},{2,6},{6,2},{3,7},{7,3},{8,12},{12,8},{9,1... | collective-permute-start | bytes 688136 | tf_op jit(solution)/shard_map/ppermute | solution.py:264
  30.5 12.7 %all-to-all-start = ((bf16[16,56,128]{2,1,0:T(8,128)(2,1)}), bf16[16,56,128]{2,1,0:T(8,128)(2,1)S(1)}, u32[]{:S(2)}, u32[]{:S(2)}) async-start(bf16[16,56,128]{2,1,0:T(8,128)(2,1)} %join.1), calls=%async_computation | async-start | bytes 458752 | tf_op jit(solution)/shard_map/all_to_all | solution.py:333
  34.2 1.0 %copy-start.4 = (bf16[512,256]{1,0:T(8,128)(2,1)S(1)}, bf16[512,256]{1,0:T(8,128)(2,1)}, u32[]{:S(2)}) copy-start(bf16[512,256]{1,0:T(8,128)(2,1)} %win_ref.3) | copy-start | bytes 786436
  35.2 1.2 %copy-start.12 = (bf16[2048,256]{1,0:T(8,128)(2,1)S(1)}, bf16[2048,256]{1,0:T(8,128)(2,1)}, u32[]{:S(2)}) copy-start(bf16[2048,256]{1,0:T(8,128)(2,1)} %copy-done.11) | copy-start | bytes 3145732
  36.4 28.0 %copy-start.6 = (s32[1,6,128]{2,0,1:T(1,128)S(1)}, s32[1,6,128]{2,0,1:T(1,128)}, u32[]{:S(2)}) copy-start(s32[1,6,128]{2,0,1:T(1,128)} %param.15) | copy-start | bytes 9220
  36.4 28.0 %copy-start.10 = (s32[1,6]{1,0:T(1,128)S(1)}, s32[1,6]{1,0:T(1,128)}, u32[]{:S(2)}) copy-start(s32[1,6]{1,0:T(1,128)} %count_ref.1) | copy-start | bytes 76
  41.2 1.3 %copy-start.16 = (f32[2048,256]{1,0:T(8,128)}, f32[2048,256]{1,0:T(8,128)S(1)}, u32[]{:S(2)}) copy-start(f32[2048,256]{1,0:T(8,128)S(1)} %get-tuple-element.75.own_ref) | copy-start | bytes 6291460
  42.5 0.6 copy-start.18
  43.9 15.8 %all-to-all-start.1 = ((bf16[8,56,128]{2,1,0:T(8,128)(2,1)}), bf16[8,56,128]{2,1,0:T(8,128)(2,1)S(1)}, u32[]{:S(2)}, u32[]{:S(2)}) async-start(bf16[8,56,128]{2,1,0:T(8,128)(2,1)} %fold.1), calls=%async_computation.1 | async-start | bytes 229376 | tf_op jit(solution)/shard_map/all_to_all | solution.py:356
  48.8 8.6 %collective-permute-start.6 = (bf16[128,256]{1,0:T(8,128)(2,1)}, bf16[128,256]{1,0:T(8,128)(2,1)S(1)}, u32[]{:S(2)}, u32[]{:S(2)}) collective-permute-start(bf16[128,256]{1,0:T(8,128)(2,1)} %copy-done.15), channel_id=1, source_target_pairs={{0,1},{1,2},{2,3},{3,0},{4,5},{5,6},{6,7},{7,4},{8,9},{9,10},{10,1... | collective-permute-start | bytes 196616 | tf_op jit(solution)/shard_map/ppermute | solution.py:264
  50.1 7.3 %collective-permute-start.7 = (bf16[128,256]{1,0:T(8,128)(2,1)}, bf16[128,256]{1,0:T(8,128)(2,1)S(1)}, u32[]{:S(2)}, u32[]{:S(2)}) collective-permute-start(bf16[128,256]{1,0:T(8,128)(2,1)} %copy-done.14), channel_id=1, source_target_pairs={{0,2},{1,3},{2,0},{3,1},{4,6},{5,7},{6,4},{7,5},{8,10},{9,11},{10,... | collective-permute-start | bytes 196616 | tf_op jit(solution)/shard_map/ppermute | solution.py:264
  52.5 4.9 %collective-permute-start.8 = (bf16[128,256]{1,0:T(8,128)(2,1)}, bf16[128,256]{1,0:T(8,128)(2,1)S(1)}, u32[]{:S(2)}, u32[]{:S(2)}) collective-permute-start(bf16[128,256]{1,0:T(8,128)(2,1)} %copy-done.13), channel_id=1, source_target_pairs={{0,3},{1,0},{2,1},{3,2},{4,7},{5,4},{6,5},{7,6},{8,11},{9,8},{10,9... | collective-permute-start | bytes 196616 | tf_op jit(solution)/shard_map/ppermute | solution.py:264
  53.7 5.6 %collective-permute-start.9 = (bf16[128,256]{1,0:T(8,128)(2,1)S(1)}, bf16[128,256]{1,0:T(8,128)(2,1)S(1)}, u32[]{:S(2)}, u32[]{:S(2)}) collective-permute-start(bf16[128,256]{1,0:T(8,128)(2,1)S(1)} %get-tuple-element.66), channel_id=1, source_target_pairs={{0,252},{4,0},{8,4},{12,8},{16,12},{20,16},{24,20},{28,24},{32,28}... | collective-permute-start | bytes 196616 | tf_op jit(solution)/shard_map/ppermute | solution.py:264
  55.8 3.9 %collective-permute-start.10 = (bf16[128,256]{1,0:T(8,128)(2,1)S(1)}, bf16[128,256]{1,0:T(8,128)(2,1)S(1)}, u32[]{:S(2)}, u32[]{:S(2)}) collective-permute-start(bf16[128,256]{1,0:T(8,128)(2,1)S(1)} %get-tuple-element.67), channel_id=1, source_target_pairs={{0,4},{4,8},{8,12},{12,16},{16,20},{20,24},{24,28},{28,32},{32,36}... | collective-permute-start | bytes 196616 | tf_op jit(solution)/shard_map/ppermute | solution.py:264
  60.4 11.2 %all-to-all-start.2 = ((bf16[16,56,128]{2,1,0:T(8,128)(2,1)}), bf16[16,56,128]{2,1,0:T(8,128)(2,1)S(1)}, u32[]{:S(2)}, u32[]{:S(2)}) async-start(bf16[16,56,128]{2,1,0:T(8,128)(2,1)} %spread.1), calls=%async_computation.2 | async-start | bytes 458752 | tf_op jit(solution)/shard_map/all_to_all | solution.py:368
  64.4 1.6 %copy-start.17 = (f32[2048,256]{1,0:T(8,128)S(1)}, f32[2048,256]{1,0:T(8,128)}, u32[]{:S(2)}) copy-start(f32[2048,256]{1,0:T(8,128)} %copy-done.16) | copy-start | bytes 6291460
  66.0 0.8 %copy-start.19 = (bf16[128,256]{1,0:T(8,128)(2,1)S(1)}, bf16[128,256]{1,0:T(8,128)(2,1)}, u32[]{:S(2)}) copy-start(bf16[128,256]{1,0:T(8,128)(2,1)} %copy-done.18) | copy-start | bytes 196612
  71.5 8.0 %collective-permute-start.11 = (bf16[16,56,128]{2,1,0:T(8,128)(2,1)S(1)}, bf16[16,56,128]{2,1,0:T(8,128)(2,1)S(1)}, u32[]{:S(2)}, u32[]{:S(2)}) collective-permute-start(bf16[16,56,128]{2,1,0:T(8,128)(2,1)S(1)} %all-to-all-done.2.keep), channel_id=1, source_target_pairs={{0,4},{4,0},{1,5},{5,1},{2,6},{6,2},{3,7},{7,3},{8,12},{12,8},{9,1... | collective-permute-start | bytes 688136 | tf_op jit(solution)/shard_map/ppermute | solution.py:264
  (3 other events, 1.9 us)

commit v4 on v3

--- a/solution.py
+++ b/solution.py
@@ -19,7 +19,9 @@
 CH = 1024
 NEAR_STEP = 16
 FAR_STEP = 8
-BACK_STEP = 32
+BACK = 512
+BACK_STEP = 64
+LAND = 512
 clip_norm = 256.0
 ln_eps = 1e-05
 F32 = jnp.float32
@@ -117,7 +119,8 @@
 
 def node_kernel(
     src_ref, dst_ref, h0, h1, h2, h3, h4, h5, feat_ref, cot_ref, vals_ref, near_ref,
-    win_ref, bin_ref, wout_ref, new_ref, gpre_ref, keep_ref, give_ref, listed, halo, total, sum_in, sum_out,
+    win_ref, bin_ref, wout_ref, new_hbm, gpre_hbm, keep_ref, give_ref, listed, halo, total, sum_in, sum_out,
+    new_rows, grad_pre, sems,
 ):
     n = list_tiles(src_ref, dst_ref, listed, NB, BUF, FAR_STEP)
     me = lax.axis_index("sub")
@@ -136,6 +139,7 @@
     lax.fori_loop(0, pl.cdiv(n, FAR_STEP), step, 0)
     w_in, b_in, w_out = win_ref[...], bin_ref[...], wout_ref[...]
     sum_bias = jnp.zeros((1, H), F32)
+    stores = []
     for c in range(N // CH):
         rows = pl.ds(c * CH, CH)
         per = CH // BLK
@@ -150,7 +154,10 @@
         centred = lifted - jnp.mean(lifted, axis=1, keepdims=True)
         inv_std = lax.rsqrt(jnp.mean(centred * centred, axis=1, keepdims=True) + ln_eps)
         normed = centred * inv_std
-        new_ref[rows, :] = (feat.astype(F32) + normed).astype(BF16)
+        new_rows[rows, :] = (feat.astype(F32) + normed).astype(BF16)
+        store = pltpu.make_async_copy(new_rows.at[rows, :], new_hbm.at[rows, :], sems.at[0, c])
+        store.start()
+        stores.append(store)
         up = cot_ref[rows, :].astype(F32)
         grad_lifted = inv_std * (
             up
@@ -159,7 +166,10 @@
         )
         grad_lifted = grad_lifted.astype(BF16)
         gpre = (dot_t1(grad_lifted, w_out) * slope).astype(BF16)
-        gpre_ref[rows, :] = gpre
+        grad_pre[rows, :] = gpre
+        store = pltpu.make_async_copy(grad_pre.at[rows, :], gpre_hbm.at[rows, :], sems.at[1, c])
+        store.start()
+        stores.append(store)
         g_out = dot_t0(act, grad_lifted)
         g_in = dot_t0(joined, gpre)
         sum_bias = sum_bias + jnp.sum(gpre.astype(F32), axis=0, keepdims=True)
@@ -180,20 +190,32 @@
                 [top[:, :HALF], low[:, :HALF], top[:, HALF:], low[:, HALF:], last], axis=0
             )
             out[k] = piece.astype(out.dtype)
+    for store in stores:
+        store.wait()
 
 
 def back_kernel(
-    src_ref, dst_ref, gpre_ref, cot_ref, vals_ref, win_ref, own_ref, o0, o1, o2, o3, o4, o5, grad_agg, total
+    src_ref, dst_ref, vals_ref, gpre_hbm, win_hbm, cot_hbm, own_hbm, o0, o1, o2, o3, o4, o5,
+    gpre, win, cot, grad_agg, total, sems,
 ):
-    w_in = win_ref[...]
-    for c in range(N // CH):
-        rows = pl.ds(c * CH, CH)
-        per = CH // BLK
-        joined = dot_t1(gpre_ref[rows, :], w_in)
+    loads = [
+        pltpu.make_async_copy(win_hbm, win, sems.at[0]),
+        pltpu.make_async_copy(gpre_hbm, gpre, sems.at[1]),
+        pltpu.make_async_copy(cot_hbm, cot, sems.at[2]),
+    ]
+    for load in loads:
+        load.start()
+    total[pl.ds(NB, PEERS)] = jnp.zeros((PEERS, BLK, H), F32)
+    for load in loads:
+        load.wait()
+    w_in = win[...]
+    per = BACK // BLK
+    for c in range(N // BACK):
+        rows = pl.ds(c * BACK, BACK)
+        joined = dot_t1(gpre[rows, :], w_in)
         grad_agg[rows, :] = joined[:, H:].astype(BF16)
-        direct = cot_ref[rows, :].astype(F32) + joined[:, :H]
+        direct = cot[rows, :].astype(F32) + joined[:, :H]
         total[pl.ds(c * per, per)] = direct.reshape(per, BLK, H)
-    total[pl.ds(NB, PEERS)] = jnp.zeros((PEERS, BLK, H), F32)
 
     def step(i, _):
         for u in range(BACK_STEP):
@@ -204,27 +226,50 @@
         return 0
 
     lax.fori_loop(0, T // BACK_STEP, step, 0)
-    own_ref[...] = total[pl.ds(0, NB)].reshape(N, H)
+    store = pltpu.make_async_copy(total.at[pl.ds(0, NB)], own_hbm, sems.at[3])
+    store.start()
     me = lax.axis_index("sub")
     for d, o in enumerate((o0, o1, o2, o3, o4, o5)):
         q = lax.rem(me + d, SUB) if d < SUB else d
         o[...] = total[NB + q].astype(BF16)
-
-
-def land_kernel(rows_ref, count_ref, r0, r1, r2, r3, r4, r5, own_ref, out_ref):
+    store.wait()
+
+
+def land_kernel(
+    rows_hbm, count_hbm, r0, r1, r2, r3, r4, r5, own_hbm, out_hbm, rows_ref, count, own, sems
+):
+    loads = [
+        pltpu.make_async_copy(rows_hbm, rows_ref, sems.at[0]),
+        pltpu.make_async_copy(count_hbm, count, sems.at[1]),
+        pltpu.make_async_copy(own_hbm, own, sems.at[2]),
+    ]
+    for load in loads:
+        load.start()
+    for load in loads[:2]:
+        load.wait()
     me = lax.axis_index("sub")
     lane = lax.broadcasted_iota(jnp.int32, (1, BLK), 1)
     ids = []
     for d in range(PEERS):
         q = lax.rem(me + SUB - d, SUB) if d < SUB else d
-        ids.append(jnp.where(lane < count_ref[0, q], rows_ref[q], -1))
+        ids.append(jnp.where(lane < count[0, q], rows_ref[q], -1))
     ids = jnp.concatenate(ids, axis=1)
     back = jnp.concatenate([r[...] for r in (r0, r1, r2, r3, r4, r5)], axis=0)
-    for c in range(N // CH):
-        rows = pl.ds(c * CH, CH)
-        hot = lax.broadcasted_iota(jnp.int32, (CH, PEERS * BLK), 0) + c * CH == ids
-        hot = jnp.where(hot, 1.0, 0.0).astype(BF16)
-        out_ref[rows, :] = own_ref[rows, :] + dot(hot, back)
+    stores = []
+    for c in range(N // LAND):
+        node = lax.broadcasted_iota(jnp.int32, (LAND, PEERS * BLK), 0) + c * LAND
+        hot = jnp.where(node == ids, 1.0, 0.0).astype(BF16)
+        landed = dot(hot, back)
+        if c == 0:
+            loads[2].wait()
+        per = LAND // BLK
+        blocks = pl.ds(c * per, per)
+        own[blocks] += landed.reshape(per, BLK, H)
+        store = pltpu.make_async_copy(own.at[blocks], out_hbm.at[blocks], sems.at[3 + c])
+        store.start()
+        stores.append(store)
+    for store in stores:
+        store.wait()
 
 
 def join_kernel(keep, other, out_ref):
@@ -264,6 +309,10 @@
     return lax.ppermute(value, axis, [(i, (i + by) % size) for i in range(size)])
 
 
+def in_hbm(*values):
+    return [pltpu.with_memory_space_constraint(v, pltpu.HBM) for v in values]
+
+
 def exchange(slots):
     got = [slots[0]]
     got += [shift(slots[d], "sub", d, SUB) for d in range(1, SUB)]
@@ -291,7 +340,7 @@
         ],
         compiler_params=params(24),
         name="pick",
-    )(*[pltpu.with_memory_space_constraint(v, pltpu.HBM) for v in (by_slot, halo_count, feat)])
+    )(*in_hbm(by_slot, halo_count, feat))
     got, dom = exchange(slots)
     got += [shift(slots[4], DOM, 1, dom), shift(slots[5], DOM, -1, dom)]
     near = pl.pallas_call(
@@ -310,18 +359,21 @@
         compiler_params=params(24),
         cost_estimate=pl.CostEstimate(flops=800_000_000, bytes_accessed=6_000_000, transcendentals=0),
         name="near",
-    )(*[pltpu.with_memory_space_constraint(v, pltpu.HBM) for v in (src, dst, feat, vals)])
+    )(*in_hbm(src, dst, feat, vals))
     new_rows, gpre, keep, give = pl.pallas_call(
         node_kernel,
-        out_shape=[sds((N, H), BF16), sds((N, H), BF16), sds(halves, F32), sds(halves, BF16)],
+        out_shape=[sds((N, H), BF16), pltpu.HBM((N, H), BF16), sds(halves, F32), sds(halves, BF16)],
         in_specs=[SM, SM] + [VM] * 13,
-        out_specs=[VM] * 4,
+        out_specs=[HB] * 2 + [VM] * 2,
         scratch_shapes=[
             pltpu.SMEM((T + NEAR_STEP,), jnp.int32),
             pltpu.VMEM((PEERS, BLK, H), BF16),
             pltpu.VMEM((NB + 1, BLK, H), F32),
             pltpu.VMEM((2 * H, H), F32),
             pltpu.VMEM((H, H), F32),
+            pltpu.VMEM((N, H), BF16),
+            pltpu.VMEM((N, H), BF16),
+            pltpu.SemaphoreType.DMA((2, N // CH)),
         ],
         compiler_params=params(32),
         name="node",
@@ -331,17 +383,24 @@
         join_kernel, out_shape=sds(halves, BF16), in_specs=[VM] * 2, out_specs=VM, compiler_params=params(4), name="join"
     )(keep, given)
     parts = lax.all_to_all(joined, PLANE, split_axis=0, concat_axis=0, tiled=True)
-    back = pl.pallas_call(
+    own, *slots = pl.pallas_call(
         back_kernel,
-        out_shape=[sds((N, H), F32)] + [block] * PEERS,
-        in_specs=[SM, SM] + [VM] * 4,
-        out_specs=[VM] * 7,
-        scratch_shapes=[pltpu.VMEM((N, H), BF16), pltpu.VMEM((BUF, BLK, H), F32)],
-        compiler_params=params(32),
+        out_shape=[pltpu.HBM((NB, BLK, H), F32)] + [block] * PEERS,
+        in_specs=[SM, SM, VM] + [HB] * 3,
+        out_specs=[HB] + [VM] * PEERS,
+        scratch_shapes=[
+            pltpu.VMEM((N, H), BF16),
+            pltpu.VMEM((2 * H, H), BF16),
+            pltpu.VMEM((N, H), BF16),
+            pltpu.VMEM((N, H), BF16),
+            pltpu.VMEM((BUF, BLK, H), F32),
+            pltpu.SemaphoreType.DMA((4,)),
+        ],
+        compiler_params=params(20),
         cost_estimate=pl.CostEstimate(flops=4_000_000_000, bytes_accessed=9_000_000, transcendentals=0),
         name="back",
-    )(src, dst, gpre, cot, vals, w_in)
-    own, slots = back[0], back[1:]
+    )(src, dst, vals, *in_hbm(gpre, w_in, cot))
+    early, late = (), (1, 2, 3, 4, 5)
     parts, own = lax.optimization_barrier((parts, own))
     depth = lax.axis_size("z")
     paired = pl.pallas_call(
@@ -352,10 +411,18 @@
         compiler_params=params(4),
         name="fold",
     )(parts)
-    paired, *slots = lax.optimization_barrier((paired, *slots))
+    got = {0: slots[0]}
+    send = {d: (lambda v, d=d: shift(v, "sub", d, SUB)) for d in range(1, SUB)}
+    send[4] = lambda v: shift(v, DOM, -1, dom)
+    send[5] = lambda v: shift(v, DOM, 1, dom)
+    for d in early:
+        got[d] = send[d](slots[d])
+    held = [slots[d] for d in late]
+    paired, *held = lax.optimization_barrier((paired, *held))
     column = lax.all_to_all(paired, "z", split_axis=0, concat_axis=0, tiled=True)
-    got, dom = exchange(slots)
-    got += [shift(slots[4], DOM, -1, dom), shift(slots[5], DOM, 1, dom)]
+    for d, slot in zip(late, held):
+        got[d] = send[d](slot)
+    got = [got[d] for d in range(PEERS)]
     column, *got = lax.optimization_barrier((column, *got))
     spread = pl.pallas_call(
         spread_kernel,
@@ -368,13 +435,19 @@
     whole = lax.all_to_all(spread, PLANE, split_axis=0, concat_axis=0, tiled=True)
     grad_features = pl.pallas_call(
         land_kernel,
-        out_shape=sds((N, H), F32),
-        in_specs=[VM, SM] + [VM] * 7,
-        out_specs=VM,
-        compiler_params=params(24),
-        cost_estimate=pl.CostEstimate(flops=3_000_000_000, bytes_accessed=5_000_000, transcendentals=0),
+        out_shape=sds((NB, BLK, H), F32),
+        in_specs=[HB] * 2 + [VM] * PEERS + [HB],
+        out_specs=HB,
+        scratch_shapes=[
+            pltpu.VMEM((PEERS, 1, BLK), jnp.int32),
+            pltpu.SMEM((1, PEERS), jnp.int32),
+            pltpu.VMEM((NB, BLK, H), F32),
+            pltpu.SemaphoreType.DMA((3 + N // LAND,)),
+        ],
+        compiler_params=params(20),
+        cost_estimate=pl.CostEstimate(flops=5_000_000_000, bytes_accessed=9_000_000, transcendentals=0),
         name="land",
-    )(by_slot, halo_count, *got, own)
+    )(*in_hbm(by_slot, halo_count), *got, *in_hbm(own)).reshape(N, H)
     whole, grad_features = lax.optimization_barrier((whole, grad_features))
     other = shift(whole, "core", 1, 2)
     g_in, g_bias, g_out = pl.pallas_call(

time: 81.1 us -> 77 us (0.949)
  local copies, waits for them, and re-layouts: 9.4 us -> 0.04 us
  waiting for transfers between devices: 6.49 us -> 9.92 us
  Pallas kernels: 21.8 us -> 25 us
  starting transfers between devices: 42.1 us -> 40.7 us
    unnamed x40 -> x16, local copies, waits for them, and re-layouts: 9.4 us -> 0.04 us
    pallas_call x3, Pallas kernels: 12.2 us -> 15.5 us  [the longest x1 6.45 us: local(): pl.pallas_call(node_kernel, out_shape=[sds((N, H), BF16), pltpu.HBM((N, H...]
    ppermute x12, starting transfers between devices: 29.5 us -> 27.5 us  [shift(): lax.ppermute(value, axis, [(i, (i + by) % size) for i in range(size)])]
    all_to_all x1, waiting for transfers between devices: 1.84 us -> 3.64 us  [local(): lax.all_to_all(spread, PLANE, split_axis=0, concat_axis=0, tiled=True)]
    all_to_all x1, waiting for transfers between devices: 0.01 us -> 1.64 us  [local(): lax.all_to_all(joined, PLANE, split_axis=0, concat_axis=0, tiled=True)]
  transfers between devices with their start and end apart: 15 -> 15, of which waited for: 6 -> 6; matrix products, arithmetic and copies ran while one was open for 0% -> 0% of each run, Pallas kernels for 11% -> 16%
where the time goes in v4:
time: 77 us; the launch traced here: 76.5 us
  starting transfers between devices  40.7 us (53%)
  Pallas kernels  25 us (32%)
  waiting for transfers between devices  9.92 us (13%)
  between operations  0.82 us (1%)
    ppermute x12, starting transfers between devices, shift(): lax.ppermute(value, axis, [(i, (i + by) % size) for i in range(size)])  27.5 us
    pallas_call x1, Pallas kernels, local(): pl.pallas_call(node_kernel, out_shape=[sds((N, H), BF16), pltpu.HBM((N, H...  6.45 us
    all_to_all x1, starting transfers between devices, local(): lax.all_to_all(paired, 'z', split_axis=0, concat_axis=0, tiled=True)  5.64 us
    pallas_call x1, Pallas kernels, local(): pl.pallas_call(back_kernel, out_shape=[pltpu.HBM((NB, BLK, H), F32)] + [b...  5.55 us
    ppermute x12, waiting for transfers between devices, shift(): lax.ppermute(value, axis, [(i, (i + by) % size) for i in range(size)])  4.64 us
    all_to_all x1, starting transfers between devices, local(): lax.all_to_all(spread, PLANE, split_axis=0, concat_axis=0, tiled=True)  3.92 us
    all_to_all x1, starting transfers between devices, local(): lax.all_to_all(joined, PLANE, split_axis=0, concat_axis=0, tiled=True)  3.71 us
    all_to_all x1, waiting for transfers between devices, local(): lax.all_to_all(spread, PLANE, split_axis=0, concat_axis=0, tiled=True)  3.64 us
  transfers between devices with their start and end apart: 15, of which 6 were waited for; matrix products, arithmetic and copies ran while one was open for 0% of the time, Pallas kernels for 16%

profile of v4, /device:TPU:1, one launch (start us, length us, event | category | flops | bytes accessed | tf_op | source)
XLA Modules:
  0.0 76.5 jit_solution(10971173228976718535)
XLA Ops:
  0.6 2.8 %pick.1 = (bf16[128,256]{1,0:T(8,128)(2,1)S(1)}, bf16[128,256]{1,0:T(8,128)(2,1)S(1)}, bf16[128,256]{1,0:T(8,128)(2,1)S(1)}, bf16[128,256]{1,0:T(8,128)(2,1)S(1)...) custom-call(s32[6,1,128]{2,1,0:T(1,128)} %bitcast.5, s32[1,6]{1,0:T(1,128)} %count_hbm.3, ...), custom_call_target="tpu_custom_call" | custom-call | tf_op jit(solution)/shard_map/pick/pallas_call | solution.py:329
  3.4 2.2 %collective-permute-start = (bf16[128,256]{1,0:T(8,128)(2,1)S(1)}, bf16[128,256]{1,0:T(8,128)(2,1)S(1)}, u32[]{:S(2)}, u32[]{:S(2)}) collective-permute-start(bf16[128,256]{1,0:T(8,128)(2,1)S(1)} %get-tuple-element.43), channel_id=1, source_target_pairs={{0,1},{1,2},{2,3},{3,0},{4,5},{5,6},{6,7},{7,4},{8,9},{9,10},{10,1... | collective-permute-start | bytes 196616 | tf_op jit(solution)/shard_map/ppermute | solution.py:309
  5.6 2.6 %collective-permute-start.1 = (bf16[128,256]{1,0:T(8,128)(2,1)S(1)}, bf16[128,256]{1,0:T(8,128)(2,1)S(1)}, u32[]{:S(2)}, u32[]{:S(2)}) collective-permute-start(bf16[128,256]{1,0:T(8,128)(2,1)S(1)} %get-tuple-element.44), channel_id=1, source_target_pairs={{0,2},{1,3},{2,0},{3,1},{4,6},{5,7},{6,4},{7,5},{8,10},{9,11},{10,... | collective-permute-start | bytes 196616 | tf_op jit(solution)/shard_map/ppermute | solution.py:309
  8.2 1.1 %collective-permute-start.2 = (bf16[128,256]{1,0:T(8,128)(2,1)S(1)}, bf16[128,256]{1,0:T(8,128)(2,1)S(1)}, u32[]{:S(2)}, u32[]{:S(2)}) collective-permute-start(bf16[128,256]{1,0:T(8,128)(2,1)S(1)} %get-tuple-element.45), channel_id=1, source_target_pairs={{0,3},{1,0},{2,1},{3,2},{4,7},{5,4},{6,5},{7,6},{8,11},{9,8},{10,9... | collective-permute-start | bytes 196616 | tf_op jit(solution)/shard_map/ppermute | solution.py:309
  9.3 3.0 %collective-permute-start.3 = (bf16[128,256]{1,0:T(8,128)(2,1)S(1)}, bf16[128,256]{1,0:T(8,128)(2,1)S(1)}, u32[]{:S(2)}, u32[]{:S(2)}) collective-permute-start(bf16[128,256]{1,0:T(8,128)(2,1)S(1)} %get-tuple-element.46), channel_id=1, source_target_pairs={{0,4},{4,8},{8,12},{12,16},{16,20},{20,24},{24,28},{28,32},{32,36}... | collective-permute-start | bytes 196616 | tf_op jit(solution)/shard_map/ppermute | solution.py:309
  12.4 0.0 copy-start.5
  12.4 0.0 copy-start.6
  12.4 0.1 collective-permute-start.4
  12.5 3.5 %near.1.near_ref = f32[17,128,256]{2,1,0:T(8,128)S(1)} custom-call(s32[64]{0:T(128)} %src_ref.3, s32[64]{0:T(128)} %dst_ref.3, bf16[2048,256]{1,0:T(8,128)(2,1)} %feat_ref.1, bf16[64,128,128]{2,1,0:T(8,128)(2,1)} %vals_ref.3), custom_call_target="tpu_custom_call" | custom-call | flops 800000000 | bytes 6000000 | tf_op jit(solution)/shard_map/near/pallas_call | solution.py:346
  16.0 0.2 collective-permute-done.4.h5
  16.2 6.5 %node.1 = (bf16[2048,256]{1,0:T(8,128)(2,1)}, bf16[2048,256]{1,0:T(8,128)(2,1)}, f32[16,56,128]{2,1,0:T(8,128)S(1)}, bf16[16,56,128]{2,1,0:T(8,128)(2,1)S(1)}) custom-call(s32[64]{0:T(128)S(1)} %copy-done.5, s32[64]{0:T(128)S(1)} %copy-done.6, bf16[128,256]{1,0:T(8,128)(2,1)S(1)} %get-tuple-element.42.h0, bf16[128,256]{1,0:T(8,128)(2,1)S(1)} %collective-permute-done.h1, ...), custom_call_target="tpu_custom_call" | custom-call | tf_op jit(solution)/shard_map/node/pallas_call | solution.py:363
  22.7 4.6 %collective-permute-start.5 = (bf16[16,56,128]{2,1,0:T(8,128)(2,1)S(1)}, bf16[16,56,128]{2,1,0:T(8,128)(2,1)S(1)}, u32[]{:S(2)}, u32[]{:S(2)}) collective-permute-start(bf16[16,56,128]{2,1,0:T(8,128)(2,1)S(1)} %get-tuple-element.50), channel_id=1, source_target_pairs={{0,4},{4,0},{1,5},{5,1},{2,6},{6,2},{3,7},{7,3},{8,12},{12,8},{9,1... | collective-permute-start | bytes 688136 | tf_op jit(solution)/shard_map/ppermute | solution.py:309
  27.3 1.1 %collective-permute-done.5.other = bf16[16,56,128]{2,1,0:T(8,128)(2,1)S(1)} collective-permute-done((bf16[16,56,128]{2,1,0:T(8,128)(2,1)S(1)}, bf16[16,56,128]{2,1,0:T(8,128)(2,1)S(1)}, u32[]{:S(2)}, u32[]{:S(2)}) %collective-permute-start.5) | collective-permute-done | bytes 229408 | tf_op jit(solution)/shard_map/ppermute | solution.py:309
  28.4 0.7 join.1
  29.2 3.7 %all-to-all-start = ((bf16[16,56,128]{2,1,0:T(8,128)(2,1)}), bf16[16,56,128]{2,1,0:T(8,128)(2,1)S(1)}, u32[]{:S(2)}, u32[]{:S(2)}) async-start(bf16[16,56,128]{2,1,0:T(8,128)(2,1)} %join.1), calls=%async_computation | async-start | bytes 458752 | tf_op jit(solution)/shard_map/all_to_all | solution.py:385
  32.9 5.6 %back.1 = (f32[16,128,256]{2,1,0:T(8,128)}, bf16[128,256]{1,0:T(8,128)(2,1)S(1)}, bf16[128,256]{1,0:T(8,128)(2,1)S(1)}, bf16[128,256]{1,0:T(8,128)(2,1)S(1)}, bf...) custom-call(s32[64]{0:T(128)S(1)} %copy-done.5, s32[64]{0:T(128)S(1)} %copy-done.6, ...), custom_call_target="tpu_custom_call" | custom-call | flops 4000000000 | bytes 9000000 | tf_op jit(solution)/shard_map/back/pallas_call | solution.py:386
  38.5 1.6 %all-to-all-done.parts = bf16[16,56,128]{2,1,0:T(8,128)(2,1)S(1)} async-done(((bf16[16,56,128]{2,1,0:T(8,128)(2,1)}), bf16[16,56,128]{2,1,0:T(8,128)(2,1)S(1)}, u32[]{:S(2)}, u32[]{:S(2)}) %all-to-all-start) | async-done | bytes 229408 | tf_op jit(solution)/shard_map/all_to_all | solution.py:385
  40.1 0.7 fold.1
  40.8 5.6 %all-to-all-start.1 = ((bf16[8,56,128]{2,1,0:T(8,128)(2,1)}), bf16[8,56,128]{2,1,0:T(8,128)(2,1)S(1)}, u32[]{:S(2)}, u32[]{:S(2)}) async-start(bf16[8,56,128]{2,1,0:T(8,128)(2,1)} %fold.1), calls=%async_computation.1 | async-start | bytes 229376 | tf_op jit(solution)/shard_map/all_to_all | solution.py:422
  46.4 0.2 collective-permute-start.6
  46.6 1.8 %collective-permute-start.7 = (bf16[128,256]{1,0:T(8,128)(2,1)S(1)}, bf16[128,256]{1,0:T(8,128)(2,1)S(1)}, u32[]{:S(2)}, u32[]{:S(2)}) collective-permute-start(bf16[128,256]{1,0:T(8,128)(2,1)S(1)} %get-tuple-element.62), channel_id=1, source_target_pairs={{0,2},{1,3},{2,0},{3,1},{4,6},{5,7},{6,4},{7,5},{8,10},{9,11},{10,... | collective-permute-start | bytes 196616 | tf_op jit(solution)/shard_map/ppermute | solution.py:309
  48.4 1.4 %collective-permute-start.8 = (bf16[128,256]{1,0:T(8,128)(2,1)S(1)}, bf16[128,256]{1,0:T(8,128)(2,1)S(1)}, u32[]{:S(2)}, u32[]{:S(2)}) collective-permute-start(bf16[128,256]{1,0:T(8,128)(2,1)S(1)} %get-tuple-element.63), channel_id=1, source_target_pairs={{0,3},{1,0},{2,1},{3,2},{4,7},{5,4},{6,5},{7,6},{8,11},{9,8},{10,9... | collective-permute-start | bytes 196616 | tf_op jit(solution)/shard_map/ppermute | solution.py:309
  49.8 2.7 %collective-permute-start.9 = (bf16[128,256]{1,0:T(8,128)(2,1)S(1)}, bf16[128,256]{1,0:T(8,128)(2,1)S(1)}, u32[]{:S(2)}, u32[]{:S(2)}) collective-permute-start(bf16[128,256]{1,0:T(8,128)(2,1)S(1)} %get-tuple-element.64), channel_id=1, source_target_pairs={{0,252},{4,0},{8,4},{12,8},{16,12},{20,16},{24,20},{28,24},{32,28}... | collective-permute-start | bytes 196616 | tf_op jit(solution)/shard_map/ppermute | solution.py:309
  52.6 1.6 %collective-permute-start.10 = (bf16[128,256]{1,0:T(8,128)(2,1)S(1)}, bf16[128,256]{1,0:T(8,128)(2,1)S(1)}, u32[]{:S(2)}, u32[]{:S(2)}) collective-permute-start(bf16[128,256]{1,0:T(8,128)(2,1)S(1)} %get-tuple-element.65), channel_id=1, source_target_pairs={{0,4},{4,8},{8,12},{12,16},{16,20},{20,24},{24,28},{28,32},{32,36}... | collective-permute-start | bytes 196616 | tf_op jit(solution)/shard_map/ppermute | solution.py:309
  54.2 2.2 %collective-permute-done.9.r4 = bf16[128,256]{1,0:T(8,128)(2,1)S(1)} collective-permute-done((bf16[128,256]{1,0:T(8,128)(2,1)S(1)}, bf16[128,256]{1,0:T(8,128)(2,1)S(1)}, u32[]{:S(2)}, u32[]{:S(2)}) %collective-permute-start.9) | collective-permute-done | bytes 65568 | tf_op jit(solution)/shard_map/ppermute | solution.py:309
  56.4 0.7 spread.1
  57.2 3.9 %all-to-all-start.2 = ((bf16[16,56,128]{2,1,0:T(8,128)(2,1)}), bf16[16,56,128]{2,1,0:T(8,128)(2,1)S(1)}, u32[]{:S(2)}, u32[]{:S(2)}) async-start(bf16[16,56,128]{2,1,0:T(8,128)(2,1)} %spread.1), calls=%async_computation.2 | async-start | bytes 458752 | tf_op jit(solution)/shard_map/all_to_all | solution.py:435
  61.1 3.5 %land.1 = f32[16,128,256]{2,1,0:T(8,128)} custom-call(s32[6,1,128]{2,1,0:T(1,128)} %bitcast.6, s32[1,6]{1,0:T(1,128)} %count_hbm.3, bf16[128,256]{1,0:T(8,128)(2,1)S(1)} %get-tuple-element.67.r0, bf16[128,256]{1,0:T(8,128)(2,1)S(1)} %collective-permute-done.6.r1, bf16[128,256]{1,0:T(8,128)(2,1)S(1)} %collective-permute-done.7.r2, ...), custom_call_target="tpu_custom_call" | custom-call | flops 5000000000 | bytes 9000000 | tf_op jit(solution)/shard_map/land/pallas_call | solution.py:436
  64.6 3.6 %all-to-all-done.2.keep = bf16[16,56,128]{2,1,0:T(8,128)(2,1)S(1)} async-done(((bf16[16,56,128]{2,1,0:T(8,128)(2,1)}), bf16[16,56,128]{2,1,0:T(8,128)(2,1)S(1)}, u32[]{:S(2)}, u32[]{:S(2)}) %all-to-all-start.2) | async-done | bytes 229408 | tf_op jit(solution)/shard_map/all_to_all | solution.py:435
  68.2 6.1 %collective-permute-start.11 = (bf16[16,56,128]{2,1,0:T(8,128)(2,1)S(1)}, bf16[16,56,128]{2,1,0:T(8,128)(2,1)S(1)}, u32[]{:S(2)}, u32[]{:S(2)}) collective-permute-start(bf16[16,56,128]{2,1,0:T(8,128)(2,1)S(1)} %all-to-all-done.2.keep), channel_id=1, source_target_pairs={{0,4},{4,0},{1,5},{5,1},{2,6},{6,2},{3,7},{7,3},{8,12},{12,8},{9,1... | collective-permute-start | bytes 688136 | tf_op jit(solution)/shard_map/ppermute | solution.py:309
  74.3 1.1 %collective-permute-done.11.other = bf16[16,56,128]{2,1,0:T(8,128)(2,1)S(1)} collective-permute-done((bf16[16,56,128]{2,1,0:T(8,128)(2,1)S(1)}, bf16[16,56,128]{2,1,0:T(8,128)(2,1)S(1)}, u32[]{:S(2)}, u32[]{:S(2)}) %collective-permute-start.11) | collective-permute-done | bytes 229408 | tf_op jit(solution)/shard_map/ppermute | solution.py:309
  75.4 1.1 %clip.1 = (f32[512,256]{1,0:T(8,128)}, f32[1,256]{1,0:T(1,128)}, f32[256,256]{1,0:T(8,128)}) custom-call(bf16[16,56,128]{2,1,0:T(8,128)(2,1)S(1)} %all-to-all-done.2.keep, bf16[16,56,128]{2,1,0:T(8,128)(2,1)S(1)} %collective-permute-done.11.other), custom_call_target="tpu_custom_call" | custom-call | tf_op jit(solution)/shard_map/clip/pallas_call | solution.py:453
  (23 shorter events, 0.1 us)
Async XLA Ops:
  3.4 12.6 %collective-permute-start = (bf16[128,256]{1,0:T(8,128)(2,1)S(1)}, bf16[128,256]{1,0:T(8,128)(2,1)S(1)}, u32[]{:S(2)}, u32[]{:S(2)}) collective-permute-start(bf16[128,256]{1,0:T(8,128)(2,1)S(1)} %get-tuple-element.43), channel_id=1, source_target_pairs={{0,1},{1,2},{2,3},{3,0},{4,5},{5,6},{6,7},{7,4},{8,9},{9,10},{10,1... | collective-permute-start | bytes 196616 | tf_op jit(solution)/shard_map/ppermute | solution.py:309
  5.6 10.4 %collective-permute-start.1 = (bf16[128,256]{1,0:T(8,128)(2,1)S(1)}, bf16[128,256]{1,0:T(8,128)(2,1)S(1)}, u32[]{:S(2)}, u32[]{:S(2)}) collective-permute-start(bf16[128,256]{1,0:T(8,128)(2,1)S(1)} %get-tuple-element.44), channel_id=1, source_target_pairs={{0,2},{1,3},{2,0},{3,1},{4,6},{5,7},{6,4},{7,5},{8,10},{9,11},{10,... | collective-permute-start | bytes 196616 | tf_op jit(solution)/shard_map/ppermute | solution.py:309
  8.2 7.8 %collective-permute-start.2 = (bf16[128,256]{1,0:T(8,128)(2,1)S(1)}, bf16[128,256]{1,0:T(8,128)(2,1)S(1)}, u32[]{:S(2)}, u32[]{:S(2)}) collective-permute-start(bf16[128,256]{1,0:T(8,128)(2,1)S(1)} %get-tuple-element.45), channel_id=1, source_target_pairs={{0,3},{1,0},{2,1},{3,2},{4,7},{5,4},{6,5},{7,6},{8,11},{9,8},{10,9... | collective-permute-start | bytes 196616 | tf_op jit(solution)/shard_map/ppermute | solution.py:309
  9.3 6.7 %collective-permute-start.3 = (bf16[128,256]{1,0:T(8,128)(2,1)S(1)}, bf16[128,256]{1,0:T(8,128)(2,1)S(1)}, u32[]{:S(2)}, u32[]{:S(2)}) collective-permute-start(bf16[128,256]{1,0:T(8,128)(2,1)S(1)} %get-tuple-element.46), channel_id=1, source_target_pairs={{0,4},{4,8},{8,12},{12,16},{16,20},{20,24},{24,28},{28,32},{32,36}... | collective-permute-start | bytes 196616 | tf_op jit(solution)/shard_map/ppermute | solution.py:309
  12.4 3.8 %copy-start = (bf16[2048,256]{1,0:T(8,128)(2,1)S(1)}, bf16[2048,256]{1,0:T(8,128)(2,1)}, u32[]{:S(2)}) copy-start(bf16[2048,256]{1,0:T(8,128)(2,1)} %feat_ref.1) | copy-start | bytes 3145732
  12.4 3.8 %copy-start.1 = (bf16[64,128,128]{2,1,0:T(8,128)(2,1)S(1)}, bf16[64,128,128]{2,1,0:T(8,128)(2,1)}, u32[]{:S(2)}) copy-start(bf16[64,128,128]{2,1,0:T(8,128)(2,1)} %vals_ref.3) | copy-start | bytes 6291460
  12.4 3.8 %copy-start.2 = (bf16[2048,256]{1,0:T(8,128)(2,1)S(1)}, bf16[2048,256]{1,0:T(8,128)(2,1)}, u32[]{:S(2)}) copy-start(bf16[2048,256]{1,0:T(8,128)(2,1)} %cot_hbm.1) | copy-start | bytes 3145732
  12.4 3.8 %copy-start.3 = (bf16[512,256]{1,0:T(8,128)(2,1)S(1)}, bf16[512,256]{1,0:T(8,128)(2,1)}, u32[]{:S(2)}) copy-start(bf16[512,256]{1,0:T(8,128)(2,1)} %win_hbm.1) | copy-start | bytes 786436
  12.4 3.8 %copy-start.4 = (bf16[256,256]{1,0:T(8,128)(2,1)S(1)}, bf16[256,256]{1,0:T(8,128)(2,1)}, u32[]{:S(2)}) copy-start(bf16[256,256]{1,0:T(8,128)(2,1)} %wout_ref.1) | copy-start | bytes 393220
  12.4 3.8 %copy-start.5 = (s32[64]{0:T(128)S(1)}, s32[64]{0:T(128)}, u32[]{:S(2)}) copy-start(s32[64]{0:T(128)} %src_ref.3) | copy-start | bytes 772
  12.4 3.8 %copy-start.6 = (s32[64]{0:T(128)S(1)}, s32[64]{0:T(128)}, u32[]{:S(2)}) copy-start(s32[64]{0:T(128)} %dst_ref.3) | copy-start | bytes 772
  12.4 3.8 %copy-start.7 = (f32[256]{0:T(256)S(1)}, f32[256]{0:T(256)}, u32[]{:S(2)}) copy-start(f32[256]{0:T(256)} %param.18) | copy-start | bytes 3076
  12.4 3.8 %collective-permute-start.4 = (bf16[128,256]{1,0:T(8,128)(2,1)S(1)}, bf16[128,256]{1,0:T(8,128)(2,1)S(1)}, u32[]{:S(2)}, u32[]{:S(2)}) collective-permute-start(bf16[128,256]{1,0:T(8,128)(2,1)S(1)} %get-tuple-element.47), channel_id=1, source_target_pairs={{0,252},{4,0},{8,4},{12,8},{16,12},{20,16},{24,20},{28,24},{32,28}... | collective-permute-start | bytes 196616 | tf_op jit(solution)/shard_map/ppermute | solution.py:309
  22.7 5.7 %collective-permute-start.5 = (bf16[16,56,128]{2,1,0:T(8,128)(2,1)S(1)}, bf16[16,56,128]{2,1,0:T(8,128)(2,1)S(1)}, u32[]{:S(2)}, u32[]{:S(2)}) collective-permute-start(bf16[16,56,128]{2,1,0:T(8,128)(2,1)S(1)} %get-tuple-element.50), channel_id=1, source_target_pairs={{0,4},{4,0},{1,5},{5,1},{2,6},{6,2},{3,7},{7,3},{8,12},{12,8},{9,1... | collective-permute-start | bytes 688136 | tf_op jit(solution)/shard_map/ppermute | solution.py:309
  29.2 10.9 %all-to-all-start = ((bf16[16,56,128]{2,1,0:T(8,128)(2,1)}), bf16[16,56,128]{2,1,0:T(8,128)(2,1)S(1)}, u32[]{:S(2)}, u32[]{:S(2)}) async-start(bf16[16,56,128]{2,1,0:T(8,128)(2,1)} %join.1), calls=%async_computation | async-start | bytes 458752 | tf_op jit(solution)/shard_map/all_to_all | solution.py:385
  40.8 15.7 %all-to-all-start.1 = ((bf16[8,56,128]{2,1,0:T(8,128)(2,1)}), bf16[8,56,128]{2,1,0:T(8,128)(2,1)S(1)}, u32[]{:S(2)}, u32[]{:S(2)}) async-start(bf16[8,56,128]{2,1,0:T(8,128)(2,1)} %fold.1), calls=%async_computation.1 | async-start | bytes 229376 | tf_op jit(solution)/shard_map/all_to_all | solution.py:422
  46.4 7.8 %collective-permute-start.6 = (bf16[128,256]{1,0:T(8,128)(2,1)S(1)}, bf16[128,256]{1,0:T(8,128)(2,1)S(1)}, u32[]{:S(2)}, u32[]{:S(2)}) collective-permute-start(bf16[128,256]{1,0:T(8,128)(2,1)S(1)} %get-tuple-element.61), channel_id=1, source_target_pairs={{0,1},{1,2},{2,3},{3,0},{4,5},{5,6},{6,7},{7,4},{8,9},{9,10},{10,1... | collective-permute-start | bytes 196616 | tf_op jit(solution)/shard_map/ppermute | solution.py:309
  46.6 7.6 %collective-permute-start.7 = (bf16[128,256]{1,0:T(8,128)(2,1)S(1)}, bf16[128,256]{1,0:T(8,128)(2,1)S(1)}, u32[]{:S(2)}, u32[]{:S(2)}) collective-permute-start(bf16[128,256]{1,0:T(8,128)(2,1)S(1)} %get-tuple-element.62), channel_id=1, source_target_pairs={{0,2},{1,3},{2,0},{3,1},{4,6},{5,7},{6,4},{7,5},{8,10},{9,11},{10,... | collective-permute-start | bytes 196616 | tf_op jit(solution)/shard_map/ppermute | solution.py:309
  48.4 5.8 %collective-permute-start.8 = (bf16[128,256]{1,0:T(8,128)(2,1)S(1)}, bf16[128,256]{1,0:T(8,128)(2,1)S(1)}, u32[]{:S(2)}, u32[]{:S(2)}) collective-permute-start(bf16[128,256]{1,0:T(8,128)(2,1)S(1)} %get-tuple-element.63), channel_id=1, source_target_pairs={{0,3},{1,0},{2,1},{3,2},{4,7},{5,4},{6,5},{7,6},{8,11},{9,8},{10,9... | collective-permute-start | bytes 196616 | tf_op jit(solution)/shard_map/ppermute | solution.py:309
  49.8 6.6 %collective-permute-start.9 = (bf16[128,256]{1,0:T(8,128)(2,1)S(1)}, bf16[128,256]{1,0:T(8,128)(2,1)S(1)}, u32[]{:S(2)}, u32[]{:S(2)}) collective-permute-start(bf16[128,256]{1,0:T(8,128)(2,1)S(1)} %get-tuple-element.64), channel_id=1, source_target_pairs={{0,252},{4,0},{8,4},{12,8},{16,12},{20,16},{24,20},{28,24},{32,28}... | collective-permute-start | bytes 196616 | tf_op jit(solution)/shard_map/ppermute | solution.py:309
  52.6 3.9 %collective-permute-start.10 = (bf16[128,256]{1,0:T(8,128)(2,1)S(1)}, bf16[128,256]{1,0:T(8,128)(2,1)S(1)}, u32[]{:S(2)}, u32[]{:S(2)}) collective-permute-start(bf16[128,256]{1,0:T(8,128)(2,1)S(1)} %get-tuple-element.65), channel_id=1, source_target_pairs={{0,4},{4,8},{8,12},{12,16},{16,20},{20,24},{24,28},{28,32},{32,36}... | collective-permute-start | bytes 196616 | tf_op jit(solution)/shard_map/ppermute | solution.py:309
  57.2 11.0 %all-to-all-start.2 = ((bf16[16,56,128]{2,1,0:T(8,128)(2,1)}), bf16[16,56,128]{2,1,0:T(8,128)(2,1)S(1)}, u32[]{:S(2)}, u32[]{:S(2)}) async-start(bf16[16,56,128]{2,1,0:T(8,128)(2,1)} %spread.1), calls=%async_computation.2 | async-start | bytes 458752 | tf_op jit(solution)/shard_map/all_to_all | solution.py:435
  68.2 7.2 %collective-permute-start.11 = (bf16[16,56,128]{2,1,0:T(8,128)(2,1)S(1)}, bf16[16,56,128]{2,1,0:T(8,128)(2,1)S(1)}, u32[]{:S(2)}, u32[]{:S(2)}) collective-permute-start(bf16[16,56,128]{2,1,0:T(8,128)(2,1)S(1)} %all-to-all-done.2.keep), channel_id=1, source_target_pairs={{0,4},{4,0},{1,5},{5,1},{2,6},{6,2},{3,7},{7,3},{8,12},{12,8},{9,1... | collective-permute-start | bytes 688136 | tf_op jit(solution)/shard_map/ppermute | solution.py:309

commit v5 on v4

--- a/solution.py
+++ b/solution.py
@@ -22,6 +22,7 @@
 BACK = 512
 BACK_STEP = 64
 LAND = 512
+LEGS = ((4, 5), (1, 3), (2,))
 clip_norm = 256.0
 ln_eps = 1e-05
 F32 = jnp.float32
@@ -198,20 +199,21 @@
     src_ref, dst_ref, vals_ref, gpre_hbm, win_hbm, cot_hbm, own_hbm, o0, o1, o2, o3, o4, o5,
     gpre, win, cot, grad_agg, total, sems,
 ):
-    loads = [
-        pltpu.make_async_copy(win_hbm, win, sems.at[0]),
-        pltpu.make_async_copy(gpre_hbm, gpre, sems.at[1]),
-        pltpu.make_async_copy(cot_hbm, cot, sems.at[2]),
-    ]
+    loads = [pltpu.make_async_copy(win_hbm, win, sems.at[0])]
+    for c in range(N // BACK):
+        rows = pl.ds(c * BACK, BACK)
+        loads.append(pltpu.make_async_copy(gpre_hbm.at[rows, :], gpre.at[rows, :], sems.at[2 * c + 1]))
+        loads.append(pltpu.make_async_copy(cot_hbm.at[rows, :], cot.at[rows, :], sems.at[2 * c + 2]))
     for load in loads:
         load.start()
     total[pl.ds(NB, PEERS)] = jnp.zeros((PEERS, BLK, H), F32)
-    for load in loads:
-        load.wait()
+    loads[0].wait()
     w_in = win[...]
     per = BACK // BLK
     for c in range(N // BACK):
         rows = pl.ds(c * BACK, BACK)
+        loads[2 * c + 1].wait()
+        loads[2 * c + 2].wait()
         joined = dot_t1(gpre[rows, :], w_in)
         grad_agg[rows, :] = joined[:, H:].astype(BF16)
         direct = cot[rows, :].astype(F32) + joined[:, :H]
@@ -226,7 +228,7 @@
         return 0
 
     lax.fori_loop(0, T // BACK_STEP, step, 0)
-    store = pltpu.make_async_copy(total.at[pl.ds(0, NB)], own_hbm, sems.at[3])
+    store = pltpu.make_async_copy(total.at[pl.ds(0, NB)], own_hbm, sems.at[len(loads)])
     store.start()
     me = lax.axis_index("sub")
     for d, o in enumerate((o0, o1, o2, o3, o4, o5)):
@@ -276,8 +278,22 @@
     out_ref[...] = (keep[...] + other[...].astype(F32)).astype(BF16)
 
 
-def spread_kernel(parts, out_ref):
-    whole = jnp.sum(parts[...].astype(F32), axis=0).astype(BF16)
+def fold_kernel(parts, out_ref):
+    out_ref[...] = jnp.sum(parts[...].astype(F32), axis=0)
+
+
+def add_kernel(mine, other, out_ref):
+    out_ref[...] = mine[...] + other[...]
+
+
+def copy_kernel(*refs):
+    half = len(refs) // 2
+    for a, b in zip(refs[:half], refs[half:]):
+        b[...] = a[...]
+
+
+def spread_kernel(mine, other, out_ref):
+    whole = (mine[...] + other[...]).astype(BF16)
     for i in range(out_ref.shape[0]):
         out_ref[i] = whole
 
@@ -394,44 +410,44 @@
             pltpu.VMEM((N, H), BF16),
             pltpu.VMEM((N, H), BF16),
             pltpu.VMEM((BUF, BLK, H), F32),
-            pltpu.SemaphoreType.DMA((4,)),
+            pltpu.SemaphoreType.DMA((2 + 2 * (N // BACK),)),
         ],
         compiler_params=params(20),
         cost_estimate=pl.CostEstimate(flops=4_000_000_000, bytes_accessed=9_000_000, transcendentals=0),
         name="back",
     )(src, dst, vals, *in_hbm(gpre, w_in, cot))
-    early, late = (), (1, 2, 3, 4, 5)
     parts, own = lax.optimization_barrier((parts, own))
+    piece = sds((PROWS, HALF), F32)
+    part = pl.pallas_call(
+        fold_kernel, out_shape=piece, in_specs=[VM], out_specs=VM, compiler_params=params(4), name="fold"
+    )(parts)
     depth = lax.axis_size("z")
-    paired = pl.pallas_call(
-        spread_kernel,
-        out_shape=sds((depth, PROWS, HALF), BF16),
-        in_specs=[VM],
-        out_specs=VM,
-        compiler_params=params(4),
-        name="fold",
-    )(parts)
-    got = {0: slots[0]}
     send = {d: (lambda v, d=d: shift(v, "sub", d, SUB)) for d in range(1, SUB)}
     send[4] = lambda v: shift(v, DOM, -1, dom)
     send[5] = lambda v: shift(v, DOM, 1, dom)
-    for d in early:
-        got[d] = send[d](slots[d])
-    held = [slots[d] for d in late]
-    paired, *held = lax.optimization_barrier((paired, *held))
-    column = lax.all_to_all(paired, "z", split_axis=0, concat_axis=0, tiled=True)
-    for d, slot in zip(late, held):
-        got[d] = send[d](slot)
+    got = {0: slots[0]}
+    for reach, now in zip((1, 2, 4), LEGS):
+        part, *held = lax.optimization_barrier((part, *[slots[d] for d in now]))
+        other = lax.ppermute(part, "z", [(i, i ^ reach) for i in range(depth)])
+        for d, slot in zip(now, held):
+            got[d] = send[d](slot)
+        ready = {1: (), 2: (), 4: (4, 5)}[reach]
+        other, *back = lax.optimization_barrier((other, *[got[d] for d in ready]))
+        for d, slot in zip(ready, back):
+            got[d] = slot
+        if reach < 4:
+            part = pl.pallas_call(
+                add_kernel, out_shape=piece, in_specs=[VM] * 2, out_specs=VM, compiler_params=params(4), name="add"
+            )(part, other)
     got = [got[d] for d in range(PEERS)]
-    column, *got = lax.optimization_barrier((column, *got))
     spread = pl.pallas_call(
         spread_kernel,
         out_shape=sds(halves, BF16),
-        in_specs=[VM],
+        in_specs=[VM] * 2,
         out_specs=VM,
         compiler_params=params(4),
         name="spread",
-    )(column)
+    )(part, other)
     whole = lax.all_to_all(spread, PLANE, split_axis=0, concat_axis=0, tiled=True)
     grad_features = pl.pallas_call(
         land_kernel,

time: 77 us -> 76.7 us (level)
  waiting for transfers between devices: 9.92 us -> 13.5 us
  starting transfers between devices: 40.7 us -> 37.4 us
    ppermute x0 -> x3, waiting for transfers between devices: none -> 5.84 us  [local(): other = lax.ppermute(part, 'z', [(i, i ^ reach) for i in range(depth)])]
    all_to_all x1 -> x0, starting transfers between devices: 5.64 us -> none  [local(): lax.all_to_all(paired, 'z', split_axis=0, concat_axis=0, tiled=True)]
    ppermute x0 -> x3, starting transfers between devices: none -> 4.42 us  [local(): other = lax.ppermute(part, 'z', [(i, i ^ reach) for i in range(depth)])]
    ppermute x12, starting transfers between devices: 27.5 us -> 24 us  [shift(): lax.ppermute(value, axis, [(i, (i + by) % size) for i in range(size)])]
    ppermute x12, waiting for transfers between devices: 4.64 us -> 2.26 us  [shift(): lax.ppermute(value, axis, [(i, (i + by) % size) for i in range(size)])]
    all_to_all x1, starting transfers between devices: 3.92 us -> 5.18 us  [local(): lax.all_to_all(spread, PLANE, split_axis=0, concat_axis=0, tiled=True)]
  transfers between devices with their start and end apart: 15 -> 17, of which waited for: 6 -> 6; matrix products, arithmetic and copies ran while one was open for 0% -> 0% of each run, Pallas kernels for 16% -> 18%
where the time goes in v5:
time: 76.7 us; the launch traced here: 76.4 us
  starting transfers between devices  37.4 us (49%)
  Pallas kernels  24.7 us (32%)
  waiting for transfers between devices  13.5 us (18%)
  between operations  0.9 us (1%)
    ppermute x12, starting transfers between devices, shift(): lax.ppermute(value, axis, [(i, (i + by) % size) for i in range(size)])  24 us
    pallas_call x1, Pallas kernels, local(): pl.pallas_call(node_kernel, out_shape=[sds((N, H), BF16), pltpu.HBM((N, H...  6.14 us
    ppermute x3, waiting for transfers between devices, local(): other = lax.ppermute(part, 'z', [(i, i ^ reach) for i in range(depth)])  5.84 us
    pallas_call x1, Pallas kernels, local(): pl.pallas_call(back_kernel, out_shape=[pltpu.HBM((NB, BLK, H), F32)] + [b...  5.69 us
    all_to_all x1, starting transfers between devices, local(): lax.all_to_all(spread, PLANE, split_axis=0, concat_axis=0, tiled=True)  5.18 us
    ppermute x3, starting transfers between devices, local(): other = lax.ppermute(part, 'z', [(i, i ^ reach) for i in range(depth)])  4.42 us
    pallas_call x1, Pallas kernels, local(): pl.pallas_call(near_kernel, out_shape=sds((NB + 1, BLK, H), F32), in_spec...  3.93 us
    all_to_all x1, waiting for transfers between devices, local(): lax.all_to_all(spread, PLANE, split_axis=0, concat_axis=0, tiled=True)  3.85 us
  transfers between devices with their start and end apart: 17, of which 6 were waited for; matrix products, arithmetic and copies ran while one was open for 0% of the time, Pallas kernels for 18%

profile of v5, /device:TPU:1, one launch (start us, length us, event | category | flops | bytes accessed | tf_op | source)
XLA Modules:
  0.0 76.4 jit_solution(7581375732722114661)
XLA Ops:
  0.6 2.8 %pick.1 = (bf16[128,256]{1,0:T(8,128)(2,1)S(1)}, bf16[128,256]{1,0:T(8,128)(2,1)S(1)}, bf16[128,256]{1,0:T(8,128)(2,1)S(1)}, bf16[128,256]{1,0:T(8,128)(2,1)S(1)...) custom-call(s32[6,1,128]{2,1,0:T(1,128)} %bitcast.5, s32[1,6]{1,0:T(1,128)} %count_hbm.3, ...), custom_call_target="tpu_custom_call" | custom-call | tf_op jit(solution)/shard_map/pick/pallas_call | solution.py:345
  3.4 2.2 %collective-permute-start = (bf16[128,256]{1,0:T(8,128)(2,1)S(1)}, bf16[128,256]{1,0:T(8,128)(2,1)S(1)}, u32[]{:S(2)}, u32[]{:S(2)}) collective-permute-start(bf16[128,256]{1,0:T(8,128)(2,1)S(1)} %get-tuple-element.41), channel_id=1, source_target_pairs={{0,1},{1,2},{2,3},{3,0},{4,5},{5,6},{6,7},{7,4},{8,9},{9,10},{10,1... | collective-permute-start | bytes 196616 | tf_op jit(solution)/shard_map/ppermute | solution.py:325
  5.6 2.6 %collective-permute-start.1 = (bf16[128,256]{1,0:T(8,128)(2,1)S(1)}, bf16[128,256]{1,0:T(8,128)(2,1)S(1)}, u32[]{:S(2)}, u32[]{:S(2)}) collective-permute-start(bf16[128,256]{1,0:T(8,128)(2,1)S(1)} %get-tuple-element.42), channel_id=1, source_target_pairs={{0,2},{1,3},{2,0},{3,1},{4,6},{5,7},{6,4},{7,5},{8,10},{9,11},{10,... | collective-permute-start | bytes 196616 | tf_op jit(solution)/shard_map/ppermute | solution.py:325
  8.2 1.1 %collective-permute-start.2 = (bf16[128,256]{1,0:T(8,128)(2,1)S(1)}, bf16[128,256]{1,0:T(8,128)(2,1)S(1)}, u32[]{:S(2)}, u32[]{:S(2)}) collective-permute-start(bf16[128,256]{1,0:T(8,128)(2,1)S(1)} %get-tuple-element.43), channel_id=1, source_target_pairs={{0,3},{1,0},{2,1},{3,2},{4,7},{5,4},{6,5},{7,6},{8,11},{9,8},{10,9... | collective-permute-start | bytes 196616 | tf_op jit(solution)/shard_map/ppermute | solution.py:325
  9.3 3.0 %collective-permute-start.3 = (bf16[128,256]{1,0:T(8,128)(2,1)S(1)}, bf16[128,256]{1,0:T(8,128)(2,1)S(1)}, u32[]{:S(2)}, u32[]{:S(2)}) collective-permute-start(bf16[128,256]{1,0:T(8,128)(2,1)S(1)} %get-tuple-element.44), channel_id=1, source_target_pairs={{0,4},{4,8},{8,12},{12,16},{16,20},{20,24},{24,28},{28,32},{32,36}... | collective-permute-start | bytes 196616 | tf_op jit(solution)/shard_map/ppermute | solution.py:325
  12.4 0.0 copy-start.4
  12.4 0.1 collective-permute-start.4
  12.5 3.9 %near.1.near_ref = f32[17,128,256]{2,1,0:T(8,128)S(1)} custom-call(s32[64]{0:T(128)} %src_ref.3, s32[64]{0:T(128)} %dst_ref.3, bf16[2048,256]{1,0:T(8,128)(2,1)} %feat_ref.1, bf16[64,128,128]{2,1,0:T(8,128)(2,1)} %vals_ref.3), custom_call_target="tpu_custom_call" | custom-call | flops 800000000 | bytes 6000000 | tf_op jit(solution)/shard_map/near/pallas_call | solution.py:362
  16.6 6.1 %node.1 = (bf16[2048,256]{1,0:T(8,128)(2,1)}, bf16[2048,256]{1,0:T(8,128)(2,1)}, f32[16,56,128]{2,1,0:T(8,128)S(1)}, bf16[16,56,128]{2,1,0:T(8,128)(2,1)S(1)}) custom-call(s32[64]{0:T(128)S(1)} %copy-done.5, s32[64]{0:T(128)S(1)} %copy-done.6, bf16[128,256]{1,0:T(8,128)(2,1)S(1)} %get-tuple-element.40.h0, bf16[128,256]{1,0:T(8,128)(2,1)S(1)} %collective-permute-done.h1, ...), custom_call_target="tpu_custom_call" | custom-call | tf_op jit(solution)/shard_map/node/pallas_call | solution.py:379
  22.7 5.1 %collective-permute-start.5 = (bf16[16,56,128]{2,1,0:T(8,128)(2,1)S(1)}, bf16[16,56,128]{2,1,0:T(8,128)(2,1)S(1)}, u32[]{:S(2)}, u32[]{:S(2)}) collective-permute-start(bf16[16,56,128]{2,1,0:T(8,128)(2,1)S(1)} %get-tuple-element.48), channel_id=1, source_target_pairs={{0,4},{4,0},{1,5},{5,1},{2,6},{6,2},{3,7},{7,3},{8,12},{12,8},{9,1... | collective-permute-start | bytes 688136 | tf_op jit(solution)/shard_map/ppermute | solution.py:325
  27.8 1.1 %collective-permute-done.5.other = bf16[16,56,128]{2,1,0:T(8,128)(2,1)S(1)} collective-permute-done((bf16[16,56,128]{2,1,0:T(8,128)(2,1)S(1)}, bf16[16,56,128]{2,1,0:T(8,128)(2,1)S(1)}, u32[]{:S(2)}, u32[]{:S(2)}) %collective-permute-start.5) | collective-permute-done | bytes 229408 | tf_op jit(solution)/shard_map/ppermute | solution.py:325
  28.9 0.7 join.1
  29.6 3.7 %all-to-all-start = ((bf16[16,56,128]{2,1,0:T(8,128)(2,1)}), bf16[16,56,128]{2,1,0:T(8,128)(2,1)S(1)}, u32[]{:S(2)}, u32[]{:S(2)}) async-start(bf16[16,56,128]{2,1,0:T(8,128)(2,1)} %join.1), calls=%async_computation | async-start | bytes 458752 | tf_op jit(solution)/shard_map/all_to_all | solution.py:401
  33.4 5.7 %back.1 = (f32[16,128,256]{2,1,0:T(8,128)}, bf16[128,256]{1,0:T(8,128)(2,1)S(1)}, bf16[128,256]{1,0:T(8,128)(2,1)S(1)}, bf16[128,256]{1,0:T(8,128)(2,1)S(1)}, bf...) custom-call(s32[64]{0:T(128)S(1)} %copy-done.5, s32[64]{0:T(128)S(1)} %copy-done.6, ...), custom_call_target="tpu_custom_call" | custom-call | flops 4000000000 | bytes 9000000 | tf_op jit(solution)/shard_map/back/pallas_call | solution.py:402
  39.1 1.5 %all-to-all-done.parts = bf16[16,56,128]{2,1,0:T(8,128)(2,1)S(1)} async-done(((bf16[16,56,128]{2,1,0:T(8,128)(2,1)}), bf16[16,56,128]{2,1,0:T(8,128)(2,1)S(1)}, u32[]{:S(2)}, u32[]{:S(2)}) %all-to-all-start) | async-done | bytes 229408 | tf_op jit(solution)/shard_map/all_to_all | solution.py:401
  40.6 0.1 collective-permute-start.6
  40.7 1.8 %collective-permute-start.9 = (bf16[128,256]{1,0:T(8,128)(2,1)S(1)}, bf16[128,256]{1,0:T(8,128)(2,1)S(1)}, u32[]{:S(2)}, u32[]{:S(2)}) collective-permute-start(bf16[128,256]{1,0:T(8,128)(2,1)S(1)} %get-tuple-element.60), channel_id=1, source_target_pairs={{0,252},{4,0},{8,4},{12,8},{16,12},{20,16},{24,20},{28,24},{32,28}... | collective-permute-start | bytes 196616 | tf_op jit(solution)/shard_map/ppermute | solution.py:325
  42.5 0.9 %collective-permute-done.6.other = f32[56,128]{1,0:T(8,128)S(1)} collective-permute-done((f32[56,128]{1,0:T(8,128)S(1)}, f32[56,128]{1,0:T(8,128)S(1)}, u32[]{:S(2)}, u32[]{:S(2)}) %collective-permute-start.6) | collective-permute-done | bytes 28704 | tf_op jit(solution)/shard_map/ppermute | solution.py:431
  43.4 2.4 %collective-permute-start.7 = (f32[56,128]{1,0:T(8,128)S(1)}, f32[56,128]{1,0:T(8,128)S(1)}, u32[]{:S(2)}, u32[]{:S(2)}) collective-permute-start(f32[56,128]{1,0:T(8,128)S(1)} %add.2.mine), channel_id=1, source_target_pairs={{0,16},{8,24},{16,0},{24,8},{32,48},{40,56},{48,32},{56,40},{1,17}... | collective-permute-start | bytes 86024 | tf_op jit(solution)/shard_map/ppermute | solution.py:431
  45.8 3.7 %collective-permute-start.10 = (bf16[128,256]{1,0:T(8,128)(2,1)S(1)}, bf16[128,256]{1,0:T(8,128)(2,1)S(1)}, u32[]{:S(2)}, u32[]{:S(2)}) collective-permute-start(bf16[128,256]{1,0:T(8,128)(2,1)S(1)} %get-tuple-element.61), channel_id=1, source_target_pairs={{0,4},{4,8},{8,12},{12,16},{16,20},{20,24},{24,28},{28,32},{32,36}... | collective-permute-start | bytes 196616 | tf_op jit(solution)/shard_map/ppermute | solution.py:325
  49.5 0.1 collective-permute-start.11
  49.6 2.5 %collective-permute-start.13 = (bf16[128,256]{1,0:T(8,128)(2,1)S(1)}, bf16[128,256]{1,0:T(8,128)(2,1)S(1)}, u32[]{:S(2)}, u32[]{:S(2)}) collective-permute-start(bf16[128,256]{1,0:T(8,128)(2,1)S(1)} %get-tuple-element.66), channel_id=1, source_target_pairs={{0,3},{1,0},{2,1},{3,2},{4,7},{5,4},{6,5},{7,6},{8,11},{9,8},{10,9... | collective-permute-start | bytes 196616 | tf_op jit(solution)/shard_map/ppermute | solution.py:325
  52.2 0.1 collective-permute-start.12
  52.3 1.9 %collective-permute-start.8 = (f32[56,128]{1,0:T(8,128)S(1)}, f32[56,128]{1,0:T(8,128)S(1)}, u32[]{:S(2)}, u32[]{:S(2)}) collective-permute-start(f32[56,128]{1,0:T(8,128)S(1)} %add.3.mine), channel_id=1, source_target_pairs={{0,32},{8,40},{16,48},{24,56},{32,0},{40,8},{48,16},{56,24},{1,33}... | collective-permute-start | bytes 86024 | tf_op jit(solution)/shard_map/ppermute | solution.py:431
  54.2 4.9 %collective-permute-done.8.other = f32[56,128]{1,0:T(8,128)S(1)} collective-permute-done((f32[56,128]{1,0:T(8,128)S(1)}, f32[56,128]{1,0:T(8,128)S(1)}, u32[]{:S(2)}, u32[]{:S(2)}) %collective-permute-start.8) | collective-permute-done | bytes 28704 | tf_op jit(solution)/shard_map/ppermute | solution.py:431
  59.1 0.7 spread.1
  59.8 5.2 %all-to-all-start.1 = ((bf16[16,56,128]{2,1,0:T(8,128)(2,1)}), bf16[16,56,128]{2,1,0:T(8,128)(2,1)S(1)}, u32[]{:S(2)}, u32[]{:S(2)}) async-start(bf16[16,56,128]{2,1,0:T(8,128)(2,1)} %spread.1), calls=%async_computation.1 | async-start | bytes 458752 | tf_op jit(solution)/shard_map/all_to_all | solution.py:451
  65.0 3.5 %land.1 = f32[16,128,256]{2,1,0:T(8,128)} custom-call(s32[6,1,128]{2,1,0:T(1,128)} %bitcast.6, s32[1,6]{1,0:T(1,128)} %count_hbm.3, bf16[128,256]{1,0:T(8,128)(2,1)S(1)} %get-tuple-element.63.r0, bf16[128,256]{1,0:T(8,128)(2,1)S(1)} %collective-permute-done.11.r1, bf16[128,256]{1,0:T(8,128)(2,1)S(1)} %collective-permute-done.12.r2, ...), custom_call_target="tpu_custom_call" | custom-call | flops 5000000000 | bytes 9000000 | tf_op jit(solution)/shard_map/land/pallas_call | solution.py:452
  68.5 3.9 %all-to-all-done.1.keep = bf16[16,56,128]{2,1,0:T(8,128)(2,1)S(1)} async-done(((bf16[16,56,128]{2,1,0:T(8,128)(2,1)}), bf16[16,56,128]{2,1,0:T(8,128)(2,1)S(1)}, u32[]{:S(2)}, u32[]{:S(2)}) %all-to-all-start.1) | async-done | bytes 229408 | tf_op jit(solution)/shard_map/all_to_all | solution.py:451
  72.4 1.8 %collective-permute-start.14 = (bf16[16,56,128]{2,1,0:T(8,128)(2,1)S(1)}, bf16[16,56,128]{2,1,0:T(8,128)(2,1)S(1)}, u32[]{:S(2)}, u32[]{:S(2)}) collective-permute-start(bf16[16,56,128]{2,1,0:T(8,128)(2,1)S(1)} %all-to-all-done.1.keep), channel_id=1, source_target_pairs={{0,4},{4,0},{1,5},{5,1},{2,6},{6,2},{3,7},{7,3},{8,12},{12,8},{9,1... | collective-permute-start | bytes 688136 | tf_op jit(solution)/shard_map/ppermute | solution.py:325
  74.1 1.1 %collective-permute-done.14.other = bf16[16,56,128]{2,1,0:T(8,128)(2,1)S(1)} collective-permute-done((bf16[16,56,128]{2,1,0:T(8,128)(2,1)S(1)}, bf16[16,56,128]{2,1,0:T(8,128)(2,1)S(1)}, u32[]{:S(2)}, u32[]{:S(2)}) %collective-permute-start.14) | collective-permute-done | bytes 229408 | tf_op jit(solution)/shard_map/ppermute | solution.py:325
  75.3 1.1 %clip.1 = (f32[512,256]{1,0:T(8,128)}, f32[1,256]{1,0:T(1,128)}, f32[256,256]{1,0:T(8,128)}) custom-call(bf16[16,56,128]{2,1,0:T(8,128)(2,1)S(1)} %all-to-all-done.1.keep, bf16[16,56,128]{2,1,0:T(8,128)(2,1)S(1)} %collective-permute-done.14.other), custom_call_target="tpu_custom_call" | custom-call | tf_op jit(solution)/shard_map/clip/pallas_call | solution.py:469
  (29 shorter events, 0.1 us)
Async XLA Ops:
  3.4 13.0 %collective-permute-start = (bf16[128,256]{1,0:T(8,128)(2,1)S(1)}, bf16[128,256]{1,0:T(8,128)(2,1)S(1)}, u32[]{:S(2)}, u32[]{:S(2)}) collective-permute-start(bf16[128,256]{1,0:T(8,128)(2,1)S(1)} %get-tuple-element.41), channel_id=1, source_target_pairs={{0,1},{1,2},{2,3},{3,0},{4,5},{5,6},{6,7},{7,4},{8,9},{9,10},{10,1... | collective-permute-start | bytes 196616 | tf_op jit(solution)/shard_map/ppermute | solution.py:325
  5.6 10.8 %collective-permute-start.1 = (bf16[128,256]{1,0:T(8,128)(2,1)S(1)}, bf16[128,256]{1,0:T(8,128)(2,1)S(1)}, u32[]{:S(2)}, u32[]{:S(2)}) collective-permute-start(bf16[128,256]{1,0:T(8,128)(2,1)S(1)} %get-tuple-element.42), channel_id=1, source_target_pairs={{0,2},{1,3},{2,0},{3,1},{4,6},{5,7},{6,4},{7,5},{8,10},{9,11},{10,... | collective-permute-start | bytes 196616 | tf_op jit(solution)/shard_map/ppermute | solution.py:325
  8.2 8.2 %collective-permute-start.2 = (bf16[128,256]{1,0:T(8,128)(2,1)S(1)}, bf16[128,256]{1,0:T(8,128)(2,1)S(1)}, u32[]{:S(2)}, u32[]{:S(2)}) collective-permute-start(bf16[128,256]{1,0:T(8,128)(2,1)S(1)} %get-tuple-element.43), channel_id=1, source_target_pairs={{0,3},{1,0},{2,1},{3,2},{4,7},{5,4},{6,5},{7,6},{8,11},{9,8},{10,9... | collective-permute-start | bytes 196616 | tf_op jit(solution)/shard_map/ppermute | solution.py:325
  9.3 7.2 %collective-permute-start.3 = (bf16[128,256]{1,0:T(8,128)(2,1)S(1)}, bf16[128,256]{1,0:T(8,128)(2,1)S(1)}, u32[]{:S(2)}, u32[]{:S(2)}) collective-permute-start(bf16[128,256]{1,0:T(8,128)(2,1)S(1)} %get-tuple-element.44), channel_id=1, source_target_pairs={{0,4},{4,8},{8,12},{12,16},{16,20},{20,24},{24,28},{28,32},{32,36}... | collective-permute-start | bytes 196616 | tf_op jit(solution)/shard_map/ppermute | solution.py:325
  12.4 4.1 %copy-start = (bf16[2048,256]{1,0:T(8,128)(2,1)S(1)}, bf16[2048,256]{1,0:T(8,128)(2,1)}, u32[]{:S(2)}) copy-start(bf16[2048,256]{1,0:T(8,128)(2,1)} %feat_ref.1) | copy-start | bytes 3145732
  12.4 4.2 %copy-start.1 = (bf16[64,128,128]{2,1,0:T(8,128)(2,1)S(1)}, bf16[64,128,128]{2,1,0:T(8,128)(2,1)}, u32[]{:S(2)}) copy-start(bf16[64,128,128]{2,1,0:T(8,128)(2,1)} %vals_ref.3) | copy-start | bytes 6291460
  12.4 4.2 %copy-start.2 = (bf16[2048,256]{1,0:T(8,128)(2,1)S(1)}, bf16[2048,256]{1,0:T(8,128)(2,1)}, u32[]{:S(2)}) copy-start(bf16[2048,256]{1,0:T(8,128)(2,1)} %cot_hbm.1) | copy-start | bytes 3145732
  12.4 4.2 %copy-start.3 = (bf16[512,256]{1,0:T(8,128)(2,1)S(1)}, bf16[512,256]{1,0:T(8,128)(2,1)}, u32[]{:S(2)}) copy-start(bf16[512,256]{1,0:T(8,128)(2,1)} %win_hbm.1) | copy-start | bytes 786436
  12.4 4.2 %copy-start.4 = (bf16[256,256]{1,0:T(8,128)(2,1)S(1)}, bf16[256,256]{1,0:T(8,128)(2,1)}, u32[]{:S(2)}) copy-start(bf16[256,256]{1,0:T(8,128)(2,1)} %wout_ref.1) | copy-start | bytes 393220
  12.4 4.2 %copy-start.5 = (s32[64]{0:T(128)S(1)}, s32[64]{0:T(128)}, u32[]{:S(2)}) copy-start(s32[64]{0:T(128)} %src_ref.3) | copy-start | bytes 772
  12.4 4.2 %copy-start.6 = (s32[64]{0:T(128)S(1)}, s32[64]{0:T(128)}, u32[]{:S(2)}) copy-start(s32[64]{0:T(128)} %dst_ref.3) | copy-start | bytes 772
  12.4 4.2 %copy-start.7 = (f32[256]{0:T(256)S(1)}, f32[256]{0:T(256)}, u32[]{:S(2)}) copy-start(f32[256]{0:T(256)} %param.18) | copy-start | bytes 3076
  12.4 4.1 %collective-permute-start.4 = (bf16[128,256]{1,0:T(8,128)(2,1)S(1)}, bf16[128,256]{1,0:T(8,128)(2,1)S(1)}, u32[]{:S(2)}, u32[]{:S(2)}) collective-permute-start(bf16[128,256]{1,0:T(8,128)(2,1)S(1)} %get-tuple-element.45), channel_id=1, source_target_pairs={{0,252},{4,0},{8,4},{12,8},{16,12},{20,16},{24,20},{28,24},{32,28}... | collective-permute-start | bytes 196616 | tf_op jit(solution)/shard_map/ppermute | solution.py:325
  22.7 6.2 %collective-permute-start.5 = (bf16[16,56,128]{2,1,0:T(8,128)(2,1)S(1)}, bf16[16,56,128]{2,1,0:T(8,128)(2,1)S(1)}, u32[]{:S(2)}, u32[]{:S(2)}) collective-permute-start(bf16[16,56,128]{2,1,0:T(8,128)(2,1)S(1)} %get-tuple-element.48), channel_id=1, source_target_pairs={{0,4},{4,0},{1,5},{5,1},{2,6},{6,2},{3,7},{7,3},{8,12},{12,8},{9,1... | collective-permute-start | bytes 688136 | tf_op jit(solution)/shard_map/ppermute | solution.py:325
  29.6 10.9 %all-to-all-start = ((bf16[16,56,128]{2,1,0:T(8,128)(2,1)}), bf16[16,56,128]{2,1,0:T(8,128)(2,1)S(1)}, u32[]{:S(2)}, u32[]{:S(2)}) async-start(bf16[16,56,128]{2,1,0:T(8,128)(2,1)} %join.1), calls=%async_computation | async-start | bytes 458752 | tf_op jit(solution)/shard_map/all_to_all | solution.py:401
  40.6 2.8 %collective-permute-start.6 = (f32[56,128]{1,0:T(8,128)S(1)}, f32[56,128]{1,0:T(8,128)S(1)}, u32[]{:S(2)}, u32[]{:S(2)}) collective-permute-start(f32[56,128]{1,0:T(8,128)S(1)} %fold.1.mine), channel_id=1, source_target_pairs={{0,8},{8,0},{16,24},{24,16},{32,40},{40,32},{48,56},{56,48},{1,9},... | collective-permute-start | bytes 86024 | tf_op jit(solution)/shard_map/ppermute | solution.py:431
  40.7 11.6 %collective-permute-start.9 = (bf16[128,256]{1,0:T(8,128)(2,1)S(1)}, bf16[128,256]{1,0:T(8,128)(2,1)S(1)}, u32[]{:S(2)}, u32[]{:S(2)}) collective-permute-start(bf16[128,256]{1,0:T(8,128)(2,1)S(1)} %get-tuple-element.60), channel_id=1, source_target_pairs={{0,252},{4,0},{8,4},{12,8},{16,12},{20,16},{24,20},{28,24},{32,28}... | collective-permute-start | bytes 196616 | tf_op jit(solution)/shard_map/ppermute | solution.py:325
  43.4 8.8 %collective-permute-start.7 = (f32[56,128]{1,0:T(8,128)S(1)}, f32[56,128]{1,0:T(8,128)S(1)}, u32[]{:S(2)}, u32[]{:S(2)}) collective-permute-start(f32[56,128]{1,0:T(8,128)S(1)} %add.2.mine), channel_id=1, source_target_pairs={{0,16},{8,24},{16,0},{24,8},{32,48},{40,56},{48,32},{56,40},{1,17}... | collective-permute-start | bytes 86024 | tf_op jit(solution)/shard_map/ppermute | solution.py:431
  45.8 8.4 %collective-permute-start.10 = (bf16[128,256]{1,0:T(8,128)(2,1)S(1)}, bf16[128,256]{1,0:T(8,128)(2,1)S(1)}, u32[]{:S(2)}, u32[]{:S(2)}) collective-permute-start(bf16[128,256]{1,0:T(8,128)(2,1)S(1)} %get-tuple-element.61), channel_id=1, source_target_pairs={{0,4},{4,8},{8,12},{12,16},{16,20},{20,24},{24,28},{28,32},{32,36}... | collective-permute-start | bytes 196616 | tf_op jit(solution)/shard_map/ppermute | solution.py:325
  49.5 15.5 %collective-permute-start.11 = (bf16[128,256]{1,0:T(8,128)(2,1)S(1)}, bf16[128,256]{1,0:T(8,128)(2,1)S(1)}, u32[]{:S(2)}, u32[]{:S(2)}) collective-permute-start(bf16[128,256]{1,0:T(8,128)(2,1)S(1)} %get-tuple-element.64), channel_id=1, source_target_pairs={{0,1},{1,2},{2,3},{3,0},{4,5},{5,6},{6,7},{7,4},{8,9},{9,10},{10,1... | collective-permute-start | bytes 196616 | tf_op jit(solution)/shard_map/ppermute | solution.py:325
  49.6 15.4 %collective-permute-start.13 = (bf16[128,256]{1,0:T(8,128)(2,1)S(1)}, bf16[128,256]{1,0:T(8,128)(2,1)S(1)}, u32[]{:S(2)}, u32[]{:S(2)}) collective-permute-start(bf16[128,256]{1,0:T(8,128)(2,1)S(1)} %get-tuple-element.66), channel_id=1, source_target_pairs={{0,3},{1,0},{2,1},{3,2},{4,7},{5,4},{6,5},{7,6},{8,11},{9,8},{10,9... | collective-permute-start | bytes 196616 | tf_op jit(solution)/shard_map/ppermute | solution.py:325
  52.2 12.9 %collective-permute-start.12 = (bf16[128,256]{1,0:T(8,128)(2,1)S(1)}, bf16[128,256]{1,0:T(8,128)(2,1)S(1)}, u32[]{:S(2)}, u32[]{:S(2)}) collective-permute-start(bf16[128,256]{1,0:T(8,128)(2,1)S(1)} %get-tuple-element.65), channel_id=1, source_target_pairs={{0,2},{1,3},{2,0},{3,1},{4,6},{5,7},{6,4},{7,5},{8,10},{9,11},{10,... | collective-permute-start | bytes 196616 | tf_op jit(solution)/shard_map/ppermute | solution.py:325
  52.3 6.8 %collective-permute-start.8 = (f32[56,128]{1,0:T(8,128)S(1)}, f32[56,128]{1,0:T(8,128)S(1)}, u32[]{:S(2)}, u32[]{:S(2)}) collective-permute-start(f32[56,128]{1,0:T(8,128)S(1)} %add.3.mine), channel_id=1, source_target_pairs={{0,32},{8,40},{16,48},{24,56},{32,0},{40,8},{48,16},{56,24},{1,33}... | collective-permute-start | bytes 86024 | tf_op jit(solution)/shard_map/ppermute | solution.py:431
  59.8 12.6 %all-to-all-start.1 = ((bf16[16,56,128]{2,1,0:T(8,128)(2,1)}), bf16[16,56,128]{2,1,0:T(8,128)(2,1)S(1)}, u32[]{:S(2)}, u32[]{:S(2)}) async-start(bf16[16,56,128]{2,1,0:T(8,128)(2,1)} %spread.1), calls=%async_computation.1 | async-start | bytes 458752 | tf_op jit(solution)/shard_map/all_to_all | solution.py:451
  72.4 2.9 %collective-permute-start.14 = (bf16[16,56,128]{2,1,0:T(8,128)(2,1)S(1)}, bf16[16,56,128]{2,1,0:T(8,128)(2,1)S(1)}, u32[]{:S(2)}, u32[]{:S(2)}) collective-permute-start(bf16[16,56,128]{2,1,0:T(8,128)(2,1)S(1)} %all-to-all-done.1.keep), channel_id=1, source_target_pairs={{0,4},{4,0},{1,5},{5,1},{2,6},{6,2},{3,7},{7,3},{8,12},{12,8},{9,1... | collective-permute-start | bytes 688136 | tf_op jit(solution)/shard_map/ppermute | solution.py:325

commit v6 on v4

--- a/solution.py
+++ b/solution.py
@@ -400,7 +400,6 @@
         cost_estimate=pl.CostEstimate(flops=4_000_000_000, bytes_accessed=9_000_000, transcendentals=0),
         name="back",
     )(src, dst, vals, *in_hbm(gpre, w_in, cot))
-    early, late = (), (1, 2, 3, 4, 5)
     parts, own = lax.optimization_barrier((parts, own))
     depth = lax.axis_size("z")
     paired = pl.pallas_call(
@@ -411,19 +410,10 @@
         compiler_params=params(4),
         name="fold",
     )(parts)
-    got = {0: slots[0]}
-    send = {d: (lambda v, d=d: shift(v, "sub", d, SUB)) for d in range(1, SUB)}
-    send[4] = lambda v: shift(v, DOM, -1, dom)
-    send[5] = lambda v: shift(v, DOM, 1, dom)
-    for d in early:
-        got[d] = send[d](slots[d])
-    held = [slots[d] for d in late]
-    paired, *held = lax.optimization_barrier((paired, *held))
+    paired, *slots[1:SUB] = lax.optimization_barrier((paired, *slots[1:SUB]))
     column = lax.all_to_all(paired, "z", split_axis=0, concat_axis=0, tiled=True)
-    for d, slot in zip(late, held):
-        got[d] = send[d](slot)
-    got = [got[d] for d in range(PEERS)]
-    column, *got = lax.optimization_barrier((column, *got))
+    got = [slots[0]] + [shift(slots[d], "sub", d, SUB) for d in range(1, SUB)]
+    column, *got[1:] = lax.optimization_barrier((column, *got[1:]))
     spread = pl.pallas_call(
         spread_kernel,
         out_shape=sds(halves, BF16),
@@ -432,7 +422,9 @@
         compiler_params=params(4),
         name="spread",
     )(column)
+    spread, *far = lax.optimization_barrier((spread, *slots[SUB:]))
     whole = lax.all_to_all(spread, PLANE, split_axis=0, concat_axis=0, tiled=True)
+    got += [shift(far[0], DOM, -1, dom), shift(far[1], DOM, 1, dom)]
     grad_features = pl.pallas_call(
         land_kernel,
         out_shape=sds((NB, BLK, H), F32),

time: 77 us -> 74.6 us (0.969)
  starting transfers between devices: 40.7 us -> 35.5 us
  waiting for transfers between devices: 9.92 us -> 12.7 us
    ppermute x12, starting transfers between devices: 27.5 us -> 21.9 us  [shift(): lax.ppermute(value, axis, [(i, (i + by) % size) for i in range(size)])]
    all_to_all x1, waiting for transfers between devices: 0.01 us -> 2.25 us  [local(): lax.all_to_all(paired, 'z', split_axis=0, concat_axis=0, tiled=True)]
    all_to_all x1, starting transfers between devices: 3.92 us -> 4.7 us  [local(): lax.all_to_all(spread, PLANE, split_axis=0, concat_axis=0, tiled=True)]
  transfers between devices with their start and end apart: 15 -> 15, of which waited for: 6 -> 8; matrix products, arithmetic and copies ran while one was open for 0% -> 0% of each run, Pallas kernels for 16% -> 17%
where the time goes in v6:
time: 74.6 us; the launch traced here: 74.1 us
  starting transfers between devices  35.5 us (48%)
  Pallas kernels  25 us (34%)
  waiting for transfers between devices  12.7 us (17%)
  between operations  0.83 us (1%)
    ppermute x12, starting transfers between devices, shift(): lax.ppermute(value, axis, [(i, (i + by) % size) for i in range(size)])  21.9 us
    pallas_call x1, Pallas kernels, local(): pl.pallas_call(node_kernel, out_shape=[sds((N, H), BF16), pltpu.HBM((N, H...  6.45 us
    pallas_call x1, Pallas kernels, local(): pl.pallas_call(back_kernel, out_shape=[pltpu.HBM((NB, BLK, H), F32)] + [b...  5.55 us
    all_to_all x1, starting transfers between devices, local(): lax.all_to_all(paired, 'z', split_axis=0, concat_axis=0, tiled=True)  5.18 us
    all_to_all x1, starting transfers between devices, local(): lax.all_to_all(spread, PLANE, split_axis=0, concat_axis=0, tiled=True)  4.7 us
    ppermute x12, waiting for transfers between devices, shift(): lax.ppermute(value, axis, [(i, (i + by) % size) for i in range(size)])  4.62 us
    all_to_all x1, waiting for transfers between devices, local(): lax.all_to_all(spread, PLANE, split_axis=0, concat_axis=0, tiled=True)  4.16 us
    all_to_all x1, starting transfers between devices, local(): lax.all_to_all(joined, PLANE, split_axis=0, concat_axis=0, tiled=True)  3.71 us
  transfers between devices with their start and end apart: 15, of which 8 were waited for; matrix products, arithmetic and copies ran while one was open for 0% of the time, Pallas kernels for 17%

profile of v6, /device:TPU:1, one launch (start us, length us, event | category | flops | bytes accessed | tf_op | source)
XLA Modules:
  0.0 74.1 jit_solution(16622205673017475769)
XLA Ops:
  0.6 2.8 %pick.1 = (bf16[128,256]{1,0:T(8,128)(2,1)S(1)}, bf16[128,256]{1,0:T(8,128)(2,1)S(1)}, bf16[128,256]{1,0:T(8,128)(2,1)S(1)}, bf16[128,256]{1,0:T(8,128)(2,1)S(1)...) custom-call(s32[6,1,128]{2,1,0:T(1,128)} %bitcast.5, s32[1,6]{1,0:T(1,128)} %count_hbm.3, ...), custom_call_target="tpu_custom_call" | custom-call | tf_op jit(solution)/shard_map/pick/pallas_call | solution.py:329
  3.4 2.2 %collective-permute-start = (bf16[128,256]{1,0:T(8,128)(2,1)S(1)}, bf16[128,256]{1,0:T(8,128)(2,1)S(1)}, u32[]{:S(2)}, u32[]{:S(2)}) collective-permute-start(bf16[128,256]{1,0:T(8,128)(2,1)S(1)} %get-tuple-element.41), channel_id=1, source_target_pairs={{0,1},{1,2},{2,3},{3,0},{4,5},{5,6},{6,7},{7,4},{8,9},{9,10},{10,1... | collective-permute-start | bytes 196616 | tf_op jit(solution)/shard_map/ppermute | solution.py:309
  5.6 2.6 %collective-permute-start.1 = (bf16[128,256]{1,0:T(8,128)(2,1)S(1)}, bf16[128,256]{1,0:T(8,128)(2,1)S(1)}, u32[]{:S(2)}, u32[]{:S(2)}) collective-permute-start(bf16[128,256]{1,0:T(8,128)(2,1)S(1)} %get-tuple-element.42), channel_id=1, source_target_pairs={{0,2},{1,3},{2,0},{3,1},{4,6},{5,7},{6,4},{7,5},{8,10},{9,11},{10,... | collective-permute-start | bytes 196616 | tf_op jit(solution)/shard_map/ppermute | solution.py:309
  8.2 1.1 %collective-permute-start.2 = (bf16[128,256]{1,0:T(8,128)(2,1)S(1)}, bf16[128,256]{1,0:T(8,128)(2,1)S(1)}, u32[]{:S(2)}, u32[]{:S(2)}) collective-permute-start(bf16[128,256]{1,0:T(8,128)(2,1)S(1)} %get-tuple-element.43), channel_id=1, source_target_pairs={{0,3},{1,0},{2,1},{3,2},{4,7},{5,4},{6,5},{7,6},{8,11},{9,8},{10,9... | collective-permute-start | bytes 196616 | tf_op jit(solution)/shard_map/ppermute | solution.py:309
  9.3 3.0 %collective-permute-start.3 = (bf16[128,256]{1,0:T(8,128)(2,1)S(1)}, bf16[128,256]{1,0:T(8,128)(2,1)S(1)}, u32[]{:S(2)}, u32[]{:S(2)}) collective-permute-start(bf16[128,256]{1,0:T(8,128)(2,1)S(1)} %get-tuple-element.44), channel_id=1, source_target_pairs={{0,4},{4,8},{8,12},{12,16},{16,20},{20,24},{24,28},{28,32},{32,36}... | collective-permute-start | bytes 196616 | tf_op jit(solution)/shard_map/ppermute | solution.py:309
  12.4 0.1 collective-permute-start.4
  12.5 3.5 %near.1.near_ref = f32[17,128,256]{2,1,0:T(8,128)S(1)} custom-call(s32[64]{0:T(128)} %src_ref.3, s32[64]{0:T(128)} %dst_ref.3, bf16[2048,256]{1,0:T(8,128)(2,1)} %feat_ref.1, bf16[64,128,128]{2,1,0:T(8,128)(2,1)} %vals_ref.3), custom_call_target="tpu_custom_call" | custom-call | flops 800000000 | bytes 6000000 | tf_op jit(solution)/shard_map/near/pallas_call | solution.py:346
  16.0 0.2 collective-permute-done.4.h5
  16.2 6.5 %node.1 = (bf16[2048,256]{1,0:T(8,128)(2,1)}, bf16[2048,256]{1,0:T(8,128)(2,1)}, f32[16,56,128]{2,1,0:T(8,128)S(1)}, bf16[16,56,128]{2,1,0:T(8,128)(2,1)S(1)}) custom-call(s32[64]{0:T(128)S(1)} %copy-done.5, s32[64]{0:T(128)S(1)} %copy-done.6, bf16[128,256]{1,0:T(8,128)(2,1)S(1)} %get-tuple-element.40.h0, bf16[128,256]{1,0:T(8,128)(2,1)S(1)} %collective-permute-done.h1, ...), custom_call_target="tpu_custom_call" | custom-call | tf_op jit(solution)/shard_map/node/pallas_call | solution.py:363
  22.7 4.9 %collective-permute-start.5 = (bf16[16,56,128]{2,1,0:T(8,128)(2,1)S(1)}, bf16[16,56,128]{2,1,0:T(8,128)(2,1)S(1)}, u32[]{:S(2)}, u32[]{:S(2)}) collective-permute-start(bf16[16,56,128]{2,1,0:T(8,128)(2,1)S(1)} %get-tuple-element.48), channel_id=1, source_target_pairs={{0,4},{4,0},{1,5},{5,1},{2,6},{6,2},{3,7},{7,3},{8,12},{12,8},{9,1... | collective-permute-start | bytes 688136 | tf_op jit(solution)/shard_map/ppermute | solution.py:309
  27.6 1.1 %collective-permute-done.5.other = bf16[16,56,128]{2,1,0:T(8,128)(2,1)S(1)} collective-permute-done((bf16[16,56,128]{2,1,0:T(8,128)(2,1)S(1)}, bf16[16,56,128]{2,1,0:T(8,128)(2,1)S(1)}, u32[]{:S(2)}, u32[]{:S(2)}) %collective-permute-start.5) | collective-permute-done | bytes 229408 | tf_op jit(solution)/shard_map/ppermute | solution.py:309
  28.8 0.7 join.1
  29.5 3.7 %all-to-all-start = ((bf16[16,56,128]{2,1,0:T(8,128)(2,1)}), bf16[16,56,128]{2,1,0:T(8,128)(2,1)S(1)}, u32[]{:S(2)}, u32[]{:S(2)}) async-start(bf16[16,56,128]{2,1,0:T(8,128)(2,1)} %join.1), calls=%async_computation | async-start | bytes 458752 | tf_op jit(solution)/shard_map/all_to_all | solution.py:385
  33.2 5.6 %back.1 = (f32[16,128,256]{2,1,0:T(8,128)}, bf16[128,256]{1,0:T(8,128)(2,1)S(1)}, bf16[128,256]{1,0:T(8,128)(2,1)S(1)}, bf16[128,256]{1,0:T(8,128)(2,1)S(1)}, bf...) custom-call(s32[64]{0:T(128)S(1)} %copy-done.5, s32[64]{0:T(128)S(1)} %copy-done.6, ...), custom_call_target="tpu_custom_call" | custom-call | flops 4000000000 | bytes 9000000 | tf_op jit(solution)/shard_map/back/pallas_call | solution.py:386
  38.8 1.6 %all-to-all-done.parts = bf16[16,56,128]{2,1,0:T(8,128)(2,1)S(1)} async-done(((bf16[16,56,128]{2,1,0:T(8,128)(2,1)}), bf16[16,56,128]{2,1,0:T(8,128)(2,1)S(1)}, u32[]{:S(2)}, u32[]{:S(2)}) %all-to-all-start) | async-done | bytes 229408 | tf_op jit(solution)/shard_map/all_to_all | solution.py:385
  40.4 0.7 fold.1
  41.1 5.2 %all-to-all-start.1 = ((bf16[8,56,128]{2,1,0:T(8,128)(2,1)}), bf16[8,56,128]{2,1,0:T(8,128)(2,1)S(1)}, u32[]{:S(2)}, u32[]{:S(2)}) async-start(bf16[8,56,128]{2,1,0:T(8,128)(2,1)} %fold.1), calls=%async_computation.1 | async-start | bytes 229376 | tf_op jit(solution)/shard_map/all_to_all | solution.py:414
  46.3 0.2 collective-permute-start.6
  46.4 1.8 %collective-permute-start.7 = (bf16[128,256]{1,0:T(8,128)(2,1)S(1)}, bf16[128,256]{1,0:T(8,128)(2,1)S(1)}, u32[]{:S(2)}, u32[]{:S(2)}) collective-permute-start(bf16[128,256]{1,0:T(8,128)(2,1)S(1)} %get-tuple-element.57), channel_id=1, source_target_pairs={{0,2},{1,3},{2,0},{3,1},{4,6},{5,7},{6,4},{7,5},{8,10},{9,11},{10,... | collective-permute-start | bytes 196616 | tf_op jit(solution)/shard_map/ppermute | solution.py:309
  48.2 1.4 %collective-permute-start.8 = (bf16[128,256]{1,0:T(8,128)(2,1)S(1)}, bf16[128,256]{1,0:T(8,128)(2,1)S(1)}, u32[]{:S(2)}, u32[]{:S(2)}) collective-permute-start(bf16[128,256]{1,0:T(8,128)(2,1)S(1)} %get-tuple-element.58), channel_id=1, source_target_pairs={{0,3},{1,0},{2,1},{3,2},{4,7},{5,4},{6,5},{7,6},{8,11},{9,8},{10,9... | collective-permute-start | bytes 196616 | tf_op jit(solution)/shard_map/ppermute | solution.py:309
  49.7 1.6 %collective-permute-done.6.r1 = bf16[128,256]{1,0:T(8,128)(2,1)S(1)} collective-permute-done((bf16[128,256]{1,0:T(8,128)(2,1)S(1)}, bf16[128,256]{1,0:T(8,128)(2,1)S(1)}, u32[]{:S(2)}, u32[]{:S(2)}) %collective-permute-start.6) | collective-permute-done | bytes 65568 | tf_op jit(solution)/shard_map/ppermute | solution.py:309
  51.3 0.6 collective-permute-done.8.r3
  51.9 2.2 %all-to-all-done.1.parts = bf16[8,56,128]{2,1,0:T(8,128)(2,1)S(1)} async-done(((bf16[8,56,128]{2,1,0:T(8,128)(2,1)}), bf16[8,56,128]{2,1,0:T(8,128)(2,1)S(1)}, u32[]{:S(2)}, u32[]{:S(2)}) %all-to-all-start.1) | async-done | bytes 114720 | tf_op jit(solution)/shard_map/all_to_all | solution.py:414
  54.1 0.7 spread.1
  54.8 3.1 %collective-permute-start.9 = (bf16[128,256]{1,0:T(8,128)(2,1)S(1)}, bf16[128,256]{1,0:T(8,128)(2,1)S(1)}, u32[]{:S(2)}, u32[]{:S(2)}) collective-permute-start(bf16[128,256]{1,0:T(8,128)(2,1)S(1)} %get-tuple-element.67), channel_id=1, source_target_pairs={{0,252},{4,0},{8,4},{12,8},{16,12},{20,16},{24,20},{28,24},{32,28}... | collective-permute-start | bytes 196616 | tf_op jit(solution)/shard_map/ppermute | solution.py:309
  57.9 0.2 collective-permute-start.10
  58.1 4.7 %all-to-all-start.2 = ((bf16[16,56,128]{2,1,0:T(8,128)(2,1)}), bf16[16,56,128]{2,1,0:T(8,128)(2,1)S(1)}, u32[]{:S(2)}, u32[]{:S(2)}) async-start(bf16[16,56,128]{2,1,0:T(8,128)(2,1)} %spread.1), calls=%async_computation.2 | async-start | bytes 458752 | tf_op jit(solution)/shard_map/all_to_all | solution.py:426
  62.8 3.5 %land.1 = f32[16,128,256]{2,1,0:T(8,128)} custom-call(s32[6,1,128]{2,1,0:T(1,128)} %bitcast.6, s32[1,6]{1,0:T(1,128)} %count_hbm.3, bf16[128,256]{1,0:T(8,128)(2,1)S(1)} %get-tuple-element.63.r0, bf16[128,256]{1,0:T(8,128)(2,1)S(1)} %collective-permute-done.6.r1, bf16[128,256]{1,0:T(8,128)(2,1)S(1)} %collective-permute-done.7.r2, ...), custom_call_target="tpu_custom_call" | custom-call | flops 5000000000 | bytes 9000000 | tf_op jit(solution)/shard_map/land/pallas_call | solution.py:428
  66.3 4.2 %all-to-all-done.2.keep = bf16[16,56,128]{2,1,0:T(8,128)(2,1)S(1)} async-done(((bf16[16,56,128]{2,1,0:T(8,128)(2,1)}), bf16[16,56,128]{2,1,0:T(8,128)(2,1)S(1)}, u32[]{:S(2)}, u32[]{:S(2)}) %all-to-all-start.2) | async-done | bytes 229408 | tf_op jit(solution)/shard_map/all_to_all | solution.py:426
  70.5 1.3 %collective-permute-start.11 = (bf16[16,56,128]{2,1,0:T(8,128)(2,1)S(1)}, bf16[16,56,128]{2,1,0:T(8,128)(2,1)S(1)}, u32[]{:S(2)}, u32[]{:S(2)}) collective-permute-start(bf16[16,56,128]{2,1,0:T(8,128)(2,1)S(1)} %all-to-all-done.2.keep), channel_id=1, source_target_pairs={{0,4},{4,0},{1,5},{5,1},{2,6},{6,2},{3,7},{7,3},{8,12},{12,8},{9,1... | collective-permute-start | bytes 688136 | tf_op jit(solution)/shard_map/ppermute | solution.py:309
  71.8 1.1 %collective-permute-done.11.other = bf16[16,56,128]{2,1,0:T(8,128)(2,1)S(1)} collective-permute-done((bf16[16,56,128]{2,1,0:T(8,128)(2,1)S(1)}, bf16[16,56,128]{2,1,0:T(8,128)(2,1)S(1)}, u32[]{:S(2)}, u32[]{:S(2)}) %collective-permute-start.11) | collective-permute-done | bytes 229408 | tf_op jit(solution)/shard_map/ppermute | solution.py:309
  72.9 1.1 %clip.1 = (f32[512,256]{1,0:T(8,128)}, f32[1,256]{1,0:T(1,128)}, f32[256,256]{1,0:T(8,128)}) custom-call(bf16[16,56,128]{2,1,0:T(8,128)(2,1)S(1)} %all-to-all-done.2.keep, bf16[16,56,128]{2,1,0:T(8,128)(2,1)S(1)} %collective-permute-done.11.other), custom_call_target="tpu_custom_call" | custom-call | tf_op jit(solution)/shard_map/clip/pallas_call | solution.py:445
  (23 shorter events, 0.1 us)
Async XLA Ops:
  3.4 12.6 %collective-permute-start = (bf16[128,256]{1,0:T(8,128)(2,1)S(1)}, bf16[128,256]{1,0:T(8,128)(2,1)S(1)}, u32[]{:S(2)}, u32[]{:S(2)}) collective-permute-start(bf16[128,256]{1,0:T(8,128)(2,1)S(1)} %get-tuple-element.41), channel_id=1, source_target_pairs={{0,1},{1,2},{2,3},{3,0},{4,5},{5,6},{6,7},{7,4},{8,9},{9,10},{10,1... | collective-permute-start | bytes 196616 | tf_op jit(solution)/shard_map/ppermute | solution.py:309
  5.6 10.4 %collective-permute-start.1 = (bf16[128,256]{1,0:T(8,128)(2,1)S(1)}, bf16[128,256]{1,0:T(8,128)(2,1)S(1)}, u32[]{:S(2)}, u32[]{:S(2)}) collective-permute-start(bf16[128,256]{1,0:T(8,128)(2,1)S(1)} %get-tuple-element.42), channel_id=1, source_target_pairs={{0,2},{1,3},{2,0},{3,1},{4,6},{5,7},{6,4},{7,5},{8,10},{9,11},{10,... | collective-permute-start | bytes 196616 | tf_op jit(solution)/shard_map/ppermute | solution.py:309
  8.2 7.8 %collective-permute-start.2 = (bf16[128,256]{1,0:T(8,128)(2,1)S(1)}, bf16[128,256]{1,0:T(8,128)(2,1)S(1)}, u32[]{:S(2)}, u32[]{:S(2)}) collective-permute-start(bf16[128,256]{1,0:T(8,128)(2,1)S(1)} %get-tuple-element.43), channel_id=1, source_target_pairs={{0,3},{1,0},{2,1},{3,2},{4,7},{5,4},{6,5},{7,6},{8,11},{9,8},{10,9... | collective-permute-start | bytes 196616 | tf_op jit(solution)/shard_map/ppermute | solution.py:309
  9.3 6.7 %collective-permute-start.3 = (bf16[128,256]{1,0:T(8,128)(2,1)S(1)}, bf16[128,256]{1,0:T(8,128)(2,1)S(1)}, u32[]{:S(2)}, u32[]{:S(2)}) collective-permute-start(bf16[128,256]{1,0:T(8,128)(2,1)S(1)} %get-tuple-element.44), channel_id=1, source_target_pairs={{0,4},{4,8},{8,12},{12,16},{16,20},{20,24},{24,28},{28,32},{32,36}... | collective-permute-start | bytes 196616 | tf_op jit(solution)/shard_map/ppermute | solution.py:309
  12.4 3.8 %copy-start = (bf16[2048,256]{1,0:T(8,128)(2,1)S(1)}, bf16[2048,256]{1,0:T(8,128)(2,1)}, u32[]{:S(2)}) copy-start(bf16[2048,256]{1,0:T(8,128)(2,1)} %feat_ref.1) | copy-start | bytes 3145732
  12.4 3.8 %copy-start.1 = (bf16[64,128,128]{2,1,0:T(8,128)(2,1)S(1)}, bf16[64,128,128]{2,1,0:T(8,128)(2,1)}, u32[]{:S(2)}) copy-start(bf16[64,128,128]{2,1,0:T(8,128)(2,1)} %vals_ref.3) | copy-start | bytes 6291460
  12.4 3.8 %copy-start.2 = (bf16[2048,256]{1,0:T(8,128)(2,1)S(1)}, bf16[2048,256]{1,0:T(8,128)(2,1)}, u32[]{:S(2)}) copy-start(bf16[2048,256]{1,0:T(8,128)(2,1)} %cot_hbm.1) | copy-start | bytes 3145732
  12.4 3.8 %copy-start.3 = (bf16[512,256]{1,0:T(8,128)(2,1)S(1)}, bf16[512,256]{1,0:T(8,128)(2,1)}, u32[]{:S(2)}) copy-start(bf16[512,256]{1,0:T(8,128)(2,1)} %win_hbm.1) | copy-start | bytes 786436
  12.4 3.8 %copy-start.4 = (bf16[256,256]{1,0:T(8,128)(2,1)S(1)}, bf16[256,256]{1,0:T(8,128)(2,1)}, u32[]{:S(2)}) copy-start(bf16[256,256]{1,0:T(8,128)(2,1)} %wout_ref.1) | copy-start | bytes 393220
  12.4 3.8 %copy-start.5 = (s32[64]{0:T(128)S(1)}, s32[64]{0:T(128)}, u32[]{:S(2)}) copy-start(s32[64]{0:T(128)} %src_ref.3) | copy-start | bytes 772
  12.4 3.8 %copy-start.6 = (s32[64]{0:T(128)S(1)}, s32[64]{0:T(128)}, u32[]{:S(2)}) copy-start(s32[64]{0:T(128)} %dst_ref.3) | copy-start | bytes 772
  12.4 3.8 %copy-start.7 = (f32[256]{0:T(256)S(1)}, f32[256]{0:T(256)}, u32[]{:S(2)}) copy-start(f32[256]{0:T(256)} %param.18) | copy-start | bytes 3076
  12.4 3.8 %collective-permute-start.4 = (bf16[128,256]{1,0:T(8,128)(2,1)S(1)}, bf16[128,256]{1,0:T(8,128)(2,1)S(1)}, u32[]{:S(2)}, u32[]{:S(2)}) collective-permute-start(bf16[128,256]{1,0:T(8,128)(2,1)S(1)} %get-tuple-element.45), channel_id=1, source_target_pairs={{0,252},{4,0},{8,4},{12,8},{16,12},{20,16},{24,20},{28,24},{32,28}... | collective-permute-start | bytes 196616 | tf_op jit(solution)/shard_map/ppermute | solution.py:309
  22.7 6.1 %collective-permute-start.5 = (bf16[16,56,128]{2,1,0:T(8,128)(2,1)S(1)}, bf16[16,56,128]{2,1,0:T(8,128)(2,1)S(1)}, u32[]{:S(2)}, u32[]{:S(2)}) collective-permute-start(bf16[16,56,128]{2,1,0:T(8,128)(2,1)S(1)} %get-tuple-element.48), channel_id=1, source_target_pairs={{0,4},{4,0},{1,5},{5,1},{2,6},{6,2},{3,7},{7,3},{8,12},{12,8},{9,1... | collective-permute-start | bytes 688136 | tf_op jit(solution)/shard_map/ppermute | solution.py:309
  29.5 10.9 %all-to-all-start = ((bf16[16,56,128]{2,1,0:T(8,128)(2,1)}), bf16[16,56,128]{2,1,0:T(8,128)(2,1)S(1)}, u32[]{:S(2)}, u32[]{:S(2)}) async-start(bf16[16,56,128]{2,1,0:T(8,128)(2,1)} %join.1), calls=%async_computation | async-start | bytes 458752 | tf_op jit(solution)/shard_map/all_to_all | solution.py:385
  41.1 13.0 %all-to-all-start.1 = ((bf16[8,56,128]{2,1,0:T(8,128)(2,1)}), bf16[8,56,128]{2,1,0:T(8,128)(2,1)S(1)}, u32[]{:S(2)}, u32[]{:S(2)}) async-start(bf16[8,56,128]{2,1,0:T(8,128)(2,1)} %fold.1), calls=%async_computation.1 | async-start | bytes 229376 | tf_op jit(solution)/shard_map/all_to_all | solution.py:414
  46.3 5.0 %collective-permute-start.6 = (bf16[128,256]{1,0:T(8,128)(2,1)S(1)}, bf16[128,256]{1,0:T(8,128)(2,1)S(1)}, u32[]{:S(2)}, u32[]{:S(2)}) collective-permute-start(bf16[128,256]{1,0:T(8,128)(2,1)S(1)} %get-tuple-element.56), channel_id=1, source_target_pairs={{0,1},{1,2},{2,3},{3,0},{4,5},{5,6},{6,7},{7,4},{8,9},{9,10},{10,1... | collective-permute-start | bytes 196616 | tf_op jit(solution)/shard_map/ppermute | solution.py:309
  46.4 4.9 %collective-permute-start.7 = (bf16[128,256]{1,0:T(8,128)(2,1)S(1)}, bf16[128,256]{1,0:T(8,128)(2,1)S(1)}, u32[]{:S(2)}, u32[]{:S(2)}) collective-permute-start(bf16[128,256]{1,0:T(8,128)(2,1)S(1)} %get-tuple-element.57), channel_id=1, source_target_pairs={{0,2},{1,3},{2,0},{3,1},{4,6},{5,7},{6,4},{7,5},{8,10},{9,11},{10,... | collective-permute-start | bytes 196616 | tf_op jit(solution)/shard_map/ppermute | solution.py:309
  48.2 3.6 %collective-permute-start.8 = (bf16[128,256]{1,0:T(8,128)(2,1)S(1)}, bf16[128,256]{1,0:T(8,128)(2,1)S(1)}, u32[]{:S(2)}, u32[]{:S(2)}) collective-permute-start(bf16[128,256]{1,0:T(8,128)(2,1)S(1)} %get-tuple-element.58), channel_id=1, source_target_pairs={{0,3},{1,0},{2,1},{3,2},{4,7},{5,4},{6,5},{7,6},{8,11},{9,8},{10,9... | collective-permute-start | bytes 196616 | tf_op jit(solution)/shard_map/ppermute | solution.py:309
  54.8 8.0 %collective-permute-start.9 = (bf16[128,256]{1,0:T(8,128)(2,1)S(1)}, bf16[128,256]{1,0:T(8,128)(2,1)S(1)}, u32[]{:S(2)}, u32[]{:S(2)}) collective-permute-start(bf16[128,256]{1,0:T(8,128)(2,1)S(1)} %get-tuple-element.67), channel_id=1, source_target_pairs={{0,252},{4,0},{8,4},{12,8},{16,12},{20,16},{24,20},{28,24},{32,28}... | collective-permute-start | bytes 196616 | tf_op jit(solution)/shard_map/ppermute | solution.py:309
  57.9 4.9 %collective-permute-start.10 = (bf16[128,256]{1,0:T(8,128)(2,1)S(1)}, bf16[128,256]{1,0:T(8,128)(2,1)S(1)}, u32[]{:S(2)}, u32[]{:S(2)}) collective-permute-start(bf16[128,256]{1,0:T(8,128)(2,1)S(1)} %get-tuple-element.68), channel_id=1, source_target_pairs={{0,4},{4,8},{8,12},{12,16},{16,20},{20,24},{24,28},{28,32},{32,36}... | collective-permute-start | bytes 196616 | tf_op jit(solution)/shard_map/ppermute | solution.py:309
  58.1 12.4 %all-to-all-start.2 = ((bf16[16,56,128]{2,1,0:T(8,128)(2,1)}), bf16[16,56,128]{2,1,0:T(8,128)(2,1)S(1)}, u32[]{:S(2)}, u32[]{:S(2)}) async-start(bf16[16,56,128]{2,1,0:T(8,128)(2,1)} %spread.1), calls=%async_computation.2 | async-start | bytes 458752 | tf_op jit(solution)/shard_map/all_to_all | solution.py:426
  70.5 2.5 %collective-permute-start.11 = (bf16[16,56,128]{2,1,0:T(8,128)(2,1)S(1)}, bf16[16,56,128]{2,1,0:T(8,128)(2,1)S(1)}, u32[]{:S(2)}, u32[]{:S(2)}) collective-permute-start(bf16[16,56,128]{2,1,0:T(8,128)(2,1)S(1)} %all-to-all-done.2.keep), channel_id=1, source_target_pairs={{0,4},{4,0},{1,5},{5,1},{2,6},{6,2},{3,7},{7,3},{8,12},{12,8},{9,1... | collective-permute-start | bytes 688136 | tf_op jit(solution)/shard_map/ppermute | solution.py:309

commit v7 on v6

--- a/solution.py
+++ b/solution.py
@@ -413,7 +413,6 @@
     paired, *slots[1:SUB] = lax.optimization_barrier((paired, *slots[1:SUB]))
     column = lax.all_to_all(paired, "z", split_axis=0, concat_axis=0, tiled=True)
     got = [slots[0]] + [shift(slots[d], "sub", d, SUB) for d in range(1, SUB)]
-    column, *got[1:] = lax.optimization_barrier((column, *got[1:]))
     spread = pl.pallas_call(
         spread_kernel,
         out_shape=sds(halves, BF16),

time: 74.6 us -> 74 us (level)
    all_to_all x1, waiting for transfers between devices: 2.25 us -> 4.46 us  [local(): lax.all_to_all(paired, 'z', split_axis=0, concat_axis=0, tiled=True)]
    ppermute x12, waiting for transfers between devices: 4.62 us -> 2.42 us  [shift(): lax.ppermute(value, axis, [(i, (i + by) % size) for i in range(size)])]
  transfers between devices with their start and end apart: 15 -> 15, of which waited for: 8 -> 6; matrix products, arithmetic and copies ran while one was open for 0% -> 0% of each run, Pallas kernels for 17% -> 18%
where the time goes in v7:
time: 74 us; the launch traced here: 73.6 us
  starting transfers between devices  35.6 us (48%)
  Pallas kernels  24.7 us (33%)
  waiting for transfers between devices  12.3 us (17%)
  between operations  0.86 us (1%)
    ppermute x12, starting transfers between devices, shift(): lax.ppermute(value, axis, [(i, (i + by) % size) for i in range(size)])  22.7 us
    pallas_call x1, Pallas kernels, local(): pl.pallas_call(node_kernel, out_shape=[sds((N, H), BF16), pltpu.HBM((N, H...  6.14 us
    pallas_call x1, Pallas kernels, local(): pl.pallas_call(back_kernel, out_shape=[pltpu.HBM((NB, BLK, H), F32)] + [b...  5.55 us
    all_to_all x1, starting transfers between devices, local(): lax.all_to_all(paired, 'z', split_axis=0, concat_axis=0, tiled=True)  5.21 us
    all_to_all x1, waiting for transfers between devices, local(): lax.all_to_all(paired, 'z', split_axis=0, concat_axis=0, tiled=True)  4.46 us
    all_to_all x1, starting transfers between devices, local(): lax.all_to_all(spread, PLANE, split_axis=0, concat_axis=0, tiled=True)  4.03 us
    all_to_all x1, waiting for transfers between devices, local(): lax.all_to_all(spread, PLANE, split_axis=0, concat_axis=0, tiled=True)  3.83 us
    all_to_all x1, starting transfers between devices, local(): lax.all_to_all(joined, PLANE, split_axis=0, concat_axis=0, tiled=True)  3.71 us
  transfers between devices with their start and end apart: 15, of which 6 were waited for; matrix products, arithmetic and copies ran while one was open for 0% of the time, Pallas kernels for 18%

profile of v7, /device:TPU:1, one launch (start us, length us, event | category | flops | bytes accessed | tf_op | source)
XLA Modules:
  0.0 73.6 jit_solution(2177563408143828888)
XLA Ops:
  0.6 2.8 %pick.1 = (bf16[128,256]{1,0:T(8,128)(2,1)S(1)}, bf16[128,256]{1,0:T(8,128)(2,1)S(1)}, bf16[128,256]{1,0:T(8,128)(2,1)S(1)}, bf16[128,256]{1,0:T(8,128)(2,1)S(1)...) custom-call(s32[6,1,128]{2,1,0:T(1,128)} %bitcast.5, s32[1,6]{1,0:T(1,128)} %count_hbm.3, ...), custom_call_target="tpu_custom_call" | custom-call | tf_op jit(solution)/shard_map/pick/pallas_call | solution.py:329
  3.4 2.2 %collective-permute-start = (bf16[128,256]{1,0:T(8,128)(2,1)S(1)}, bf16[128,256]{1,0:T(8,128)(2,1)S(1)}, u32[]{:S(2)}, u32[]{:S(2)}) collective-permute-start(bf16[128,256]{1,0:T(8,128)(2,1)S(1)} %get-tuple-element.37), channel_id=1, source_target_pairs={{0,1},{1,2},{2,3},{3,0},{4,5},{5,6},{6,7},{7,4},{8,9},{9,10},{10,1... | collective-permute-start | bytes 196616 | tf_op jit(solution)/shard_map/ppermute | solution.py:309
  5.6 2.6 %collective-permute-start.1 = (bf16[128,256]{1,0:T(8,128)(2,1)S(1)}, bf16[128,256]{1,0:T(8,128)(2,1)S(1)}, u32[]{:S(2)}, u32[]{:S(2)}) collective-permute-start(bf16[128,256]{1,0:T(8,128)(2,1)S(1)} %get-tuple-element.38), channel_id=1, source_target_pairs={{0,2},{1,3},{2,0},{3,1},{4,6},{5,7},{6,4},{7,5},{8,10},{9,11},{10,... | collective-permute-start | bytes 196616 | tf_op jit(solution)/shard_map/ppermute | solution.py:309
  8.2 1.1 %collective-permute-start.2 = (bf16[128,256]{1,0:T(8,128)(2,1)S(1)}, bf16[128,256]{1,0:T(8,128)(2,1)S(1)}, u32[]{:S(2)}, u32[]{:S(2)}) collective-permute-start(bf16[128,256]{1,0:T(8,128)(2,1)S(1)} %get-tuple-element.39), channel_id=1, source_target_pairs={{0,3},{1,0},{2,1},{3,2},{4,7},{5,4},{6,5},{7,6},{8,11},{9,8},{10,9... | collective-permute-start | bytes 196616 | tf_op jit(solution)/shard_map/ppermute | solution.py:309
  9.3 3.0 %collective-permute-start.3 = (bf16[128,256]{1,0:T(8,128)(2,1)S(1)}, bf16[128,256]{1,0:T(8,128)(2,1)S(1)}, u32[]{:S(2)}, u32[]{:S(2)}) collective-permute-start(bf16[128,256]{1,0:T(8,128)(2,1)S(1)} %get-tuple-element.40), channel_id=1, source_target_pairs={{0,4},{4,8},{8,12},{12,16},{16,20},{20,24},{24,28},{28,32},{32,36}... | collective-permute-start | bytes 196616 | tf_op jit(solution)/shard_map/ppermute | solution.py:309
  12.4 0.0 copy-start.5
  12.4 0.0 copy-start.6
  12.4 0.1 collective-permute-start.4
  12.5 3.5 %near.1.near_ref = f32[17,128,256]{2,1,0:T(8,128)S(1)} custom-call(s32[64]{0:T(128)} %src_ref.3, s32[64]{0:T(128)} %dst_ref.3, bf16[2048,256]{1,0:T(8,128)(2,1)} %feat_ref.1, bf16[64,128,128]{2,1,0:T(8,128)(2,1)} %vals_ref.3), custom_call_target="tpu_custom_call" | custom-call | flops 800000000 | bytes 6000000 | tf_op jit(solution)/shard_map/near/pallas_call | solution.py:346
  16.0 0.2 collective-permute-done.4.h5
  16.2 6.1 %node.1 = (bf16[2048,256]{1,0:T(8,128)(2,1)}, bf16[2048,256]{1,0:T(8,128)(2,1)}, f32[16,56,128]{2,1,0:T(8,128)S(1)}, bf16[16,56,128]{2,1,0:T(8,128)(2,1)S(1)}) custom-call(s32[64]{0:T(128)S(1)} %copy-done.5, s32[64]{0:T(128)S(1)} %copy-done.6, bf16[128,256]{1,0:T(8,128)(2,1)S(1)} %get-tuple-element.36.h0, bf16[128,256]{1,0:T(8,128)(2,1)S(1)} %collective-permute-done.h1, ...), custom_call_target="tpu_custom_call" | custom-call | tf_op jit(solution)/shard_map/node/pallas_call | solution.py:363
  22.4 5.2 %collective-permute-start.5 = (bf16[16,56,128]{2,1,0:T(8,128)(2,1)S(1)}, bf16[16,56,128]{2,1,0:T(8,128)(2,1)S(1)}, u32[]{:S(2)}, u32[]{:S(2)}) collective-permute-start(bf16[16,56,128]{2,1,0:T(8,128)(2,1)S(1)} %get-tuple-element.44), channel_id=1, source_target_pairs={{0,4},{4,0},{1,5},{5,1},{2,6},{6,2},{3,7},{7,3},{8,12},{12,8},{9,1... | collective-permute-start | bytes 688136 | tf_op jit(solution)/shard_map/ppermute | solution.py:309
  27.6 1.1 %collective-permute-done.5.other = bf16[16,56,128]{2,1,0:T(8,128)(2,1)S(1)} collective-permute-done((bf16[16,56,128]{2,1,0:T(8,128)(2,1)S(1)}, bf16[16,56,128]{2,1,0:T(8,128)(2,1)S(1)}, u32[]{:S(2)}, u32[]{:S(2)}) %collective-permute-start.5) | collective-permute-done | bytes 229408 | tf_op jit(solution)/shard_map/ppermute | solution.py:309
  28.8 0.7 %join.1 = bf16[16,56,128]{2,1,0:T(8,128)(2,1)} custom-call(f32[16,56,128]{2,1,0:T(8,128)S(1)} %get-tuple-element.43.keep, bf16[16,56,128]{2,1,0:T(8,128)(2,1)S(1)} %collective-permute-done.5.other), custom_call_target="tpu_custom_call" | custom-call | tf_op jit(solution)/shard_map/join/pallas_call | solution.py:382
  29.5 3.7 %all-to-all-start = ((bf16[16,56,128]{2,1,0:T(8,128)(2,1)}), bf16[16,56,128]{2,1,0:T(8,128)(2,1)S(1)}, u32[]{:S(2)}, u32[]{:S(2)}) async-start(bf16[16,56,128]{2,1,0:T(8,128)(2,1)} %join.1), calls=%async_computation | async-start | bytes 458752 | tf_op jit(solution)/shard_map/all_to_all | solution.py:385
  33.2 5.6 %back.1 = (f32[16,128,256]{2,1,0:T(8,128)}, bf16[128,256]{1,0:T(8,128)(2,1)S(1)}, bf16[128,256]{1,0:T(8,128)(2,1)S(1)}, bf16[128,256]{1,0:T(8,128)(2,1)S(1)}, bf...) custom-call(s32[64]{0:T(128)S(1)} %copy-done.5, s32[64]{0:T(128)S(1)} %copy-done.6, ...), custom_call_target="tpu_custom_call" | custom-call | flops 4000000000 | bytes 9000000 | tf_op jit(solution)/shard_map/back/pallas_call | solution.py:386
  38.8 1.6 %all-to-all-done.parts = bf16[16,56,128]{2,1,0:T(8,128)(2,1)S(1)} async-done(((bf16[16,56,128]{2,1,0:T(8,128)(2,1)}), bf16[16,56,128]{2,1,0:T(8,128)(2,1)S(1)}, u32[]{:S(2)}, u32[]{:S(2)}) %all-to-all-start) | async-done | bytes 229408 | tf_op jit(solution)/shard_map/all_to_all | solution.py:385
  40.4 0.7 fold.1
  41.1 5.2 %all-to-all-start.1 = ((bf16[8,56,128]{2,1,0:T(8,128)(2,1)}), bf16[8,56,128]{2,1,0:T(8,128)(2,1)S(1)}, u32[]{:S(2)}, u32[]{:S(2)}) async-start(bf16[8,56,128]{2,1,0:T(8,128)(2,1)} %fold.1), calls=%async_computation.1 | async-start | bytes 229376 | tf_op jit(solution)/shard_map/all_to_all | solution.py:414
  46.3 0.2 collective-permute-start.6
  46.5 1.8 %collective-permute-start.7 = (bf16[128,256]{1,0:T(8,128)(2,1)S(1)}, bf16[128,256]{1,0:T(8,128)(2,1)S(1)}, u32[]{:S(2)}, u32[]{:S(2)}) collective-permute-start(bf16[128,256]{1,0:T(8,128)(2,1)S(1)} %get-tuple-element.57), channel_id=1, source_target_pairs={{0,2},{1,3},{2,0},{3,1},{4,6},{5,7},{6,4},{7,5},{8,10},{9,11},{10,... | collective-permute-start | bytes 196616 | tf_op jit(solution)/shard_map/ppermute | solution.py:309
  48.3 1.4 %collective-permute-start.8 = (bf16[128,256]{1,0:T(8,128)(2,1)S(1)}, bf16[128,256]{1,0:T(8,128)(2,1)S(1)}, u32[]{:S(2)}, u32[]{:S(2)}) collective-permute-start(bf16[128,256]{1,0:T(8,128)(2,1)S(1)} %get-tuple-element.58), channel_id=1, source_target_pairs={{0,3},{1,0},{2,1},{3,2},{4,7},{5,4},{6,5},{7,6},{8,11},{9,8},{10,9... | collective-permute-start | bytes 196616 | tf_op jit(solution)/shard_map/ppermute | solution.py:309
  49.7 4.5 %all-to-all-done.1.parts = bf16[8,56,128]{2,1,0:T(8,128)(2,1)S(1)} async-done(((bf16[8,56,128]{2,1,0:T(8,128)(2,1)}), bf16[8,56,128]{2,1,0:T(8,128)(2,1)S(1)}, u32[]{:S(2)}, u32[]{:S(2)}) %all-to-all-start.1) | async-done | bytes 114720 | tf_op jit(solution)/shard_map/all_to_all | solution.py:414
  54.2 0.7 spread.1
  54.9 3.1 %collective-permute-start.9 = (bf16[128,256]{1,0:T(8,128)(2,1)S(1)}, bf16[128,256]{1,0:T(8,128)(2,1)S(1)}, u32[]{:S(2)}, u32[]{:S(2)}) collective-permute-start(bf16[128,256]{1,0:T(8,128)(2,1)S(1)} %get-tuple-element.59), channel_id=1, source_target_pairs={{0,252},{4,0},{8,4},{12,8},{16,12},{20,16},{24,20},{28,24},{32,28}... | collective-permute-start | bytes 196616 | tf_op jit(solution)/shard_map/ppermute | solution.py:309
  58.0 0.2 collective-permute-start.10
  58.1 4.0 %all-to-all-start.2 = ((bf16[16,56,128]{2,1,0:T(8,128)(2,1)}), bf16[16,56,128]{2,1,0:T(8,128)(2,1)S(1)}, u32[]{:S(2)}, u32[]{:S(2)}) async-start(bf16[16,56,128]{2,1,0:T(8,128)(2,1)} %spread.1), calls=%async_computation.2 | async-start | bytes 458752 | tf_op jit(solution)/shard_map/all_to_all | solution.py:425
  62.2 3.5 %land.1 = f32[16,128,256]{2,1,0:T(8,128)} custom-call(s32[6,1,128]{2,1,0:T(1,128)} %bitcast.6, s32[1,6]{1,0:T(1,128)} %count_hbm.3, bf16[128,256]{1,0:T(8,128)(2,1)S(1)} %get-tuple-element.55.r0, bf16[128,256]{1,0:T(8,128)(2,1)S(1)} %collective-permute-done.6.r1, bf16[128,256]{1,0:T(8,128)(2,1)S(1)} %collective-permute-done.7.r2, ...), custom_call_target="tpu_custom_call" | custom-call | flops 5000000000 | bytes 9000000 | tf_op jit(solution)/shard_map/land/pallas_call | solution.py:427
  65.7 3.8 %all-to-all-done.2.keep = bf16[16,56,128]{2,1,0:T(8,128)(2,1)S(1)} async-done(((bf16[16,56,128]{2,1,0:T(8,128)(2,1)}), bf16[16,56,128]{2,1,0:T(8,128)(2,1)S(1)}, u32[]{:S(2)}, u32[]{:S(2)}) %all-to-all-start.2) | async-done | bytes 229408 | tf_op jit(solution)/shard_map/all_to_all | solution.py:425
  69.5 1.8 %collective-permute-start.11 = (bf16[16,56,128]{2,1,0:T(8,128)(2,1)S(1)}, bf16[16,56,128]{2,1,0:T(8,128)(2,1)S(1)}, u32[]{:S(2)}, u32[]{:S(2)}) collective-permute-start(bf16[16,56,128]{2,1,0:T(8,128)(2,1)S(1)} %all-to-all-done.2.keep), channel_id=1, source_target_pairs={{0,4},{4,0},{1,5},{5,1},{2,6},{6,2},{3,7},{7,3},{8,12},{12,8},{9,1... | collective-permute-start | bytes 688136 | tf_op jit(solution)/shard_map/ppermute | solution.py:309
  71.3 1.1 %collective-permute-done.11.other = bf16[16,56,128]{2,1,0:T(8,128)(2,1)S(1)} collective-permute-done((bf16[16,56,128]{2,1,0:T(8,128)(2,1)S(1)}, bf16[16,56,128]{2,1,0:T(8,128)(2,1)S(1)}, u32[]{:S(2)}, u32[]{:S(2)}) %collective-permute-start.11) | collective-permute-done | bytes 229408 | tf_op jit(solution)/shard_map/ppermute | solution.py:309
  72.4 1.1 %clip.1 = (f32[512,256]{1,0:T(8,128)}, f32[1,256]{1,0:T(1,128)}, f32[256,256]{1,0:T(8,128)}) custom-call(bf16[16,56,128]{2,1,0:T(8,128)(2,1)S(1)} %all-to-all-done.2.keep, bf16[16,56,128]{2,1,0:T(8,128)(2,1)S(1)} %collective-permute-done.11.other), custom_call_target="tpu_custom_call" | custom-call | tf_op jit(solution)/shard_map/clip/pallas_call | solution.py:444
  (23 shorter events, 0.1 us)
Async XLA Ops:
  3.4 12.6 %collective-permute-start = (bf16[128,256]{1,0:T(8,128)(2,1)S(1)}, bf16[128,256]{1,0:T(8,128)(2,1)S(1)}, u32[]{:S(2)}, u32[]{:S(2)}) collective-permute-start(bf16[128,256]{1,0:T(8,128)(2,1)S(1)} %get-tuple-element.37), channel_id=1, source_target_pairs={{0,1},{1,2},{2,3},{3,0},{4,5},{5,6},{6,7},{7,4},{8,9},{9,10},{10,1... | collective-permute-start | bytes 196616 | tf_op jit(solution)/shard_map/ppermute | solution.py:309
  5.6 10.4 %collective-permute-start.1 = (bf16[128,256]{1,0:T(8,128)(2,1)S(1)}, bf16[128,256]{1,0:T(8,128)(2,1)S(1)}, u32[]{:S(2)}, u32[]{:S(2)}) collective-permute-start(bf16[128,256]{1,0:T(8,128)(2,1)S(1)} %get-tuple-element.38), channel_id=1, source_target_pairs={{0,2},{1,3},{2,0},{3,1},{4,6},{5,7},{6,4},{7,5},{8,10},{9,11},{10,... | collective-permute-start | bytes 196616 | tf_op jit(solution)/shard_map/ppermute | solution.py:309
  8.2 7.8 %collective-permute-start.2 = (bf16[128,256]{1,0:T(8,128)(2,1)S(1)}, bf16[128,256]{1,0:T(8,128)(2,1)S(1)}, u32[]{:S(2)}, u32[]{:S(2)}) collective-permute-start(bf16[128,256]{1,0:T(8,128)(2,1)S(1)} %get-tuple-element.39), channel_id=1, source_target_pairs={{0,3},{1,0},{2,1},{3,2},{4,7},{5,4},{6,5},{7,6},{8,11},{9,8},{10,9... | collective-permute-start | bytes 196616 | tf_op jit(solution)/shard_map/ppermute | solution.py:309
  9.3 6.7 %collective-permute-start.3 = (bf16[128,256]{1,0:T(8,128)(2,1)S(1)}, bf16[128,256]{1,0:T(8,128)(2,1)S(1)}, u32[]{:S(2)}, u32[]{:S(2)}) collective-permute-start(bf16[128,256]{1,0:T(8,128)(2,1)S(1)} %get-tuple-element.40), channel_id=1, source_target_pairs={{0,4},{4,8},{8,12},{12,16},{16,20},{20,24},{24,28},{28,32},{32,36}... | collective-permute-start | bytes 196616 | tf_op jit(solution)/shard_map/ppermute | solution.py:309
  12.4 3.8 %copy-start = (bf16[2048,256]{1,0:T(8,128)(2,1)S(1)}, bf16[2048,256]{1,0:T(8,128)(2,1)}, u32[]{:S(2)}) copy-start(bf16[2048,256]{1,0:T(8,128)(2,1)} %feat_ref.1) | copy-start | bytes 3145732
  12.4 3.8 %copy-start.1 = (bf16[64,128,128]{2,1,0:T(8,128)(2,1)S(1)}, bf16[64,128,128]{2,1,0:T(8,128)(2,1)}, u32[]{:S(2)}) copy-start(bf16[64,128,128]{2,1,0:T(8,128)(2,1)} %vals_ref.3) | copy-start | bytes 6291460
  12.4 3.8 %copy-start.2 = (bf16[2048,256]{1,0:T(8,128)(2,1)S(1)}, bf16[2048,256]{1,0:T(8,128)(2,1)}, u32[]{:S(2)}) copy-start(bf16[2048,256]{1,0:T(8,128)(2,1)} %cot_hbm.1) | copy-start | bytes 3145732
  12.4 3.8 %copy-start.3 = (bf16[512,256]{1,0:T(8,128)(2,1)S(1)}, bf16[512,256]{1,0:T(8,128)(2,1)}, u32[]{:S(2)}) copy-start(bf16[512,256]{1,0:T(8,128)(2,1)} %win_hbm.1) | copy-start | bytes 786436
  12.4 3.8 %copy-start.4 = (bf16[256,256]{1,0:T(8,128)(2,1)S(1)}, bf16[256,256]{1,0:T(8,128)(2,1)}, u32[]{:S(2)}) copy-start(bf16[256,256]{1,0:T(8,128)(2,1)} %wout_ref.1) | copy-start | bytes 393220
  12.4 3.8 %copy-start.5 = (s32[64]{0:T(128)S(1)}, s32[64]{0:T(128)}, u32[]{:S(2)}) copy-start(s32[64]{0:T(128)} %src_ref.3) | copy-start | bytes 772
  12.4 3.8 %copy-start.6 = (s32[64]{0:T(128)S(1)}, s32[64]{0:T(128)}, u32[]{:S(2)}) copy-start(s32[64]{0:T(128)} %dst_ref.3) | copy-start | bytes 772
  12.4 3.8 %copy-start.7 = (f32[256]{0:T(256)S(1)}, f32[256]{0:T(256)}, u32[]{:S(2)}) copy-start(f32[256]{0:T(256)} %param.18) | copy-start | bytes 3076
  12.4 3.8 %collective-permute-start.4 = (bf16[128,256]{1,0:T(8,128)(2,1)S(1)}, bf16[128,256]{1,0:T(8,128)(2,1)S(1)}, u32[]{:S(2)}, u32[]{:S(2)}) collective-permute-start(bf16[128,256]{1,0:T(8,128)(2,1)S(1)} %get-tuple-element.41), channel_id=1, source_target_pairs={{0,252},{4,0},{8,4},{12,8},{16,12},{20,16},{24,20},{28,24},{32,28}... | collective-permute-start | bytes 196616 | tf_op jit(solution)/shard_map/ppermute | solution.py:309
  22.4 6.4 %collective-permute-start.5 = (bf16[16,56,128]{2,1,0:T(8,128)(2,1)S(1)}, bf16[16,56,128]{2,1,0:T(8,128)(2,1)S(1)}, u32[]{:S(2)}, u32[]{:S(2)}) collective-permute-start(bf16[16,56,128]{2,1,0:T(8,128)(2,1)S(1)} %get-tuple-element.44), channel_id=1, source_target_pairs={{0,4},{4,0},{1,5},{5,1},{2,6},{6,2},{3,7},{7,3},{8,12},{12,8},{9,1... | collective-permute-start | bytes 688136 | tf_op jit(solution)/shard_map/ppermute | solution.py:309
  29.5 10.9 %all-to-all-start = ((bf16[16,56,128]{2,1,0:T(8,128)(2,1)}), bf16[16,56,128]{2,1,0:T(8,128)(2,1)S(1)}, u32[]{:S(2)}, u32[]{:S(2)}) async-start(bf16[16,56,128]{2,1,0:T(8,128)(2,1)} %join.1), calls=%async_computation | async-start | bytes 458752 | tf_op jit(solution)/shard_map/all_to_all | solution.py:385
  41.1 13.1 %all-to-all-start.1 = ((bf16[8,56,128]{2,1,0:T(8,128)(2,1)}), bf16[8,56,128]{2,1,0:T(8,128)(2,1)S(1)}, u32[]{:S(2)}, u32[]{:S(2)}) async-start(bf16[8,56,128]{2,1,0:T(8,128)(2,1)} %fold.1), calls=%async_computation.1 | async-start | bytes 229376 | tf_op jit(solution)/shard_map/all_to_all | solution.py:414
  46.3 15.9 %collective-permute-start.6 = (bf16[128,256]{1,0:T(8,128)(2,1)S(1)}, bf16[128,256]{1,0:T(8,128)(2,1)S(1)}, u32[]{:S(2)}, u32[]{:S(2)}) collective-permute-start(bf16[128,256]{1,0:T(8,128)(2,1)S(1)} %get-tuple-element.56), channel_id=1, source_target_pairs={{0,1},{1,2},{2,3},{3,0},{4,5},{5,6},{6,7},{7,4},{8,9},{9,10},{10,1... | collective-permute-start | bytes 196616 | tf_op jit(solution)/shard_map/ppermute | solution.py:309
  46.5 15.7 %collective-permute-start.7 = (bf16[128,256]{1,0:T(8,128)(2,1)S(1)}, bf16[128,256]{1,0:T(8,128)(2,1)S(1)}, u32[]{:S(2)}, u32[]{:S(2)}) collective-permute-start(bf16[128,256]{1,0:T(8,128)(2,1)S(1)} %get-tuple-element.57), channel_id=1, source_target_pairs={{0,2},{1,3},{2,0},{3,1},{4,6},{5,7},{6,4},{7,5},{8,10},{9,11},{10,... | collective-permute-start | bytes 196616 | tf_op jit(solution)/shard_map/ppermute | solution.py:309
  48.3 13.9 %collective-permute-start.8 = (bf16[128,256]{1,0:T(8,128)(2,1)S(1)}, bf16[128,256]{1,0:T(8,128)(2,1)S(1)}, u32[]{:S(2)}, u32[]{:S(2)}) collective-permute-start(bf16[128,256]{1,0:T(8,128)(2,1)S(1)} %get-tuple-element.58), channel_id=1, source_target_pairs={{0,3},{1,0},{2,1},{3,2},{4,7},{5,4},{6,5},{7,6},{8,11},{9,8},{10,9... | collective-permute-start | bytes 196616 | tf_op jit(solution)/shard_map/ppermute | solution.py:309
  54.9 7.3 %collective-permute-start.9 = (bf16[128,256]{1,0:T(8,128)(2,1)S(1)}, bf16[128,256]{1,0:T(8,128)(2,1)S(1)}, u32[]{:S(2)}, u32[]{:S(2)}) collective-permute-start(bf16[128,256]{1,0:T(8,128)(2,1)S(1)} %get-tuple-element.59), channel_id=1, source_target_pairs={{0,252},{4,0},{8,4},{12,8},{16,12},{20,16},{24,20},{28,24},{32,28}... | collective-permute-start | bytes 196616 | tf_op jit(solution)/shard_map/ppermute | solution.py:309
  58.0 4.3 %collective-permute-start.10 = (bf16[128,256]{1,0:T(8,128)(2,1)S(1)}, bf16[128,256]{1,0:T(8,128)(2,1)S(1)}, u32[]{:S(2)}, u32[]{:S(2)}) collective-permute-start(bf16[128,256]{1,0:T(8,128)(2,1)S(1)} %get-tuple-element.60), channel_id=1, source_target_pairs={{0,4},{4,8},{8,12},{12,16},{16,20},{20,24},{24,28},{28,32},{32,36}... | collective-permute-start | bytes 196616 | tf_op jit(solution)/shard_map/ppermute | solution.py:309
  58.1 11.4 %all-to-all-start.2 = ((bf16[16,56,128]{2,1,0:T(8,128)(2,1)}), bf16[16,56,128]{2,1,0:T(8,128)(2,1)S(1)}, u32[]{:S(2)}, u32[]{:S(2)}) async-start(bf16[16,56,128]{2,1,0:T(8,128)(2,1)} %spread.1), calls=%async_computation.2 | async-start | bytes 458752 | tf_op jit(solution)/shard_map/all_to_all | solution.py:425
  69.5 2.9 %collective-permute-start.11 = (bf16[16,56,128]{2,1,0:T(8,128)(2,1)S(1)}, bf16[16,56,128]{2,1,0:T(8,128)(2,1)S(1)}, u32[]{:S(2)}, u32[]{:S(2)}) collective-permute-start(bf16[16,56,128]{2,1,0:T(8,128)(2,1)S(1)} %all-to-all-done.2.keep), channel_id=1, source_target_pairs={{0,4},{4,0},{1,5},{5,1},{2,6},{6,2},{3,7},{7,3},{8,12},{12,8},{9,1... | collective-permute-start | bytes 688136 | tf_op jit(solution)/shard_map/ppermute | solution.py:309
